TPU v7x, 256 devices: a whole 4x4x8 slice. The times are simulated.
256 devices in a mesh: lat: 32 (over y, x, core), src: 8 (over z).
Axes of the slice: x: 4, y: 4, z: 8, core: 2. Of those that a mesh axis runs over, the one named last changes fastest.
Arguments:
- swath: bfloat16 [8, 1024, 616, 128], P('src', 'lat'), may hold values from -6 to 6
- tile_band: int32 [8, 1024, 1], P('src', 'lat'), may hold values from 0 to 31; in each aligned block of 32 rows (0 to 31, 32 to 63, ..., all dimensions but the last counted through in order) at most 2 rows name the same one
- tile_patch: int32 [8, 1024], P('src', 'lat'), may hold values from 0 to 31
- fp_pos: bfloat16 [8, 1024, 2, 128], P('src', 'lat'), may hold values from 0 to 24, as said below
- conv_weight: bfloat16 [8, 4, 4, 616, 512], P('src', None, None, None, 'lat'), may hold values from -0.0625 to 0.0625
- conv_bias: float32 [8, 512], P('src'), may hold values from -6 to 6
- norm_gain: float32 [512], replicated, may hold values from 0.1 to 1.9
- latents: float32 [4, 512], replicated, may hold values from -200 to 200
- kv_weight: bfloat16 [512, 1024], replicated, may hold values from -0.25 to 0.25
- out_weight: bfloat16 [512, 512], replicated, may hold values from -0.25 to 0.25
Outputs:
- latent_out: float32 [1024, 4, 512], P(('lat', 'src'))
Inputs may be any that keep to these rules, and one draw needn't show every extreme that they name: `tile_band`: among the tiles of one source on one index of lat no band is named more than 2 times; some band is named exactly 2 times. `fp_pos`: the first of the two rows lies in [0, 8), the second in [0, 24).
All inputs are finite; a program needn't handle non-finite values.
Results may differ from a plain program's by a relative error of at most 0.035.
Values may be sent and summed in bfloat16 or wider, within the bound.
No kernel may reach another device: no remote copies, remote signals or barrier semaphores. Data moves between devices by JAX's collectives and lax.ppermute only.
A program may use at most 192 MiB of HBM per device.

v0:
```python
import functools
import math

import jax
import jax.numpy as jnp
import numpy as np
from jax import lax
from jax.experimental import pallas as pl
from jax.experimental.pallas import tpu as pltpu
from jax.sharding import PartitionSpec as P

HEADS = 8
HD = 64
PW = 24
KS = 4
TPS = 12
LEVELS = 4
TILES = 32
PATCHES = 32
CHIPS = 16
SIDE = 4
CELLS = 192
TAPS = KS * KS
SLOTS = 4
FP = 128
PAIR = 2 * TPS
FAR = 1.0e4
OFFSETS = (0, -1, 1, 2)
ROW_TOKEN = np.array(list(range(TPS)) + [8, 9, 10, 11, 0, 1, 2, 3, 4, 5, 6, 7])
BF = jnp.bfloat16
F32 = jnp.float32
NT = (((1,), (1,)), ((), ()))
VMEM_LIMIT = 56 * 2**20


def centers(tokens):
    rows, cols = [], []
    for tap in range(TAPS):
        for token in tokens:
            rows.append(token // 6 * KS + tap // KS + 0.5 if token >= 0 else FAR)
            cols.append(token % 6 * KS + tap % KS + 0.5 if token >= 0 else FAR)
    wide = [np.repeat(np.array(v, np.float32)[:, None], FP, 1) for v in (rows, cols)]
    return np.stack(wide)


def weights_at(pos, center_ref, index):
    down = pos[0:1] - center_ref[index]
    across = pos[1:2] - center_ref[index + 1]
    return jnp.exp((down * down + across * across) * (-1.0 / 1.125))


def mass_kernel(pos_ref, center_ref, out_ref):
    ones = jnp.ones((8, FP), BF)
    place = lax.broadcasted_iota(jnp.int32, (8, CELLS), 0)

    def group(g, carry):
        base = pl.multiple_of(g * 8, 8)
        total = jnp.zeros((8, CELLS), F32)
        for j in range(8):
            table = weights_at(pos_ref[base + j], center_ref, 0).astype(BF)
            row = lax.dot_general(ones, table, NT, preferred_element_type=F32)
            total = jnp.where(place == j, row, total)
        out_ref[pl.ds(base, 8), :] = total
        return carry

    lax.fori_loop(0, TILES // 8, group, 0)


def tile_mass(pos):
    return pl.pallas_call(
        mass_kernel,
        out_shape=jax.ShapeDtypeStruct((TILES, CELLS), F32),
        cost_estimate=pl.CostEstimate(flops=2 * TILES * 8 * FP * CELLS, bytes_accessed=300000, transcendentals=TILES * FP * CELLS),
        name="tile_mass",
    )(pos, jnp.asarray(centers(range(TPS))))


def grid_kernel(swath_ref, pos_ref, inverse_ref, center_ref, out_ref):
    blocks = []
    gap = jnp.zeros((TAPS, 8, FP), F32)
    channels = swath_ref.shape[1]
    for pair in range(2):
        first, second = 2 * pair, 2 * pair + 1
        left = weights_at(pos_ref[first], center_ref, 0).reshape(TAPS, 16, FP)
        right = weights_at(pos_ref[second], center_ref, 2).reshape(TAPS, 16, FP)
        left = jnp.concatenate([left, gap], 1).reshape(TAPS * PAIR, FP)
        right = jnp.concatenate([gap, right], 1).reshape(TAPS * PAIR, FP)
        table = jnp.concatenate([left, right], 1).astype(BF)
        data = jnp.concatenate([swath_ref[first], swath_ref[second]], 1)
        total = lax.dot_general(table, data, NT, preferred_element_type=F32)
        scale = jnp.broadcast_to(inverse_ref[pair], (FP, TAPS * PAIR)).T
        scale = jnp.concatenate([scale] * (-(-channels // FP)), 1)[:, :channels]
        blocks.append((total * scale).reshape(TAPS, PAIR, channels))
    out_ref[...] = jnp.concatenate(blocks, 1).astype(BF)


def gridded(swath, pos, inverse, center):
    channels = swath.shape[1]
    return pl.pallas_call(
        grid_kernel,
        grid=(TILES // 4,),
        in_specs=[
            pl.BlockSpec((4, channels, FP), lambda i: (i, 0, 0)),
            pl.BlockSpec((4, 2, FP), lambda i: (i, 0, 0)),
            pl.BlockSpec((2, 1, TAPS * PAIR), lambda i: (i, 0, 0)),
            pl.BlockSpec((4, TAPS * 16, FP), lambda i: (0, 0, 0)),
        ],
        out_specs=pl.BlockSpec((TAPS, 2 * PAIR, channels), lambda i: (0, i, 0)),
        out_shape=jax.ShapeDtypeStruct((TAPS, TILES * TPS, channels), BF),
        compiler_params=pltpu.CompilerParams(vmem_limit_bytes=VMEM_LIMIT),
        cost_estimate=pl.CostEstimate(
            flops=2 * (TILES // 2) * TAPS * PAIR * 2 * FP * 768,
            bytes_accessed=TILES * channels * (FP + CELLS) * 2,
            transcendentals=TILES * FP * 256,
        ),
        name="grid_tiles",
    )(swath, pos, inverse, center)


def embed_kernel(own_ref, sib_ref, w0, w1, w2, w3, w4, column_ref, row_ref, out_ref, total, spread):
    step = pl.program_id(0)
    slot_rows = out_ref.shape[0]
    part = slot_rows // TAPS

    @pl.when(step == 0)
    def _():
        total[...] = jnp.zeros_like(total)

    channels = own_ref.shape[2]
    weight = jnp.concatenate([w[...].reshape(-1, channels) for w in (w0, w1, w2, w3, w4)], 0)
    half = TILES * TPS
    total[:half] += lax.dot_general(own_ref[0], weight, NT, preferred_element_type=F32)
    total[half:] += lax.dot_general(sib_ref[0], weight, NT, preferred_element_type=F32)
    base = pl.multiple_of(step * part, part)
    here = lax.broadcasted_iota(jnp.int32, (part, 2 * half), 0) + base
    spread[pl.ds(base, part), :] = jnp.where(here == row_ref[...], 1.0, 0.0).astype(BF)

    @pl.when(step == TAPS - 1)
    def _():
        width = total.shape[1]
        columns = lax.broadcasted_iota(jnp.int32, (width, width), 0)
        order = jnp.where(columns == column_ref[...], 1.0, 0.0).astype(BF)
        tokens = total[...].astype(BF)
        tokens = lax.dot_general(tokens, order, NT, preferred_element_type=F32).astype(BF)
        out_ref[...] = jnp.dot(spread[...], tokens, preferred_element_type=F32).astype(BF)


def embed(own, sib, weights, columns, rows):
    channels = own.shape[2]
    cols = weights[0].shape[2]
    width = CHIPS * cols
    slot_rows = 32 * SLOTS * TPS
    half = TILES * TPS
    return pl.pallas_call(
        embed_kernel,
        grid=(TAPS,),
        in_specs=[pl.BlockSpec((1, half, channels), lambda i: (i, 0, 0))] * 2
        + [pl.BlockSpec((w.shape[0], 1, cols, channels), lambda i: (0, i, 0, 0)) for w in weights]
        + [
            pl.BlockSpec((1, width), lambda i: (0, 0)),
            pl.BlockSpec((1, 2 * half), lambda i: (0, 0)),
        ],
        out_specs=pl.BlockSpec((slot_rows, width), lambda i: (0, 0)),
        out_shape=jax.ShapeDtypeStruct((slot_rows, width), BF),
        scratch_shapes=[pltpu.VMEM((2 * half, width), F32), pltpu.VMEM((slot_rows, 2 * half), BF)],
        compiler_params=pltpu.CompilerParams(vmem_limit_bytes=VMEM_LIMIT),
        cost_estimate=pl.CostEstimate(
            flops=2 * TAPS * 2 * half * 768 * width,
            bytes_accessed=TAPS * (2 * half + width) * 640 * 2,
            transcendentals=0,
        ),
        name="embed_tiles",
    )(own, sib, *weights, columns, rows)


def attend_kernel(tokens_ref, row_ref, bias_ref, gain_ref, kv_ref, latent_ref, out_ref):
    rows = TPS * PATCHES
    per_core = tokens_ref.shape[0] * tokens_ref.shape[2]
    width = 2 * tokens_ref.shape[3]
    hot = lax.broadcasted_iota(jnp.int32, (rows, per_core), 0) == row_ref[...]
    hot = jnp.where(hot, 1.0, 0.0).astype(BF)
    halves = [
        jnp.dot(hot, tokens_ref[:, c].reshape(per_core, width // 2), preferred_element_type=F32) for c in range(2)
    ]
    tokens = (jnp.concatenate(halves, 1) + bias_ref[...]).astype(BF).astype(F32)
    mean = jnp.mean(tokens, axis=1, keepdims=True)
    shifted = tokens - mean
    var = jnp.mean(shifted * shifted, axis=1, keepdims=True)
    normed = (shifted * lax.rsqrt(var + 1e-05) * gain_ref[...]).astype(BF)
    keys_values = jnp.dot(normed, kv_ref[...], preferred_element_type=F32).astype(BF)
    keys, values = keys_values[:, :width], keys_values[:, width:].astype(F32)
    head = lax.broadcasted_iota(jnp.int32, (HEADS, width), 0)
    lane_head = lax.shift_right_logical(lax.broadcasted_iota(jnp.int32, (HEADS, width), 1), int(math.log2(HD)))
    query = jnp.concatenate(
        [jnp.where(head == lane_head, jnp.broadcast_to(latent_ref[l : l + 1], (HEADS, width)), 0.0) for l in range(LEVELS)],
        0,
    )
    scores = jnp.zeros((rows, LEVELS * HEADS), F32)
    for _ in range(3):
        piece = query.astype(BF)
        scores += lax.dot_general(keys, piece, NT, preferred_element_type=F32)
        query = query - piece.astype(F32)
    scores = (scores * (1.0 / math.sqrt(HD))).reshape(TPS, PATCHES, LEVELS * HEADS)
    top = jnp.max(scores, axis=0)
    expo = jnp.exp(scores - top[None])
    mass = jnp.sum(expo, axis=0)
    expo = expo.reshape(rows, LEVELS * HEADS).astype(BF)
    values = values.reshape(TPS, PATCHES, width)
    parts = []
    for value, count in ((top, 3), (mass, 2)):
        for _ in range(count):
            piece = value.astype(BF)
            parts.append(piece)
            value = value - piece.astype(F32)
    pick = lax.broadcasted_iota(jnp.int32, (LEVELS * HEADS, width), 0)
    stat_row = lax.broadcasted_iota(jnp.int32, (LEVELS * HEADS, FP), 0)
    stat_lane = lax.broadcasted_iota(jnp.int32, (LEVELS * HEADS, FP), 1)
    lane = lax.shift_right_logical(lax.broadcasted_iota(jnp.int32, (LEVELS * HEADS, width), 1), int(math.log2(HD)))
    blocks = []
    for level in range(LEVELS):
        wide = jnp.where(pick == lane + level * HEADS, 1.0, 0.0).astype(BF)
        share = jnp.dot(expo, wide, preferred_element_type=F32).reshape(TPS, PATCHES, width)
        partial = jnp.sum(share * values, axis=0)
        stats = jnp.zeros((PATCHES, FP), F32)
        for n, piece in enumerate(parts):
            to = (stat_row - level * HEADS == stat_lane - n * HEADS) & (stat_row >= level * HEADS) & (stat_row < (level + 1) * HEADS)
            stats += jnp.dot(piece, jnp.where(to, 1.0, 0.0).astype(BF), preferred_element_type=F32)
        blocks.append(jnp.concatenate([partial, stats], 1).astype(BF))
    stacked = jnp.concatenate(blocks, 0)
    count = LEVELS * PATCHES
    target = lax.broadcasted_iota(jnp.int32, (count, count), 0)
    source = lax.broadcasted_iota(jnp.int32, (count, count), 1)
    moved = (target & (LEVELS - 1)) * PATCHES + lax.shift_right_logical(target, 2) == source
    out_ref[...] = jnp.dot(jnp.where(moved, 1.0, 0.0).astype(BF), stacked, preferred_element_type=F32).astype(BF)


def attend(tokens, rows, bias, gain, kv_weight, latents):
    width = kv_weight.shape[0]
    return pl.pallas_call(
        attend_kernel,
        out_shape=jax.ShapeDtypeStruct((PATCHES * LEVELS, width + FP), BF),
        compiler_params=pltpu.CompilerParams(vmem_limit_bytes=VMEM_LIMIT),
        cost_estimate=pl.CostEstimate(flops=2 * 384 * 512 * 4000, bytes_accessed=3000000, transcendentals=12288),
        name="attend_source",
    )(tokens, rows, bias, gain, kv_weight, latents)


def finish_kernel(parts_ref, weight_ref, out_ref):
    sources, rows, wide = parts_ref.shape
    width = wide - FP
    stats = parts_ref[:, :, width:].reshape(sources * rows, FP)
    row = lax.broadcasted_iota(jnp.int32, (FP, width), 0)
    head = lax.shift_right_logical(lax.broadcasted_iota(jnp.int32, (FP, width), 1), int(math.log2(HD)))
    same = (row & (HEADS - 1)) == head
    is_top = jnp.where(same & (row < 3 * HEADS), 1.0, 0.0).astype(BF)
    is_mass = jnp.where(same & (row >= 3 * HEADS) & (row < 5 * HEADS), 1.0, 0.0).astype(BF)
    top = jnp.dot(stats, is_top, preferred_element_type=F32).reshape(sources, rows, width)
    mass = jnp.dot(stats, is_mass, preferred_element_type=F32).reshape(sources, rows, width)
    scale = jnp.exp(top - jnp.max(top, axis=0)[None])
    above = jnp.sum(scale * parts_ref[:, :, :width].astype(F32), axis=0)
    attended = (above / jnp.sum(scale * mass, axis=0)).astype(BF)
    out_ref[...] = jnp.dot(attended, weight_ref[...], preferred_element_type=F32)


def finish(parts, out_weight):
    return pl.pallas_call(
        finish_kernel,
        out_shape=jax.ShapeDtypeStruct((parts.shape[1], out_weight.shape[1]), F32),
        cost_estimate=pl.CostEstimate(flops=2 * 128 * 128 * 1024, bytes_accessed=800000, transcendentals=65536),
        name="combine_sources",
    )(parts, out_weight)


def device_at(y, x, core):
    return ((y % SIDE) * SIDE + x % SIDE) * 2 + core


def shift(offset, second):
    pairs = []
    for y in range(SIDE):
        for x in range(SIDE):
            for core in range(2):
                along_x = (core == 0) != second
                to = device_at(y, x + offset, core) if along_x else device_at(y + offset, x, core)
                pairs.append((device_at(y, x, core), to))
    return pairs


def send(array, offset, second):
    return lax.ppermute(array, "lat", shift(offset, second))


def gather_weights(shard):
    half = TAPS // 2
    up, down = send(shard, 1, False), send(shard, -1, False)
    far = [send(up[:half], 1, False), send(down[half:], -1, False)]
    line = jnp.stack([shard, up, down, jnp.concatenate(far, 0)], 0)
    above, below = send(line, 1, True), send(line, -1, True)
    return [line, above, below, send(above[:2], 1, True), send(below[2:], -1, True)]


def body(
    swath,
    tile_band,
    tile_patch,
    fp_pos,
    conv_weight,
    conv_bias,
    norm_gain,
    latents,
    kv_weight,
    out_weight,
):
    place = lax.axis_index("lat")
    core, chip = place % 2, place // 2
    chip_y, chip_x = chip // SIDE, chip % SIDE
    swath, fp_pos = swath[0], fp_pos[0]
    channels, cols = swath.shape[1], conv_weight.shape[4]
    width = kv_weight.shape[0]
    swap = [(i, i ^ 1) for i in range(2 * CHIPS)]

    shard = jnp.transpose(conv_weight[0].reshape(TAPS, channels, cols), (0, 2, 1))
    weights = gather_weights(shard)
    sib_swath = lax.ppermute(swath, "lat", swap)
    pos = fp_pos.astype(F32)
    sib_pos = lax.ppermute(fp_pos, "lat", swap).astype(F32)

    about = jnp.stack([tile_band[0, :, 0], tile_patch[0]], 1).astype(F32)
    record = jnp.concatenate([tile_mass(pos), about, jnp.zeros((TILES, 256 - CELLS - 2), F32)], 1)
    records = lax.all_gather(record, "lat")
    bands = records[:, :, CELLS].astype(jnp.int32)
    patches = records[:, :, CELLS + 1].astype(jnp.int32)
    target = bands * PATCHES + patches
    earlier = jnp.asarray(np.tril(np.ones((TILES, TILES), np.int32), -1))
    rank = jnp.sum((bands[:, :, None] == bands[:, None, :]).astype(jnp.int32) * earlier, axis=2)

    pick = jnp.stack([place, place ^ 1])
    bands_here, rank_here = jnp.take(bands, pick, axis=0), jnp.take(rank, pick, axis=0)
    target_here = jnp.take(target, pick, axis=0).reshape(2 * TILES)
    same = (target_here[:, None] == target.reshape(-1)[None, :]).astype(F32)
    density = 1.0 + jnp.dot(
        same, records[:, :, :CELLS].reshape(-1, CELLS), precision=lax.Precision.HIGHEST, preferred_element_type=F32
    )
    inverse = (1.0 / density).reshape(TILES, 2, TAPS, TPS)
    even, odd = inverse[:, 0], inverse[:, 1]
    inverse = jnp.concatenate([even, odd[..., 8:], odd[..., :8]], -1).reshape(2, TILES // 2, 1, TAPS * PAIR)

    center = jnp.asarray(
        np.concatenate([centers(list(range(TPS)) + [-1] * 4), centers([-1] * 4 + list(ROW_TOKEN[TPS:]))], 0)
    )
    own = gridded(swath, pos, inverse[0], center)
    sib = gridded(sib_swath, sib_pos, inverse[1], center)

    origin = jnp.stack([core, 1 - core])[:, None]
    slot = (bands_here * SLOTS + 2 * origin + rank_here) * TPS
    token_rows = jnp.asarray(np.tile(ROW_TOKEN, TILES))
    rows = (jnp.repeat(slot.reshape(-1), TPS) + token_rows)[None, :].astype(jnp.int32)
    near = jnp.tile(jnp.asarray(OFFSETS), SIDE)
    farther = jnp.repeat(jnp.asarray(OFFSETS), SIDE)
    at_y = (chip_y + jnp.where(core == 0, farther, near)) % SIDE
    at_x = (chip_x + jnp.where(core == 0, near, farther)) % SIDE
    columns = (jnp.repeat((at_y * SIDE + at_x) * cols, cols) + jnp.asarray(np.tile(np.arange(cols), CHIPS)))[None, :]
    outgoing = embed(own, sib, weights, columns.astype(jnp.int32), rows)

    outgoing = outgoing.reshape(2 * CHIPS, SLOTS * TPS, CHIPS * cols)
    incoming = lax.all_to_all(outgoing, "lat", split_axis=0, concat_axis=0, tiled=True)
    mine = (bands == place)[:, :, None] & (rank[:, :, None] == jnp.arange(2)[None, None, :])
    patch_in = jnp.sum(jnp.where(mine, patches[:, :, None] + 1, 0), axis=1).reshape(-1, 1) - 1
    token_in = jnp.where(patch_in < 0, -1, patch_in + PATCHES * jnp.arange(TPS)[None, :]).reshape(1, -1)

    def by_core(array):
        shape = array.shape[1:]
        split = array.reshape((CHIPS, 2, cols) + shape)
        return jnp.swapaxes(split, 0, 1).reshape((width,) + shape)

    parts = attend(
        incoming.reshape(CHIPS, 2, SLOTS * TPS, CHIPS * cols),
        token_in.astype(jnp.int32),
        by_core(conv_bias[0])[None],
        by_core(norm_gain)[None],
        by_core(kv_weight),
        latents,
    )
    sources = lax.axis_size("src")
    parts = lax.all_to_all(
        parts.reshape(sources, -1, width + FP), "src", split_axis=0, concat_axis=0, tiled=True
    )
    return finish(parts, out_weight).reshape(-1, LEVELS, width)


def solution(mesh):
    in_specs = (
        P("src", "lat", None, None),
        P("src", "lat", None),
        P("src", "lat"),
        P("src", "lat", None, None),
        P("src", None, None, None, "lat"),
        P("src", None),
        P(),
        P(),
        P(),
        P(),
    )
    out_specs = P(("lat", "src"), None, None)
    return jax.shard_map(body, mesh=mesh, in_specs=in_specs, out_specs=out_specs, check_vma=False)
```

profile of v0, /device:TPU:2, one launch (start us, length us, event | category | flops | bytes accessed | tf_op | source)
XLA Modules:
  0.0 162.8 jit_solution(10129240595077669601)
XLA Ops:
  6.5 1.4 bitcast_convert_fusion.pos_ref
  8.7 2.9 %tile_mass.1 = f32[32,192]{1,0:T(8,128)} custom-call(f32[32,2,128]{2,1,0:T(2,128)} %bitcast_convert_fusion.pos_ref, f32[2,192,128]{2,1,0:T(8,128)} %constant.105.clone.center_ref), custom_call_target="tpu_custom_call" | custom-call | flops 12582912 | bytes 300000 | tf_op jit(solution)/shard_map/tile_mass/pallas_call | solution.py:70
  11.7 1.5 maximum_maximum_fusion
  13.2 1.6 collective-permute-start.2
  14.8 0.9 collective-permute-start.3
  15.7 5.0 %collective-permute-done.2 = bf16[16,16,616]{2,1,0:T(8,128)(2,1)S(1)} collective-permute-done((bf16[16,16,616]{2,1,0:T(8,128)(2,1)S(1)}, bf16[16,16,616]{2,1,0:T(8,128)(2,1)S(1)}, u32[]{:S(2)}, u32[]{:S(2)}) %collective-permute-start.2) | collective-permute-done | bytes 315424 | tf_op jit(solution)/shard_map/ppermute | solution.py:290
  20.6 1.3 collective-permute-start.4
  22.0 2.1 %collective-permute-start.5 = (bf16[8,16,616]{2,1,0:T(8,128)(2,1)S(1)}, bf16[8,16,616]{2,1,0:T(8,128)(2,1)S(1)}, u32[]{:S(2)}, u32[]{:S(2)}) collective-permute-start(bf16[8,16,616]{2,1,0:T(8,128)(2,1)S(1)} %slice.70), channel_id=1, source_target_pairs={{0,48},{8,200},{16,0},{24,216},{32,16},{40,232},{48,32},{56,248},{... | collective-permute-start | bytes 473096 | tf_op jit(solution)/shard_map/ppermute | solution.py:290
  24.1 3.2 %collective-permute-done.4 = bf16[8,16,616]{2,1,0:T(8,128)(2,1)S(1)} collective-permute-done((bf16[8,16,616]{2,1,0:T(8,128)(2,1)S(1)}, bf16[8,16,616]{2,1,0:T(8,128)(2,1)S(1)}, u32[]{:S(2)}, u32[]{:S(2)}) %collective-permute-start.4) | collective-permute-done | bytes 157728 | tf_op jit(solution)/shard_map/ppermute | solution.py:290
  27.8 1.7 %collective-permute-start.6 = (bf16[4,16,16,616]{3,2,1,0:T(8,128)(2,1)S(1)}, bf16[4,16,16,616]{3,2,1,0:T(8,128)(2,1)S(1)}, u32[]{:S(2)}, u32[]{:S(2)}) collective-permute-start(bf16[4,16,16,616]{3,2,1,0:T(8,128)(2,1)S(1)} %pad_maximum_fusion.w0), channel_id=1, source_target_pairs={{0,64},{8,24},{16,80},{24,40},{32,96},{40,56},{48,112},{56,8},{64,... | collective-permute-start | bytes 3784712 | tf_op jit(solution)/shard_map/ppermute | solution.py:290
  29.4 1.7 %collective-permute-start.7 = (bf16[4,16,16,616]{3,2,1,0:T(8,128)(2,1)S(1)}, bf16[4,16,16,616]{3,2,1,0:T(8,128)(2,1)}, u32[]{:S(2)}, u32[]{:S(2)}) collective-permute-start(bf16[4,16,16,616]{3,2,1,0:T(8,128)(2,1)S(1)} %pad_maximum_fusion.w0), channel_id=1, source_target_pairs={{0,192},{8,56},{16,208},{24,8},{32,224},{40,24},{48,240},{56,40},{... | collective-permute-start | bytes 3784712 | tf_op jit(solution)/shard_map/ppermute | solution.py:290
  32.2 2.4 %copy.52 = bf16[16,2,16,1024]{3,2,0,1:T(8,128)(2,1)} copy(bf16[16,2,16,1024]{3,2,1,0:T(8,128)(2,1)} %bitcast.56) | data formatting | bytes 2097152 | tf_op jit(solution)/shard_map/reshape | solution.py:373
  38.0 9.2 %collective-permute-done.6.w1 = bf16[4,16,16,616]{3,2,1,0:T(8,128)(2,1)S(1)} collective-permute-done((bf16[4,16,16,616]{3,2,1,0:T(8,128)(2,1)S(1)}, bf16[4,16,16,616]{3,2,1,0:T(8,128)(2,1)S(1)}, u32[]{:S(2)}, u32[]{:S(2)}) %collective-permute-start.6) | collective-permute-done | bytes 1261600 | tf_op jit(solution)/shard_map/ppermute | solution.py:290
  47.2 1.0 slice.71
  48.4 2.0 %slice.72 = bf16[2,16,16,616]{3,2,1,0:T(8,128)(2,1)} slice(bf16[4,16,16,616]{3,2,1,0:T(8,128)(2,1)} %collective-permute-done.7.w2), slice={[2:4], [0:16], [0:16], [0:616]} | slice | bytes 1261568 | tf_op jit(solution)/shard_map/slice | solution.py:299
  50.4 3.0 %collective-permute-start.9 = (bf16[2,16,16,616]{3,2,1,0:T(8,128)(2,1)}, bf16[2,16,16,616]{3,2,1,0:T(8,128)(2,1)}, u32[]{:S(2)}, u32[]{:S(2)}) collective-permute-start(bf16[2,16,16,616]{3,2,1,0:T(8,128)(2,1)} %slice.72), channel_id=1, source_target_pairs={{0,192},{8,56},{16,208},{24,8},{32,224},{40,24},{48,240},{56,40},{... | collective-permute-start | bytes 1892360 | tf_op jit(solution)/shard_map/ppermute | solution.py:290
  53.4 10.9 %all-gather.3.cloned.1.call-done = f32[1024,256]{1,0:T(8,128)} async-done(((f32[32,256]{1,0:T(8,128)}), f32[1024,256]{1,0:T(8,128)}) %all-gather.3.cloned.1.call-update) | async-done | bytes 1048592 | tf_op jit(solution)/shard_map/all_gather | solution.py:330
  64.3 1.6 fusion.13
  67.6 0.8 select_reduce_fusion
  70.5 0.7 squeeze.25.inverse_ref
  71.2 0.7 squeeze.24.inverse_ref
  72.8 9.4 %grid_tiles.2.own_ref = bf16[16,384,616]{2,1,0:T(8,128)(2,1)} custom-call(bf16[32,616,128]{2,1,0:T(8,128)(2,1)} %bitcast.51, f32[32,2,128]{2,1,0:T(2,128)} %bitcast_convert_fusion.pos_ref, f32[16,1,384]{2,1,0:T(1,128)} %squeeze.24.inverse_ref, f32[4,256,128]{2,1,0:T(8,128)} %constant.107.clone.center_ref), custom_call_target="tpu_custom_call" | custom-call | flops 2415919104 | bytes 12615680 | tf_op jit(solution)/shard_map/grid_tiles/pallas_call | solution.py:99
  82.3 9.4 %grid_tiles.3.sib_ref = bf16[16,384,616]{2,1,0:T(8,128)(2,1)} custom-call(bf16[32,616,128]{2,1,0:T(8,128)(2,1)} %collective-permute-done.swath_ref, f32[32,2,128]{2,1,0:T(2,128)} %convert_element_type.46.pos_ref, f32[16,1,384]{2,1,0:T(1,128)} %squeeze.25.inverse_ref, f32[4,256,128]{2,1,0:T(8,128)} %constant.107.clone.center_ref), custom_call_target="tpu_custom_call" | custom-call | flops 2415919104 | bytes 12615680 | tf_op jit(solution)/shard_map/grid_tiles/pallas_call | solution.py:99
  91.6 0.8 copy-done.4
  92.5 17.4 %embed_tiles.1 = bf16[1536,256]{1,0:T(8,128)(2,1)} custom-call(bf16[16,384,616]{2,1,0:T(8,128)(2,1)} %grid_tiles.2.own_ref, bf16[16,384,616]{2,1,0:T(8,128)(2,1)} %grid_tiles.3.sib_ref, bf16[4,16,16,616]{3,2,1,0:T(8,128)(2,1)} %copy-done, bf16[4,16,16,616]{3,2,1,0:T(8,128)(2,1)} %copy-done.2, bf16[4,16,16,616]{3,2,1,0:T(8,128)(2,1)} %collective-permute-done.7.w2, ...), custom_call_target="tpu_custom_call" | custom-call | flops 4831838208 | bytes 20971520 | tf_op jit(solution)/shard_map/embed_tiles/pallas_call | solution.py:154
  109.9 6.0 %all-to-all-start = ((bf16[32,48,256]{2,1,0:T(8,128)(2,1)}), bf16[32,48,256]{2,1,0:T(8,128)(2,1)S(1)}, u32[]{:S(2)}, u32[]{:S(2)}) async-start(bf16[32,48,256]{2,1,0:T(8,128)(2,1)} %bitcast.54), calls=%async_computation | async-start | bytes 1572864 | tf_op jit(solution)/shard_map/all_to_all | solution.py:366
  117.0 12.2 %all-to-all-done = bf16[32,48,256]{2,1,0:T(8,128)(2,1)S(1)} async-done(((bf16[32,48,256]{2,1,0:T(8,128)(2,1)}), bf16[32,48,256]{2,1,0:T(8,128)(2,1)S(1)}, u32[]{:S(2)}, u32[]{:S(2)}) %all-to-all-start) | async-done | bytes 786464 | tf_op jit(solution)/shard_map/all_to_all | solution.py:366
  129.2 0.9 copy-done.3
  130.1 5.1 %attend_source.1 = bf16[128,640]{1,0:T(8,128)(2,1)} custom-call(bf16[16,2,48,256]{3,2,1,0:T(8,128)(2,1)} %bitcast.58, s32[1,768]{1,0:T(1,128)} %select_n.80.row_ref, f32[1,512]{1,0:T(1,128)} %broadcast_in_dim_reshape.8.bias_ref, f32[1,512]{1,0:T(1,128)} %broadcast_in_dim_reshape.9.gain_ref, bf16[512,1024]{1,0:T(8,128)(2,1)} %bitcast.57, f32[4,512]{1,0:T(4,128)} %latent_ref.1), custom_call_target="tpu_custom_call" | custom-call | flops 1572864000 | bytes 3000000 | tf_op jit(solution)/shard_map/attend_source/pallas_call | solution.py:239
  135.1 17.3 %all_to_all.10.parts_ref = bf16[8,16,640]{2,1,0:T(8,128)(2,1)} all-to-all(bf16[8,16,640]{2,1,0:T(8,128)(2,1)} %bitcast.64), channel_id=1, replica_groups=mesh['lat'=32,'src'=8] {'src'}, dimensions={0} | all-to-all | bytes 327680 | tf_op jit(solution)/shard_map/all_to_all | solution.py:385
  152.5 2.1 %combine_sources.1 = f32[16,512]{1,0:T(8,128)} custom-call(bf16[8,16,640]{2,1,0:T(8,128)(2,1)} %all_to_all.10.parts_ref, bf16[512,512]{1,0:T(8,128)(2,1)} %weight_ref.1), custom_call_target="tpu_custom_call" | custom-call | flops 33554432 | bytes 800000 | tf_op jit(solution)/shard_map/combine_sources/pallas_call | solution.py:266
  154.6 1.4 reshape.170
  (91 shorter events, 11.7 us)
Async XLA Ops:
  6.5 6.7 %copy-start.5 = (bf16[1,4,4,616,16]{3,4,2,1,0:T(8,128)(2,1)S(1)}, bf16[1,4,4,616,16]{3,4,2,1,0:T(8,128)(2,1)}, u32[]{:S(2)}) copy-start(bf16[1,4,4,616,16]{3,4,2,1,0:T(8,128)(2,1)} %param.23) | copy-start | bytes 946180
  6.5 57.7 %all-gather.3.cloned.1.call-start = ((), (), s32[]{:S(2)}) async-start(), calls=%async_computation.2 | async-start | bytes 1081344 | tf_op jit(solution)/shard_map/all_gather | solution.py:330
  6.5 75.7 %collective-permute-start = (bf16[32,616,128]{2,1,0:T(8,128)(2,1)}, bf16[32,616,128]{2,1,0:T(8,128)(2,1)}, u32[]{:S(2)}, u32[]{:S(2)}) collective-permute-start(bf16[32,616,128]{2,1,0:T(8,128)(2,1)} %bitcast.50), channel_id=1, source_target_pairs={{0,8},{8,0},{16,24},{24,16},{32,40},{40,32},{48,56},{56,48},{64,72... | collective-permute-start | bytes 15138824 | tf_op jit(solution)/shard_map/ppermute | solution.py:324
  13.2 7.4 %collective-permute-start.2 = (bf16[16,16,616]{2,1,0:T(8,128)(2,1)S(1)}, bf16[16,16,616]{2,1,0:T(8,128)(2,1)S(1)}, u32[]{:S(2)}, u32[]{:S(2)}) collective-permute-start(bf16[16,16,616]{2,1,0:T(8,128)(2,1)S(1)} %bitcast.61), channel_id=1, source_target_pairs={{0,16},{8,72},{16,32},{24,88},{32,48},{40,104},{48,0},{56,120},{64... | collective-permute-start | bytes 946184 | tf_op jit(solution)/shard_map/ppermute | solution.py:290
  14.8 7.2 %collective-permute-start.3 = (bf16[16,16,616]{2,1,0:T(8,128)(2,1)S(1)}, bf16[16,16,616]{2,1,0:T(8,128)(2,1)S(1)}, u32[]{:S(2)}, u32[]{:S(2)}) collective-permute-start(bf16[16,16,616]{2,1,0:T(8,128)(2,1)S(1)} %bitcast.62), channel_id=1, source_target_pairs={{0,48},{8,200},{16,0},{24,216},{32,16},{40,232},{48,32},{56,248},{... | collective-permute-start | bytes 946184 | tf_op jit(solution)/shard_map/ppermute | solution.py:290
  20.6 6.6 %collective-permute-start.4 = (bf16[8,16,616]{2,1,0:T(8,128)(2,1)S(1)}, bf16[8,16,616]{2,1,0:T(8,128)(2,1)S(1)}, u32[]{:S(2)}, u32[]{:S(2)}) collective-permute-start(bf16[8,16,616]{2,1,0:T(8,128)(2,1)S(1)} %slice.69), channel_id=1, source_target_pairs={{0,16},{8,72},{16,32},{24,88},{32,48},{40,104},{48,0},{56,120},{64... | collective-permute-start | bytes 473096 | tf_op jit(solution)/shard_map/ppermute | solution.py:290
  22.0 5.4 %collective-permute-start.5 = (bf16[8,16,616]{2,1,0:T(8,128)(2,1)S(1)}, bf16[8,16,616]{2,1,0:T(8,128)(2,1)S(1)}, u32[]{:S(2)}, u32[]{:S(2)}) collective-permute-start(bf16[8,16,616]{2,1,0:T(8,128)(2,1)S(1)} %slice.70), channel_id=1, source_target_pairs={{0,48},{8,200},{16,0},{24,216},{32,16},{40,232},{48,32},{56,248},{... | collective-permute-start | bytes 473096 | tf_op jit(solution)/shard_map/ppermute | solution.py:290
  27.4 3.7 %copy-start.7 = (bf16[1,32,2,128]{3,2,1,0:T(2,128)(2,1)S(1)}, bf16[1,32,2,128]{3,2,1,0:T(2,128)(2,1)}, u32[]{:S(2)}) copy-start(bf16[1,32,2,128]{3,2,1,0:T(2,128)(2,1)} %param.22) | copy-start | bytes 49156
  27.4 3.6 %copy-start.12 = (s32[4]{0:T(128)S(1)}, s32[4]{0:T(128)}, u32[]{:S(2)}) copy-start(s32[4]{0:T(128)} %constant.109.clone) | copy-start | bytes 52
  27.4 4.0 %copy-start.9 = (s32[16,16]{1,0:T(8,128)S(1)}, s32[16,16]{1,0:T(8,128)}, u32[]{:S(2)}) copy-start(s32[16,16]{1,0:T(8,128)} %constant.117) | copy-start | bytes 3076
  27.7 20.5 %copy-start = (bf16[4,16,16,616]{3,2,1,0:T(8,128)(2,1)}, bf16[4,16,16,616]{3,2,1,0:T(8,128)(2,1)S(1)}, u32[]{:S(2)}) copy-start(bf16[4,16,16,616]{3,2,1,0:T(8,128)(2,1)S(1)} %pad_maximum_fusion.w0) | copy-start | bytes 3784708
  27.7 7.5 %copy-start.11 = (f32[1,512]{1,0:T(1,128)S(1)}, f32[1,512]{1,0:T(1,128)}, u32[]{:S(2)}) copy-start(f32[1,512]{1,0:T(1,128)} %param.24) | copy-start | bytes 6148
  27.7 8.9 %copy-start.10 = (f32[512]{0:T(512)S(1)}, f32[512]{0:T(512)}, u32[]{:S(2)}) copy-start(f32[512]{0:T(512)} %param.25) | copy-start | bytes 6148
  27.8 19.4 %collective-permute-start.6 = (bf16[4,16,16,616]{3,2,1,0:T(8,128)(2,1)S(1)}, bf16[4,16,16,616]{3,2,1,0:T(8,128)(2,1)S(1)}, u32[]{:S(2)}, u32[]{:S(2)}) collective-permute-start(bf16[4,16,16,616]{3,2,1,0:T(8,128)(2,1)S(1)} %pad_maximum_fusion.w0), channel_id=1, source_target_pairs={{0,64},{8,24},{16,80},{24,40},{32,96},{40,56},{48,112},{56,8},{64,... | collective-permute-start | bytes 3784712 | tf_op jit(solution)/shard_map/ppermute | solution.py:290
  29.4 19.0 %collective-permute-start.7 = (bf16[4,16,16,616]{3,2,1,0:T(8,128)(2,1)S(1)}, bf16[4,16,16,616]{3,2,1,0:T(8,128)(2,1)}, u32[]{:S(2)}, u32[]{:S(2)}) collective-permute-start(bf16[4,16,16,616]{3,2,1,0:T(8,128)(2,1)S(1)} %pad_maximum_fusion.w0), channel_id=1, source_target_pairs={{0,192},{8,56},{16,208},{24,8},{32,224},{40,24},{48,240},{56,40},{... | collective-permute-start | bytes 3784712 | tf_op jit(solution)/shard_map/ppermute | solution.py:290
  31.1 6.3 %collective-permute-start.1 = (bf16[32,2,128]{2,1,0:T(2,128)(2,1)S(1)}, bf16[32,2,128]{2,1,0:T(2,128)(2,1)S(1)}, u32[]{:S(2)}, u32[]{:S(2)}) collective-permute-start(bf16[32,2,128]{2,1,0:T(2,128)(2,1)S(1)} %bitcast.67), channel_id=1, source_target_pairs={{0,8},{8,0},{16,24},{24,16},{32,40},{40,32},{48,56},{56,48},{64,72... | collective-permute-start | bytes 49160 | tf_op jit(solution)/shard_map/ppermute | solution.py:326
  47.2 3.2 %copy-start.2 = (bf16[4,16,16,616]{3,2,1,0:T(8,128)(2,1)}, bf16[4,16,16,616]{3,2,1,0:T(8,128)(2,1)S(1)}, u32[]{:S(2)}) copy-start(bf16[4,16,16,616]{3,2,1,0:T(8,128)(2,1)S(1)} %collective-permute-done.6.w1) | copy-start | bytes 3784708
  48.2 43.4 %collective-permute-start.8 = (bf16[2,16,16,616]{3,2,1,0:T(8,128)(2,1)}, bf16[2,16,16,616]{3,2,1,0:T(8,128)(2,1)S(1)}, u32[]{:S(2)}, u32[]{:S(2)}) collective-permute-start(bf16[2,16,16,616]{3,2,1,0:T(8,128)(2,1)} %slice.71), channel_id=1, source_target_pairs={{0,64},{8,24},{16,80},{24,40},{32,96},{40,56},{48,112},{56,8},{64,... | collective-permute-start | bytes 1892360 | tf_op jit(solution)/shard_map/ppermute | solution.py:290
  50.4 41.3 %collective-permute-start.9 = (bf16[2,16,16,616]{3,2,1,0:T(8,128)(2,1)}, bf16[2,16,16,616]{3,2,1,0:T(8,128)(2,1)}, u32[]{:S(2)}, u32[]{:S(2)}) collective-permute-start(bf16[2,16,16,616]{3,2,1,0:T(8,128)(2,1)} %slice.72), channel_id=1, source_target_pairs={{0,192},{8,56},{16,208},{24,8},{32,224},{40,24},{48,240},{56,40},{... | collective-permute-start | bytes 1892360 | tf_op jit(solution)/shard_map/ppermute | solution.py:290
  64.3 3.3 %copy-start.8 = (s32[32,32]{1,0:T(8,128)S(1)}, s32[32,32]{1,0:T(8,128)}, u32[]{:S(2)}) copy-start(s32[32,32]{1,0:T(8,128)} %constant.106.clone) | copy-start | bytes 12292
  64.3 4.9 %copy-start.1 = (f32[1024,256]{1,0:T(8,128)S(1)}, f32[1024,256]{1,0:T(8,128)}, u32[]{:S(2)}) copy-start(f32[1024,256]{1,0:T(8,128)} %all-gather.3.cloned.1.call-done) | copy-start | bytes 3145732
  70.1 1.9 %copy-start.6 = (s32[64,12]{1,0:T(8,128)S(1)}, s32[64,12]{1,0:T(8,128)}, u32[]{:S(2)}) copy-start(s32[64,12]{1,0:T(8,128)} %constant.118) | copy-start | bytes 9220
  91.6 0.9 copy-start.4
  109.9 19.3 %all-to-all-start = ((bf16[32,48,256]{2,1,0:T(8,128)(2,1)}), bf16[32,48,256]{2,1,0:T(8,128)(2,1)S(1)}, u32[]{:S(2)}, u32[]{:S(2)}) async-start(bf16[32,48,256]{2,1,0:T(8,128)(2,1)} %bitcast.54), calls=%async_computation | async-start | bytes 1572864 | tf_op jit(solution)/shard_map/all_to_all | solution.py:366
  129.2 0.9 copy-start.3
Sparse Core Ops, SparseCore 0:
  13.3 50.9 all-gather.2
where the time goes:
time: 164 us; the launch traced here: 163 us
  Pallas kernels  46.3 us (28%)
  waiting for transfers between devices  40.5 us (25%)
  local copies, waits for them, and re-layouts  19.3 us (12%)
  starting transfers between devices  18.4 us (11%)
  blocking collectives  17.3 us (11%)
  between operations  13.7 us (8%)
  other arithmetic  6.78 us (4%)
    pallas_call x2, Pallas kernels, gridded(): pl.pallas_call(grid_kernel, grid=(TILES // 4,), in_specs=[pl.BlockSpec((4...  18.8 us
    ppermute x8, waiting for transfers between devices, send(): return lax.ppermute(array, 'lat', shift(offset, second))  17.4 us
    pallas_call x1, Pallas kernels, embed(): pl.pallas_call(embed_kernel, grid=(TAPS,), in_specs=[pl.BlockSpec((1, hal...  17.4 us
    all_to_all x1, blocking collectives, body(): lax.all_to_all(parts.reshape(sources, -1, width + FP), 'src', split_axis=...  17.3 us
    ppermute x8, starting transfers between devices, send(): return lax.ppermute(array, 'lat', shift(offset, second))  12.4 us
    all_to_all x1, waiting for transfers between devices, body(): lax.all_to_all(outgoing, 'lat', split_axis=0, concat_axis=0, tiled=True)  12.2 us
    all_gather x1, waiting for transfers between devices, body(): records = lax.all_gather(record, 'lat')  10.9 us
    all_to_all x1, starting transfers between devices, body(): lax.all_to_all(outgoing, 'lat', split_axis=0, concat_axis=0, tiled=True)  6.01 us
  transfers between devices with their start and end apart: 12, of which 6 were waited for; matrix products, arithmetic and copies ran while one was open for 14% of the time, Pallas kernels for 13%

commit v1 on v0

--- a/solution.py
+++ b/solution.py
@@ -1,4 +1,3 @@
-import functools
 import math
 
 import jax
@@ -30,7 +29,8 @@
 BF = jnp.bfloat16
 F32 = jnp.float32
 NT = (((1,), (1,)), ((), ()))
-VMEM_LIMIT = 56 * 2**20
+KERNEL_VMEM = 24 * 2**20
+RECORD = 256
 
 
 def centers(tokens):
@@ -57,120 +57,144 @@
         base = pl.multiple_of(g * 8, 8)
         total = jnp.zeros((8, CELLS), F32)
         for j in range(8):
-            table = weights_at(pos_ref[base + j], center_ref, 0).astype(BF)
+            table = weights_at(pos_ref[base + j].astype(F32), center_ref, 0).astype(BF)
             row = lax.dot_general(ones, table, NT, preferred_element_type=F32)
             total = jnp.where(place == j, row, total)
-        out_ref[pl.ds(base, 8), :] = total
+        target = jnp.broadcast_to(pos_ref[pl.ds(base, 8), 2].astype(F32) * PATCHES + pos_ref[pl.ds(base, 8), 3].astype(F32), (8, FP))
+        out_ref[pl.ds(base, 8), :] = jnp.concatenate([total, target[:, : RECORD - CELLS]], 1)
         return carry
 
     lax.fori_loop(0, TILES // 8, group, 0)
 
 
-def tile_mass(pos):
+def tile_records(pos):
     return pl.pallas_call(
         mass_kernel,
-        out_shape=jax.ShapeDtypeStruct((TILES, CELLS), F32),
+        out_shape=jax.ShapeDtypeStruct((TILES, RECORD), F32),
         cost_estimate=pl.CostEstimate(flops=2 * TILES * 8 * FP * CELLS, bytes_accessed=300000, transcendentals=TILES * FP * CELLS),
-        name="tile_mass",
+        name="tile_records",
     )(pos, jnp.asarray(centers(range(TPS))))
 
 
-def grid_kernel(swath_ref, pos_ref, inverse_ref, center_ref, out_ref):
-    blocks = []
+def inverse_kernel(record_ref, target_ref, row_tile_ref, own_cell_ref, tap_ref, out_ref):
+    same = jnp.where(record_ref[:, CELLS : CELLS + 1] == target_ref[...], 1.0, 0.0).astype(BF)
+    mass = record_ref[:, :CELLS]
+    total = jnp.ones((CELLS, target_ref.shape[1]), F32)
+    for _ in range(3):
+        piece = mass.astype(BF)
+        total += lax.dot_general(piece, same, (((0,), (0,)), ((), ())), preferred_element_type=F32)
+        mass = mass - piece.astype(F32)
+    inverse = 1.0 / total
+    out = jnp.zeros(out_ref.shape, F32)
+    for _ in range(3):
+        piece = inverse.astype(BF)
+        spread = jnp.dot(piece, row_tile_ref[...], preferred_element_type=F32).astype(BF) * own_cell_ref[...]
+        out += jnp.dot(tap_ref[...], spread, preferred_element_type=F32)
+        inverse = inverse - piece.astype(F32)
+    out_ref[...] = out
+
+
+def inverse_density(records, targets):
+    rows = 2 * TILES * TPS
+    row_tile = (np.arange(2 * TILES)[:, None] == np.arange(rows)[None, :] // TPS).astype(np.float32)
+    token = np.tile(ROW_TOKEN, TILES)
+    own_cell = (np.arange(CELLS)[:, None] % TPS == token[None, :]).astype(np.float32)
+    tap = (np.arange(TAPS)[:, None] == np.arange(CELLS)[None, :] // TPS).astype(np.float32)
+    return pl.pallas_call(
+        inverse_kernel,
+        out_shape=jax.ShapeDtypeStruct((TAPS, rows), F32),
+        compiler_params=pltpu.CompilerParams(vmem_limit_bytes=KERNEL_VMEM),
+        cost_estimate=pl.CostEstimate(flops=6 * 1024 * CELLS * 128, bytes_accessed=2000000, transcendentals=0),
+        name="inverse_density",
+    )(records, targets, *(jnp.asarray(v, BF) for v in (row_tile, own_cell, tap)))
+
+
+def grid_kernel(swath_ref, pos_ref, center_ref, out_ref):
+    channels = swath_ref.shape[1]
     gap = jnp.zeros((TAPS, 8, FP), F32)
-    channels = swath_ref.shape[1]
-    for pair in range(2):
-        first, second = 2 * pair, 2 * pair + 1
-        left = weights_at(pos_ref[first], center_ref, 0).reshape(TAPS, 16, FP)
-        right = weights_at(pos_ref[second], center_ref, 2).reshape(TAPS, 16, FP)
-        left = jnp.concatenate([left, gap], 1).reshape(TAPS * PAIR, FP)
-        right = jnp.concatenate([gap, right], 1).reshape(TAPS * PAIR, FP)
-        table = jnp.concatenate([left, right], 1).astype(BF)
-        data = jnp.concatenate([swath_ref[first], swath_ref[second]], 1)
-        total = lax.dot_general(table, data, NT, preferred_element_type=F32)
-        scale = jnp.broadcast_to(inverse_ref[pair], (FP, TAPS * PAIR)).T
-        scale = jnp.concatenate([scale] * (-(-channels // FP)), 1)[:, :channels]
-        blocks.append((total * scale).reshape(TAPS, PAIR, channels))
-    out_ref[...] = jnp.concatenate(blocks, 1).astype(BF)
-
-
-def gridded(swath, pos, inverse, center):
+
+    def step(tiles_ref):
+        i = pl.program_id(0)
+        blocks = []
+        for pair in range(2):
+            first, second = 4 * i + 2 * pair, 4 * i + 2 * pair + 1
+            left = weights_at(pos_ref[first].astype(F32), center_ref, 0).reshape(TAPS, 16, FP)
+            right = weights_at(pos_ref[second].astype(F32), center_ref, 2).reshape(TAPS, 16, FP)
+            left = jnp.concatenate([left, gap], 1).reshape(TAPS * PAIR, FP)
+            right = jnp.concatenate([gap, right], 1).reshape(TAPS * PAIR, FP)
+            table = jnp.concatenate([left, right], 1).astype(BF)
+            data = jnp.concatenate([tiles_ref[2 * pair], tiles_ref[2 * pair + 1]], 1)
+            total = lax.dot_general(table, data, NT, preferred_element_type=F32)
+            blocks.append(total.reshape(TAPS, PAIR, channels))
+        base = pl.multiple_of(i * 2 * PAIR, 2 * PAIR)
+        out_ref[:, pl.ds(base, 2 * PAIR), :] = jnp.concatenate(blocks, 1).astype(BF)
+
+    pltpu.emit_pipeline(
+        step, grid=(TILES // 4,), in_specs=[pl.BlockSpec((4, channels, FP), lambda i: (i, 0, 0))]
+    )(swath_ref)
+
+
+def gridded(swath, pos, center):
     channels = swath.shape[1]
+    vmem = pl.BlockSpec(memory_space=pltpu.VMEM)
     return pl.pallas_call(
         grid_kernel,
-        grid=(TILES // 4,),
-        in_specs=[
-            pl.BlockSpec((4, channels, FP), lambda i: (i, 0, 0)),
-            pl.BlockSpec((4, 2, FP), lambda i: (i, 0, 0)),
-            pl.BlockSpec((2, 1, TAPS * PAIR), lambda i: (i, 0, 0)),
-            pl.BlockSpec((4, TAPS * 16, FP), lambda i: (0, 0, 0)),
-        ],
-        out_specs=pl.BlockSpec((TAPS, 2 * PAIR, channels), lambda i: (0, i, 0)),
-        out_shape=jax.ShapeDtypeStruct((TAPS, TILES * TPS, channels), BF),
-        compiler_params=pltpu.CompilerParams(vmem_limit_bytes=VMEM_LIMIT),
+        in_specs=[pl.BlockSpec(memory_space=pl.ANY), vmem, vmem],
+        out_specs=vmem,
+        out_shape=pltpu.VMEM((TAPS, TILES * TPS, channels), BF),
+        compiler_params=pltpu.CompilerParams(vmem_limit_bytes=KERNEL_VMEM),
         cost_estimate=pl.CostEstimate(
             flops=2 * (TILES // 2) * TAPS * PAIR * 2 * FP * 768,
-            bytes_accessed=TILES * channels * (FP + CELLS) * 2,
+            bytes_accessed=TILES * channels * FP * 2,
             transcendentals=TILES * FP * 256,
         ),
         name="grid_tiles",
-    )(swath, pos, inverse, center)
-
-
-def embed_kernel(own_ref, sib_ref, w0, w1, w2, w3, w4, column_ref, row_ref, out_ref, total, spread):
-    step = pl.program_id(0)
-    slot_rows = out_ref.shape[0]
+    )(swath, pos, center)
+
+
+def embed_kernel(own_ref, sib_ref, w0, w1, w2, w3, w4, inverse_ref, column_ref, row_ref, out_ref, total, spread):
+    channels = own_ref.shape[2]
+    slot_rows, half = out_ref.shape[0], own_ref.shape[1]
     part = slot_rows // TAPS
-
-    @pl.when(step == 0)
-    def _():
-        total[...] = jnp.zeros_like(total)
-
-    channels = own_ref.shape[2]
-    weight = jnp.concatenate([w[...].reshape(-1, channels) for w in (w0, w1, w2, w3, w4)], 0)
+    width = total.shape[1]
+    total[...] = jnp.zeros_like(total)
+
+    def tap(k, carry):
+        weight = jnp.concatenate([w[:, k].reshape(-1, channels) for w in (w0, w1, w2, w3, w4)], 0)
+        scale = jnp.broadcast_to(inverse_ref[pl.ds(k, 1), :], (FP, 2 * half)).T
+        scale = jnp.concatenate([scale] * (width // FP), 1)
+        for n, ref in enumerate((own_ref, sib_ref)):
+            rows = slice(n * half, (n + 1) * half)
+            product = lax.dot_general(ref[k], weight, NT, preferred_element_type=F32)
+            total[rows] += product * scale[rows]
+        base = pl.multiple_of(k * part, part)
+        here = lax.broadcasted_iota(jnp.int32, (part, 2 * half), 0) + base
+        spread[pl.ds(base, part), :] = jnp.where(here == row_ref[...], 1.0, 0.0).astype(BF)
+        return carry
+
+    lax.fori_loop(0, TAPS, tap, 0)
+    columns = lax.broadcasted_iota(jnp.int32, (width, width), 0)
+    order = jnp.where(columns == column_ref[...], 1.0, 0.0).astype(BF)
+    tokens = lax.dot_general(total[...].astype(BF), order, NT, preferred_element_type=F32).astype(BF)
+    out_ref[...] = jnp.dot(spread[...], tokens, preferred_element_type=F32).astype(BF)
+
+
+def embed(own, sib, weights, inverse, columns, rows):
+    width = CHIPS * weights[0].shape[2]
+    slot_rows = 2 * CHIPS * SLOTS * TPS
     half = TILES * TPS
-    total[:half] += lax.dot_general(own_ref[0], weight, NT, preferred_element_type=F32)
-    total[half:] += lax.dot_general(sib_ref[0], weight, NT, preferred_element_type=F32)
-    base = pl.multiple_of(step * part, part)
-    here = lax.broadcasted_iota(jnp.int32, (part, 2 * half), 0) + base
-    spread[pl.ds(base, part), :] = jnp.where(here == row_ref[...], 1.0, 0.0).astype(BF)
-
-    @pl.when(step == TAPS - 1)
-    def _():
-        width = total.shape[1]
-        columns = lax.broadcasted_iota(jnp.int32, (width, width), 0)
-        order = jnp.where(columns == column_ref[...], 1.0, 0.0).astype(BF)
-        tokens = total[...].astype(BF)
-        tokens = lax.dot_general(tokens, order, NT, preferred_element_type=F32).astype(BF)
-        out_ref[...] = jnp.dot(spread[...], tokens, preferred_element_type=F32).astype(BF)
-
-
-def embed(own, sib, weights, columns, rows):
-    channels = own.shape[2]
-    cols = weights[0].shape[2]
-    width = CHIPS * cols
-    slot_rows = 32 * SLOTS * TPS
-    half = TILES * TPS
+    vmem = pl.BlockSpec(memory_space=pltpu.VMEM)
+    large = [pltpu.with_memory_space_constraint(a, pltpu.VMEM) for a in (own, sib, *weights)]
     return pl.pallas_call(
         embed_kernel,
-        grid=(TAPS,),
-        in_specs=[pl.BlockSpec((1, half, channels), lambda i: (i, 0, 0))] * 2
-        + [pl.BlockSpec((w.shape[0], 1, cols, channels), lambda i: (0, i, 0, 0)) for w in weights]
-        + [
-            pl.BlockSpec((1, width), lambda i: (0, 0)),
-            pl.BlockSpec((1, 2 * half), lambda i: (0, 0)),
-        ],
-        out_specs=pl.BlockSpec((slot_rows, width), lambda i: (0, 0)),
+        in_specs=[vmem] * (len(large) + 3),
+        out_specs=vmem,
         out_shape=jax.ShapeDtypeStruct((slot_rows, width), BF),
         scratch_shapes=[pltpu.VMEM((2 * half, width), F32), pltpu.VMEM((slot_rows, 2 * half), BF)],
-        compiler_params=pltpu.CompilerParams(vmem_limit_bytes=VMEM_LIMIT),
-        cost_estimate=pl.CostEstimate(
-            flops=2 * TAPS * 2 * half * 768 * width,
-            bytes_accessed=TAPS * (2 * half + width) * 640 * 2,
-            transcendentals=0,
-        ),
+        compiler_params=pltpu.CompilerParams(vmem_limit_bytes=KERNEL_VMEM),
+        cost_estimate=pl.CostEstimate(flops=2 * TAPS * 2 * half * 768 * width * 2, bytes_accessed=1000000, transcendentals=0),
         name="embed_tiles",
-    )(own, sib, *weights, columns, rows)
+    )(*large, inverse, columns, rows)
 
 
 def attend_kernel(tokens_ref, row_ref, bias_ref, gain_ref, kv_ref, latent_ref, out_ref):
@@ -239,7 +263,7 @@
     return pl.pallas_call(
         attend_kernel,
         out_shape=jax.ShapeDtypeStruct((PATCHES * LEVELS, width + FP), BF),
-        compiler_params=pltpu.CompilerParams(vmem_limit_bytes=VMEM_LIMIT),
+        compiler_params=pltpu.CompilerParams(vmem_limit_bytes=KERNEL_VMEM),
         cost_estimate=pl.CostEstimate(flops=2 * 384 * 512 * 4000, bytes_accessed=3000000, transcendentals=12288),
         name="attend_source",
     )(tokens, rows, bias, gain, kv_weight, latents)
@@ -259,13 +283,15 @@
     scale = jnp.exp(top - jnp.max(top, axis=0)[None])
     above = jnp.sum(scale * parts_ref[:, :, :width].astype(F32), axis=0)
     attended = (above / jnp.sum(scale * mass, axis=0)).astype(BF)
-    out_ref[...] = jnp.dot(attended, weight_ref[...], preferred_element_type=F32)
+    result = jnp.dot(attended, weight_ref[...], preferred_element_type=F32)
+    for patch in range(rows // LEVELS):
+        out_ref[patch] = result[patch * LEVELS : (patch + 1) * LEVELS]
 
 
 def finish(parts, out_weight):
     return pl.pallas_call(
         finish_kernel,
-        out_shape=jax.ShapeDtypeStruct((parts.shape[1], out_weight.shape[1]), F32),
+        out_shape=jax.ShapeDtypeStruct((parts.shape[1] // LEVELS, LEVELS, out_weight.shape[1]), F32),
         cost_estimate=pl.CostEstimate(flops=2 * 128 * 128 * 1024, bytes_accessed=800000, transcendentals=65536),
         name="combine_sources",
     )(parts, out_weight)
@@ -322,37 +348,30 @@
     shard = jnp.transpose(conv_weight[0].reshape(TAPS, channels, cols), (0, 2, 1))
     weights = gather_weights(shard)
     sib_swath = lax.ppermute(swath, "lat", swap)
-    pos = fp_pos.astype(F32)
-    sib_pos = lax.ppermute(fp_pos, "lat", swap).astype(F32)
-
-    about = jnp.stack([tile_band[0, :, 0], tile_patch[0]], 1).astype(F32)
-    record = jnp.concatenate([tile_mass(pos), about, jnp.zeros((TILES, 256 - CELLS - 2), F32)], 1)
-    records = lax.all_gather(record, "lat")
-    bands = records[:, :, CELLS].astype(jnp.int32)
-    patches = records[:, :, CELLS + 1].astype(jnp.int32)
-    target = bands * PATCHES + patches
-    earlier = jnp.asarray(np.tril(np.ones((TILES, TILES), np.int32), -1))
-    rank = jnp.sum((bands[:, :, None] == bands[:, None, :]).astype(jnp.int32) * earlier, axis=2)
-
-    pick = jnp.stack([place, place ^ 1])
-    bands_here, rank_here = jnp.take(bands, pick, axis=0), jnp.take(rank, pick, axis=0)
-    target_here = jnp.take(target, pick, axis=0).reshape(2 * TILES)
-    same = (target_here[:, None] == target.reshape(-1)[None, :]).astype(F32)
-    density = 1.0 + jnp.dot(
-        same, records[:, :, :CELLS].reshape(-1, CELLS), precision=lax.Precision.HIGHEST, preferred_element_type=F32
-    )
-    inverse = (1.0 / density).reshape(TILES, 2, TAPS, TPS)
-    even, odd = inverse[:, 0], inverse[:, 1]
-    inverse = jnp.concatenate([even, odd[..., 8:], odd[..., :8]], -1).reshape(2, TILES // 2, 1, TAPS * PAIR)
-
+    band, patch = tile_band[0, :, 0], tile_patch[0]
+    about = jnp.broadcast_to(jnp.stack([band, patch], 1).astype(BF)[:, :, None], fp_pos.shape)
+    pos = jnp.concatenate([fp_pos, about], 1)
+    sib_pos = lax.ppermute(pos, "lat", swap)
+
+    records = lax.all_gather(tile_records(pos), "lat")
     center = jnp.asarray(
         np.concatenate([centers(list(range(TPS)) + [-1] * 4), centers([-1] * 4 + list(ROW_TOKEN[TPS:]))], 0)
     )
-    own = gridded(swath, pos, inverse[0], center)
-    sib = gridded(sib_swath, sib_pos, inverse[1], center)
+    own = gridded(swath, pos, center)
+    sib = gridded(sib_swath, sib_pos, center)
+    sib_about = sib_pos[:, 2:, 0].astype(jnp.int32)
+    bands_here = jnp.stack([band, sib_about[:, 0]])
+    patches_here = jnp.stack([patch, sib_about[:, 1]])
+    targets = (bands_here * PATCHES + patches_here).reshape(1, -1).astype(F32)
+    inverse = inverse_density(records.reshape(-1, RECORD), targets)
+
+    earlier = jnp.asarray(np.tril(np.ones((TILES, TILES), np.int32), -1))
+
+    def rank_of(named):
+        return jnp.sum((named[:, :, None] == named[:, None, :]).astype(jnp.int32) * earlier, axis=2)
 
     origin = jnp.stack([core, 1 - core])[:, None]
-    slot = (bands_here * SLOTS + 2 * origin + rank_here) * TPS
+    slot = (bands_here * SLOTS + 2 * origin + rank_of(bands_here)) * TPS
     token_rows = jnp.asarray(np.tile(ROW_TOKEN, TILES))
     rows = (jnp.repeat(slot.reshape(-1), TPS) + token_rows)[None, :].astype(jnp.int32)
     near = jnp.tile(jnp.asarray(OFFSETS), SIDE)
@@ -360,10 +379,13 @@
     at_y = (chip_y + jnp.where(core == 0, farther, near)) % SIDE
     at_x = (chip_x + jnp.where(core == 0, near, farther)) % SIDE
     columns = (jnp.repeat((at_y * SIDE + at_x) * cols, cols) + jnp.asarray(np.tile(np.arange(cols), CHIPS)))[None, :]
-    outgoing = embed(own, sib, weights, columns.astype(jnp.int32), rows)
+    outgoing = embed(own, sib, weights, inverse, columns.astype(jnp.int32), rows)
 
     outgoing = outgoing.reshape(2 * CHIPS, SLOTS * TPS, CHIPS * cols)
     incoming = lax.all_to_all(outgoing, "lat", split_axis=0, concat_axis=0, tiled=True)
+    target = records[:, :, CELLS].astype(jnp.int32)
+    bands, patches = target // PATCHES, target % PATCHES
+    rank = rank_of(bands)
     mine = (bands == place)[:, :, None] & (rank[:, :, None] == jnp.arange(2)[None, None, :])
     patch_in = jnp.sum(jnp.where(mine, patches[:, :, None] + 1, 0), axis=1).reshape(-1, 1) - 1
     token_in = jnp.where(patch_in < 0, -1, patch_in + PATCHES * jnp.arange(TPS)[None, :]).reshape(1, -1)
@@ -385,7 +407,7 @@
     parts = lax.all_to_all(
         parts.reshape(sources, -1, width + FP), "src", split_axis=0, concat_axis=0, tiled=True
     )
-    return finish(parts, out_weight).reshape(-1, LEVELS, width)
+    return finish(parts, out_weight)
 
 
 def solution(mesh):

time: 164 us -> 140 us (0.85)
  Pallas kernels: 46.3 us -> 34.1 us
  waiting for transfers between devices: 40.5 us -> 30.9 us
    pallas_call x4 -> x5, Pallas kernels: 39.1 us -> 29 us  [the longest x2 12.7 us: gridded(): pl.pallas_call(grid_kernel, in_specs=[pl.BlockSpec(memory_space=pl.ANY),...]
    unnamed x29 -> x64, local copies, waits for them, and re-layouts: 2.87 us -> 8.84 us
    all_gather x1, waiting for transfers between devices: 10.9 us -> 5.46 us  [body(): records = lax.all_gather(tile_records(pos), 'lat')]
    ppermute x8, waiting for transfers between devices: 17.4 us -> 12.7 us  [send(): return lax.ppermute(array, 'lat', shift(offset, second))]
    convert_element_type x4 -> x1, other arithmetic: 2.69 us -> 0.03 us  [body(): sib_about = sib_pos[:, 2:, 0].astype(jnp.int32)]
    pallas_call x1, Pallas kernels: 5.06 us -> 2.9 us  [attend(): pl.pallas_call(attend_kernel, out_shape=jax.ShapeDtypeStruct((PATCHES * L...]
    reshape x3 -> x0, local copies, waits for them, and re-layouts: 1.77 us -> none  [the longest x1 1.38 us: body(): return finish(parts, out_weight).reshape(-1, LEVELS, width)]
    gather x3 -> x0, local copies, waits for them, and re-layouts: 1.68 us -> none  [the longest x1 0.56 us: body(): jnp.take(rank, pick, axis=0)]
  transfers between devices with their start and end apart: 12 -> 12, of which waited for: 6 -> 5; matrix products, arithmetic and copies ran while one was open for 14% -> 13% of each run, Pallas kernels for 13% -> 12%
where the time goes in v1:
time: 140 us; the launch traced here: 139 us
  Pallas kernels  34.1 us (24%)
  waiting for transfers between devices  30.9 us (22%)
  local copies, waits for them, and re-layouts  19.5 us (14%)
  starting transfers between devices  18.5 us (13%)
  blocking collectives  17.1 us (12%)
  between operations  13.9 us (10%)
  other arithmetic  5.28 us (4%)
    all_to_all x1, blocking collectives, body(): lax.all_to_all(parts.reshape(sources, -1, width + FP), 'src', split_axis=...  17.1 us
    all_to_all x1, waiting for transfers between devices, body(): lax.all_to_all(outgoing, 'lat', split_axis=0, concat_axis=0, tiled=True)  12.8 us
    pallas_call x2, Pallas kernels, gridded(): pl.pallas_call(grid_kernel, in_specs=[pl.BlockSpec(memory_space=pl.ANY),...  12.7 us
    ppermute x8, waiting for transfers between devices, send(): return lax.ppermute(array, 'lat', shift(offset, second))  12.7 us
    pallas_call x1, Pallas kernels, embed(): pl.pallas_call(embed_kernel, in_specs=[vmem] * (len(large) + 3), out_spec...  11.9 us
    ppermute x8, starting transfers between devices, send(): return lax.ppermute(array, 'lat', shift(offset, second))  11.8 us
    unnamed x64, local copies, waits for them, and re-layouts  8.84 us
    all_to_all x1, starting transfers between devices, body(): lax.all_to_all(outgoing, 'lat', split_axis=0, concat_axis=0, tiled=True)  5.73 us
  transfers between devices with their start and end apart: 12, of which 5 were waited for; matrix products, arithmetic and copies ran while one was open for 13% of the time, Pallas kernels for 12%

profile of v1, /device:TPU:2, one launch (start us, length us, event | category | flops | bytes accessed | tf_op | source)
XLA Modules:
  0.0 139.4 jit_solution(9401530631207392633)
XLA Ops:
  6.5 1.5 %collective-permute-start.2 = (bf16[16,16,616]{2,1,0:T(8,128)(2,1)}, bf16[16,16,616]{2,1,0:T(8,128)(2,1)S(1)}, u32[]{:S(2)}, u32[]{:S(2)}) collective-permute-start(bf16[16,16,616]{2,1,0:T(8,128)(2,1)} %bitcast.72), channel_id=1, source_target_pairs={{0,16},{8,72},{16,32},{24,88},{32,48},{40,104},{48,0},{56,120},{64... | collective-permute-start | bytes 946184 | tf_op jit(solution)/shard_map/ppermute | solution.py:316
  8.0 0.9 collective-permute-start.3
  10.4 0.8 pad_maximum_fusion.1.pos_ref
  11.2 1.0 collective-permute-start.1
  12.2 3.0 %tile_records.1 = f32[32,256]{1,0:T(8,128)} custom-call(bf16[32,4,128]{2,1,0:T(4,128)(2,1)} %copy-done.8, f32[2,192,128]{2,1,0:T(8,128)} %constant.122.clone.center_ref), custom_call_target="tpu_custom_call" | custom-call | flops 12582912 | bytes 300000 | tf_op jit(solution)/shard_map/tile_records/pallas_call | solution.py:71
  15.3 2.4 %copy-done.1 = bf16[1,32,616,128]{3,2,1,0:T(8,128)(2,1)S(1)} copy-done((bf16[1,32,616,128]{3,2,1,0:T(8,128)(2,1)S(1)}, bf16[1,32,616,128]{3,2,1,0:T(8,128)(2,1)}, u32[]{:S(2)}) %copy-start.1) | copy-done | bytes 5046296
  17.7 0.8 copy-done.9
  18.4 5.5 %grid_tiles.2.own_ref = bf16[16,384,616]{2,1,0:T(8,128)(2,1)S(1)} custom-call(bf16[32,616,128]{2,1,0:T(8,128)(2,1)S(1)} %bitcast.64, bf16[32,4,128]{2,1,0:T(4,128)(2,1)S(1)} %copy-done.9, f32[4,256,128]{2,1,0:T(8,128)S(1)} %copy-done.3), custom_call_target="tpu_custom_call" | custom-call | flops 2415919104 | bytes 5046272 | tf_op jit(solution)/shard_map/grid_tiles/pallas_call | solution.py:140
  24.0 3.1 %copy-done = bf16[16,384,616]{2,1,0:T(8,128)(2,1)} copy-done((bf16[16,384,616]{2,1,0:T(8,128)(2,1)}, bf16[16,384,616]{2,1,0:T(8,128)(2,1)S(1)}, u32[]{:S(2)}) %copy-start) | copy-done | bytes 7569432
  27.3 1.6 %collective-permute-start.4 = (bf16[8,16,616]{2,1,0:T(8,128)(2,1)S(1)}, bf16[8,16,616]{2,1,0:T(8,128)(2,1)S(1)}, u32[]{:S(2)}, u32[]{:S(2)}) collective-permute-start(bf16[8,16,616]{2,1,0:T(8,128)(2,1)S(1)} %slice.32), channel_id=1, source_target_pairs={{0,16},{8,72},{16,32},{24,88},{32,48},{40,104},{48,0},{56,120},{64... | collective-permute-start | bytes 473096 | tf_op jit(solution)/shard_map/ppermute | solution.py:316
  28.9 1.4 collective-permute-start.5
  30.4 3.2 %collective-permute-done.4 = bf16[8,16,616]{2,1,0:T(8,128)(2,1)S(1)} collective-permute-done((bf16[8,16,616]{2,1,0:T(8,128)(2,1)S(1)}, bf16[8,16,616]{2,1,0:T(8,128)(2,1)S(1)}, u32[]{:S(2)}, u32[]{:S(2)}) %collective-permute-start.4) | collective-permute-done | bytes 157728 | tf_op jit(solution)/shard_map/ppermute | solution.py:316
  33.6 0.9 collective-permute-done.5
  34.9 1.0 collective-permute-start.6
  35.9 2.3 %collective-permute-start.7 = (bf16[4,16,16,616]{3,2,1,0:T(8,128)(2,1)S(1)}, bf16[4,16,16,616]{3,2,1,0:T(8,128)(2,1)}, u32[]{:S(2)}, u32[]{:S(2)}) collective-permute-start(bf16[4,16,16,616]{3,2,1,0:T(8,128)(2,1)S(1)} %pad_maximum_fusion.w0), channel_id=1, source_target_pairs={{0,192},{8,56},{16,208},{24,8},{32,224},{40,24},{48,240},{56,40},{... | collective-permute-start | bytes 3784712 | tf_op jit(solution)/shard_map/ppermute | solution.py:316
  39.5 2.3 %copy.44 = bf16[16,2,16,1024]{3,2,0,1:T(8,128)(2,1)} copy(bf16[16,2,16,1024]{3,2,1,0:T(8,128)(2,1)} %bitcast.69) | data formatting | bytes 2097152 | tf_op jit(solution)/shard_map/reshape | solution.py:395
  45.3 8.6 %collective-permute-done.6.w1 = bf16[4,16,16,616]{3,2,1,0:T(8,128)(2,1)S(1)} collective-permute-done((bf16[4,16,16,616]{3,2,1,0:T(8,128)(2,1)S(1)}, bf16[4,16,16,616]{3,2,1,0:T(8,128)(2,1)S(1)}, u32[]{:S(2)}, u32[]{:S(2)}) %collective-permute-start.6) | collective-permute-done | bytes 1261600 | tf_op jit(solution)/shard_map/ppermute | solution.py:316
  53.9 1.0 slice.34
  54.9 2.0 %slice.35 = bf16[2,16,16,616]{3,2,1,0:T(8,128)(2,1)} slice(bf16[4,16,16,616]{3,2,1,0:T(8,128)(2,1)} %collective-permute-done.7.w2), slice={[2:4], [0:16], [0:16], [0:616]} | slice | bytes 1261568 | tf_op jit(solution)/shard_map/slice | solution.py:325
  57.0 3.2 %collective-permute-start.9 = (bf16[2,16,16,616]{3,2,1,0:T(8,128)(2,1)}, bf16[2,16,16,616]{3,2,1,0:T(8,128)(2,1)}, u32[]{:S(2)}, u32[]{:S(2)}) collective-permute-start(bf16[2,16,16,616]{3,2,1,0:T(8,128)(2,1)} %slice.35), channel_id=1, source_target_pairs={{0,192},{8,56},{16,208},{24,8},{32,224},{40,24},{48,240},{56,40},{... | collective-permute-start | bytes 1892360 | tf_op jit(solution)/shard_map/ppermute | solution.py:316
  60.2 5.5 %all-gather.3.cloned.1.call-done.record_ref = f32[1024,256]{1,0:T(8,128)} async-done(((f32[32,256]{1,0:T(8,128)}), f32[1024,256]{1,0:T(8,128)}) %all-gather.3.cloned.1.call-update) | async-done | bytes 1048592 | tf_op jit(solution)/shard_map/all_gather | solution.py:356
  65.6 2.1 %slice.37 = f32[32,32,1]{2,1,0:T(8,128)} slice(f32[32,32,256]{2,1,0:T(8,128)} %bitcast.65), slice={[0:32], [0:32], [192:193]} | slice | bytes 8192 | tf_op jit(solution)/shard_map/slice | solution.py:386
  67.8 1.3 copy.45
  69.8 1.4 inverse_density.1.inverse_ref
  71.2 0.8 select_reduce_fusion
  72.1 7.2 %grid_tiles.3.sib_ref = bf16[16,384,616]{2,1,0:T(8,128)(2,1)S(1)} custom-call(bf16[32,616,128]{2,1,0:T(8,128)(2,1)} %collective-permute-done.swath_ref, bf16[32,4,128]{2,1,0:T(4,128)(2,1)S(1)} %copy-done.12, f32[4,256,128]{2,1,0:T(8,128)S(1)} %copy-done.3), custom_call_target="tpu_custom_call" | custom-call | flops 2415919104 | bytes 5046272 | tf_op jit(solution)/shard_map/grid_tiles/pallas_call | solution.py:140
  79.4 11.9 %embed_tiles.1 = bf16[1536,256]{1,0:T(8,128)(2,1)} custom-call(bf16[16,384,616]{2,1,0:T(8,128)(2,1)S(1)} %bitcast.62, bf16[16,384,616]{2,1,0:T(8,128)(2,1)S(1)} %grid_tiles.3.sib_ref, bf16[4,16,16,616]{3,2,1,0:T(8,128)(2,1)S(1)} %pad_maximum_fusion.w0, bf16[4,16,16,616]{3,2,1,0:T(8,128)(2,1)S(1)} %copy-done.6, ...), custom_call_target="tpu_custom_call" | custom-call | flops 9663676416 | bytes 1000000 | tf_op jit(solution)/shard_map/embed_tiles/pallas_call | solution.py:188
  91.3 5.7 %all-to-all-start = ((bf16[32,48,256]{2,1,0:T(8,128)(2,1)}), bf16[32,48,256]{2,1,0:T(8,128)(2,1)S(1)}, u32[]{:S(2)}, u32[]{:S(2)}) async-start(bf16[32,48,256]{2,1,0:T(8,128)(2,1)} %bitcast.17), calls=%async_computation | async-start | bytes 1572864 | tf_op jit(solution)/shard_map/all_to_all | solution.py:385
  97.6 12.8 %all-to-all-done = bf16[32,48,256]{2,1,0:T(8,128)(2,1)S(1)} async-done(((bf16[32,48,256]{2,1,0:T(8,128)(2,1)}), bf16[32,48,256]{2,1,0:T(8,128)(2,1)S(1)}, u32[]{:S(2)}, u32[]{:S(2)}) %all-to-all-start) | async-done | bytes 786464 | tf_op jit(solution)/shard_map/all_to_all | solution.py:385
  110.4 2.9 %attend_source.1 = bf16[128,640]{1,0:T(8,128)(2,1)S(1)} custom-call(bf16[16,2,48,256]{3,2,1,0:T(8,128)(2,1)S(1)} %bitcast.67, s32[1,768]{1,0:T(1,128)S(1)} %select_n.96.row_ref, f32[1,512]{1,0:T(1,128)S(1)} %broadcast_in_dim_reshape.6.bias_ref, f32[1,512]{1,0:T(1,128)S(1)} %copy-done.14, bf16[512,1024]{1,0:T(8,128)(2,1)S(1)} %bitcast.66, f32[4,512]{1,0:T(4,128)S(1)} %copy-done.17), custom_call_target="tpu_custom_call" | custom-call | flops 1572864000 | bytes 3000000 | tf_op jit(solution)/shard_map/attend_source/pallas_call | solution.py:263
  113.3 17.1 %all_to_all.10.parts_ref = bf16[8,16,640]{2,1,0:T(8,128)(2,1)} all-to-all(bf16[8,16,640]{2,1,0:T(8,128)(2,1)S(1)} %bitcast.68), channel_id=1, replica_groups=mesh['lat'=32,'src'=8] {'src'}, dimensions={0} | all-to-all | bytes 327680 | tf_op jit(solution)/shard_map/all_to_all | solution.py:407
  130.4 2.1 %combine_sources.1 = f32[4,4,512]{2,1,0:T(4,128)} custom-call(bf16[8,16,640]{2,1,0:T(8,128)(2,1)} %all_to_all.10.parts_ref, bf16[512,512]{1,0:T(8,128)(2,1)} %weight_ref.1), custom_call_target="tpu_custom_call" | custom-call | flops 33554432 | bytes 800000 | tf_op jit(solution)/shard_map/combine_sources/pallas_call | solution.py:292
  (116 shorter events, 8.3 us)
Async XLA Ops:
  6.5 8.7 %copy-start.3 = (f32[4,256,128]{2,1,0:T(8,128)S(1)}, f32[4,256,128]{2,1,0:T(8,128)}, u32[]{:S(2)}) copy-start(f32[4,256,128]{2,1,0:T(8,128)} %constant.123.clone.center_ref) | copy-start | bytes 1572868
  6.5 59.1 %all-gather.3.cloned.1.call-start = ((), (), s32[]{:S(2)}) async-start(), calls=%async_computation.2 | async-start | bytes 1081344 | tf_op jit(solution)/shard_map/all_gather | solution.py:356
  6.5 65.5 %collective-permute-start = (bf16[32,616,128]{2,1,0:T(8,128)(2,1)}, bf16[32,616,128]{2,1,0:T(8,128)(2,1)}, u32[]{:S(2)}, u32[]{:S(2)}) collective-permute-start(bf16[32,616,128]{2,1,0:T(8,128)(2,1)} %bitcast.63), channel_id=1, source_target_pairs={{0,8},{8,0},{16,24},{24,16},{32,40},{40,32},{48,56},{56,48},{64,72... | collective-permute-start | bytes 15138824 | tf_op jit(solution)/shard_map/ppermute | solution.py:350
  6.5 20.8 %collective-permute-start.2 = (bf16[16,16,616]{2,1,0:T(8,128)(2,1)}, bf16[16,16,616]{2,1,0:T(8,128)(2,1)S(1)}, u32[]{:S(2)}, u32[]{:S(2)}) collective-permute-start(bf16[16,16,616]{2,1,0:T(8,128)(2,1)} %bitcast.72), channel_id=1, source_target_pairs={{0,16},{8,72},{16,32},{24,88},{32,48},{40,104},{48,0},{56,120},{64... | collective-permute-start | bytes 946184 | tf_op jit(solution)/shard_map/ppermute | solution.py:316
  8.0 20.9 %collective-permute-start.3 = (bf16[16,16,616]{2,1,0:T(8,128)(2,1)}, bf16[16,16,616]{2,1,0:T(8,128)(2,1)S(1)}, u32[]{:S(2)}, u32[]{:S(2)}) collective-permute-start(bf16[16,16,616]{2,1,0:T(8,128)(2,1)} %bitcast.73), channel_id=1, source_target_pairs={{0,48},{8,200},{16,0},{24,216},{32,16},{40,232},{48,32},{56,248},{... | collective-permute-start | bytes 946184 | tf_op jit(solution)/shard_map/ppermute | solution.py:316
  11.2 32.8 %collective-permute-start.1 = (bf16[32,4,128]{2,1,0:T(4,128)(2,1)S(1)}, bf16[32,4,128]{2,1,0:T(4,128)(2,1)S(1)}, u32[]{:S(2)}, u32[]{:S(2)}) collective-permute-start(bf16[32,4,128]{2,1,0:T(4,128)(2,1)S(1)} %pad_maximum_fusion.1.pos_ref), channel_id=1, source_target_pairs={{0,8},{8,0},{16,24},{24,16},{32,40},{40,32},{48,56},{56,48},{64,72... | collective-permute-start | bytes 98312 | tf_op jit(solution)/shard_map/ppermute | solution.py:354
  18.4 8.6 %copy-start.25 = (s32[4]{0:T(128)S(1)}, s32[4]{0:T(128)}, u32[]{:S(2)}) copy-start(s32[4]{0:T(128)} %constant.129.clone) | copy-start | bytes 52
  18.4 11.9 %copy-start.22 = (s32[16,16]{1,0:T(8,128)S(1)}, s32[16,16]{1,0:T(8,128)}, u32[]{:S(2)}) copy-start(s32[16,16]{1,0:T(8,128)} %constant.137) | copy-start | bytes 3076
  27.1 7.5 %copy-start.18 = (bf16[1,4,4,616,16]{3,4,2,1,0:T(8,128)(2,1)S(1)}, bf16[1,4,4,616,16]{3,4,2,1,0:T(8,128)(2,1)}, u32[]{:S(2)}) copy-start(bf16[1,4,4,616,16]{3,4,2,1,0:T(8,128)(2,1)} %param.24) | copy-start | bytes 946180
  27.3 6.2 %collective-permute-start.4 = (bf16[8,16,616]{2,1,0:T(8,128)(2,1)S(1)}, bf16[8,16,616]{2,1,0:T(8,128)(2,1)S(1)}, u32[]{:S(2)}, u32[]{:S(2)}) collective-permute-start(bf16[8,16,616]{2,1,0:T(8,128)(2,1)S(1)} %slice.32), channel_id=1, source_target_pairs={{0,16},{8,72},{16,32},{24,88},{32,48},{40,104},{48,0},{56,120},{64... | collective-permute-start | bytes 473096 | tf_op jit(solution)/shard_map/ppermute | solution.py:316
  28.9 5.5 %collective-permute-start.5 = (bf16[8,16,616]{2,1,0:T(8,128)(2,1)S(1)}, bf16[8,16,616]{2,1,0:T(8,128)(2,1)S(1)}, u32[]{:S(2)}, u32[]{:S(2)}) collective-permute-start(bf16[8,16,616]{2,1,0:T(8,128)(2,1)S(1)} %slice.33), channel_id=1, source_target_pairs={{0,48},{8,200},{16,0},{24,216},{32,16},{40,232},{48,32},{56,248},{... | collective-permute-start | bytes 473096 | tf_op jit(solution)/shard_map/ppermute | solution.py:316
  34.8 7.5 %copy-start.24 = (f32[1,512]{1,0:T(1,128)S(1)}, f32[1,512]{1,0:T(1,128)}, u32[]{:S(2)}) copy-start(f32[1,512]{1,0:T(1,128)} %param.25) | copy-start | bytes 6148
  34.8 8.4 %copy-start.23 = (f32[512]{0:T(512)S(1)}, f32[512]{0:T(512)}, u32[]{:S(2)}) copy-start(f32[512]{0:T(512)} %param.26) | copy-start | bytes 6148
  34.8 9.3 %copy-start.26 = (s32[1,32,1]{1,2,0:T(1,128)S(1)}, s32[1,32,1]{1,2,0:T(1,128)}, u32[]{:S(2)}) copy-start(s32[1,32,1]{1,2,0:T(1,128)} %param.21) | copy-start | bytes 388
  34.9 9.3 %copy-start.19 = (s32[32,32]{1,0:T(8,128)S(1)}, s32[32,32]{1,0:T(8,128)}, u32[]{:S(2)}) copy-start(s32[32,32]{1,0:T(8,128)} %constant.127.clone) | copy-start | bytes 12292
  34.9 9.4 %copy-start.28 = (s32[1,32]{1,0:T(1,128)S(1)}, s32[1,32]{1,0:T(1,128)}, u32[]{:S(2)}) copy-start(s32[1,32]{1,0:T(1,128)} %param.22) | copy-start | bytes 388
  34.9 10.3 %copy-start.21 = (s32[64,12]{1,0:T(8,128)S(1)}, s32[64,12]{1,0:T(8,128)}, u32[]{:S(2)}) copy-start(s32[64,12]{1,0:T(8,128)} %constant.138) | copy-start | bytes 9220
  34.9 19.0 %collective-permute-start.6 = (bf16[4,16,16,616]{3,2,1,0:T(8,128)(2,1)S(1)}, bf16[4,16,16,616]{3,2,1,0:T(8,128)(2,1)S(1)}, u32[]{:S(2)}, u32[]{:S(2)}) collective-permute-start(bf16[4,16,16,616]{3,2,1,0:T(8,128)(2,1)S(1)} %pad_maximum_fusion.w0), channel_id=1, source_target_pairs={{0,64},{8,24},{16,80},{24,40},{32,96},{40,56},{48,112},{56,8},{64,... | collective-permute-start | bytes 3784712 | tf_op jit(solution)/shard_map/ppermute | solution.py:316
  35.9 19.0 %collective-permute-start.7 = (bf16[4,16,16,616]{3,2,1,0:T(8,128)(2,1)S(1)}, bf16[4,16,16,616]{3,2,1,0:T(8,128)(2,1)}, u32[]{:S(2)}, u32[]{:S(2)}) collective-permute-start(bf16[4,16,16,616]{3,2,1,0:T(8,128)(2,1)S(1)} %pad_maximum_fusion.w0), channel_id=1, source_target_pairs={{0,192},{8,56},{16,208},{24,8},{32,224},{40,24},{48,240},{56,40},{... | collective-permute-start | bytes 3784712 | tf_op jit(solution)/shard_map/ppermute | solution.py:316
  44.0 9.9 %copy-start.11 = (bf16[32,4,128]{2,1,0:T(4,128)(2,1)}, bf16[32,4,128]{2,1,0:T(4,128)(2,1)S(1)}, u32[]{:S(2)}) copy-start(bf16[32,4,128]{2,1,0:T(4,128)(2,1)S(1)} %collective-permute-done.1.pos_ref) | copy-start | bytes 98308
  54.9 14.2 %copy-start.7 = (bf16[192,768]{1,0:T(8,128)(2,1)S(1)}, bf16[192,768]{1,0:T(8,128)(2,1)}, u32[]{:S(2)}) copy-start(bf16[192,768]{1,0:T(8,128)(2,1)} %constant.125.clone.own_cell_ref) | copy-start | bytes 884740
  54.9 14.2 %copy-start.10 = (bf16[64,768]{1,0:T(8,128)(2,1)S(1)}, bf16[64,768]{1,0:T(8,128)(2,1)}, u32[]{:S(2)}) copy-start(bf16[64,768]{1,0:T(8,128)(2,1)} %constant.124.clone.row_tile_ref) | copy-start | bytes 294916
  54.9 14.2 %copy-start.13 = (bf16[16,192]{1,0:T(8,128)(2,1)S(1)}, bf16[16,192]{1,0:T(8,128)(2,1)}, u32[]{:S(2)}) copy-start(bf16[16,192]{1,0:T(8,128)(2,1)} %constant.126.clone.tap_ref) | copy-start | bytes 18436
  54.9 24.4 %collective-permute-start.8 = (bf16[2,16,16,616]{3,2,1,0:T(8,128)(2,1)}, bf16[2,16,16,616]{3,2,1,0:T(8,128)(2,1)}, u32[]{:S(2)}, u32[]{:S(2)}) collective-permute-start(bf16[2,16,16,616]{3,2,1,0:T(8,128)(2,1)} %slice.34), channel_id=1, source_target_pairs={{0,64},{8,24},{16,80},{24,40},{32,96},{40,56},{48,112},{56,8},{64,... | collective-permute-start | bytes 1892360 | tf_op jit(solution)/shard_map/ppermute | solution.py:316
  57.0 22.3 %collective-permute-start.9 = (bf16[2,16,16,616]{3,2,1,0:T(8,128)(2,1)}, bf16[2,16,16,616]{3,2,1,0:T(8,128)(2,1)}, u32[]{:S(2)}, u32[]{:S(2)}) collective-permute-start(bf16[2,16,16,616]{3,2,1,0:T(8,128)(2,1)} %slice.35), channel_id=1, source_target_pairs={{0,192},{8,56},{16,208},{24,8},{32,224},{40,24},{48,240},{56,40},{... | collective-permute-start | bytes 1892360 | tf_op jit(solution)/shard_map/ppermute | solution.py:316
  69.8 9.5 %slice-start = ((s8[7864320]{0:T(1024)(128)(4,1)}), s8[4194304]{0:T(1024)(128)(4,1)S(1)}, s32[]{:S(2)}) async-start(s8[7864320]{0:T(1024)(128)(4,1)} %bitcast.61), calls=%async_computation.3 | async-start | bytes 8388608
  72.0 7.3 %slice-start.1 = ((s8[7864320]{0:T(1024)(128)(4,1)}), s8[3670016]{0:T(1024)(128)(4,1)S(1)}, s32[]{:S(2)}) async-start(s8[7864320]{0:T(1024)(128)(4,1)} %bitcast.61), calls=%async_computation.4 | async-start | bytes 7340032
  72.0 7.3 %copy-start.6 = (bf16[4,16,16,616]{3,2,1,0:T(8,128)(2,1)S(1)}, bf16[4,16,16,616]{3,2,1,0:T(8,128)(2,1)}, u32[]{:S(2)}) copy-start(bf16[4,16,16,616]{3,2,1,0:T(8,128)(2,1)} %copy-done.5) | copy-start | bytes 3784708
  91.3 19.1 %copy-start.4 = (bf16[16,2,16,1024]{3,2,0,1:T(8,128)(2,1)S(1)}, bf16[16,2,16,1024]{3,2,0,1:T(8,128)(2,1)}, u32[]{:S(2)}) copy-start(bf16[16,2,16,1024]{3,2,0,1:T(8,128)(2,1)} %copy.44) | copy-start | bytes 3145732
  91.3 19.1 %copy-start.14 = (f32[1,512]{1,0:T(1,128)S(1)}, f32[1,512]{1,0:T(1,128)}, u32[]{:S(2)}) copy-start(f32[1,512]{1,0:T(1,128)} %broadcast_in_dim_reshape.7.gain_ref) | copy-start | bytes 6148
  91.3 19.1 %copy-start.17 = (f32[4,512]{1,0:T(4,128)S(1)}, f32[4,512]{1,0:T(4,128)}, u32[]{:S(2)}) copy-start(f32[4,512]{1,0:T(4,128)} %latent_ref.1) | copy-start | bytes 24580
  91.3 19.0 %all-to-all-start = ((bf16[32,48,256]{2,1,0:T(8,128)(2,1)}), bf16[32,48,256]{2,1,0:T(8,128)(2,1)S(1)}, u32[]{:S(2)}, u32[]{:S(2)}) async-start(bf16[32,48,256]{2,1,0:T(8,128)(2,1)} %bitcast.17), calls=%async_computation | async-start | bytes 1572864 | tf_op jit(solution)/shard_map/all_to_all | solution.py:385
  (11 other events, 35.7 us)
Sparse Core Ops, SparseCore 0:
  15.3 50.2 all-gather.2

commit v2 on v1

--- a/solution.py
+++ b/solution.py
@@ -49,42 +49,43 @@
     return jnp.exp((down * down + across * across) * (-1.0 / 1.125))
 
 
-def mass_kernel(pos_ref, center_ref, out_ref):
+def record_kernel(band_ref, patch_ref, pos_ref, center_ref, out_ref):
     ones = jnp.ones((8, FP), BF)
-    place = lax.broadcasted_iota(jnp.int32, (8, CELLS), 0)
+    place = lax.broadcasted_iota(jnp.int32, (8, RECORD), 0)
+    lane = lax.broadcasted_iota(jnp.int32, (8, RECORD - CELLS), 1)
 
     def group(g, carry):
         base = pl.multiple_of(g * 8, 8)
-        total = jnp.zeros((8, CELLS), F32)
+        total = jnp.zeros((8, RECORD), F32)
         for j in range(8):
             table = weights_at(pos_ref[base + j].astype(F32), center_ref, 0).astype(BF)
             row = lax.dot_general(ones, table, NT, preferred_element_type=F32)
-            total = jnp.where(place == j, row, total)
-        target = jnp.broadcast_to(pos_ref[pl.ds(base, 8), 2].astype(F32) * PATCHES + pos_ref[pl.ds(base, 8), 3].astype(F32), (8, FP))
-        out_ref[pl.ds(base, 8), :] = jnp.concatenate([total, target[:, : RECORD - CELLS]], 1)
-        return carry
-
-    lax.fori_loop(0, TILES // 8, group, 0)
-
-
-def tile_records(pos):
-    return pl.pallas_call(
-        mass_kernel,
-        out_shape=jax.ShapeDtypeStruct((TILES, RECORD), F32),
+            about = jnp.where(lane == 0, band_ref[base + j], patch_ref[base + j]).astype(F32)
+            total = jnp.where(place == j, jnp.concatenate([row, about], 1), total)
+        return carry + (total,)
+
+    rows = ()
+    for g in range(TILES // 8):
+        rows = group(g, rows)
+    out_ref[...] = jnp.concatenate(rows, 0).astype(BF)
+
+
+def tile_records(band, patch, pos):
+    vmem, smem = pl.BlockSpec(memory_space=pltpu.VMEM), pl.BlockSpec(memory_space=pltpu.SMEM)
+    return pl.pallas_call(
+        record_kernel,
+        in_specs=[smem, smem, vmem, vmem],
+        out_shape=jax.ShapeDtypeStruct((TILES, RECORD), BF),
         cost_estimate=pl.CostEstimate(flops=2 * TILES * 8 * FP * CELLS, bytes_accessed=300000, transcendentals=TILES * FP * CELLS),
         name="tile_records",
-    )(pos, jnp.asarray(centers(range(TPS))))
-
-
-def inverse_kernel(record_ref, target_ref, row_tile_ref, own_cell_ref, tap_ref, out_ref):
-    same = jnp.where(record_ref[:, CELLS : CELLS + 1] == target_ref[...], 1.0, 0.0).astype(BF)
-    mass = record_ref[:, :CELLS]
-    total = jnp.ones((CELLS, target_ref.shape[1]), F32)
-    for _ in range(3):
-        piece = mass.astype(BF)
-        total += lax.dot_general(piece, same, (((0,), (0,)), ((), ())), preferred_element_type=F32)
-        mass = mass - piece.astype(F32)
-    inverse = 1.0 / total
+    )(band, patch, pos, jnp.asarray(centers(range(TPS))))
+
+
+def inverse_kernel(record_ref, target_ref, slot_ref, token_ref, row_tile_ref, own_cell_ref, tap_ref, out_ref, row_ref):
+    about = record_ref[:, CELLS:].astype(F32)
+    same = jnp.where(about[:, :1] * PATCHES + about[:, 1:2] == target_ref[...], 1.0, 0.0).astype(BF)
+    total = lax.dot_general(record_ref[:, :CELLS], same, (((0,), (0,)), ((), ())), preferred_element_type=F32)
+    inverse = 1.0 / (1.0 + total)
     out = jnp.zeros(out_ref.shape, F32)
     for _ in range(3):
         piece = inverse.astype(BF)
@@ -92,9 +93,11 @@
         out += jnp.dot(tap_ref[...], spread, preferred_element_type=F32)
         inverse = inverse - piece.astype(F32)
     out_ref[...] = out
-
-
-def inverse_density(records, targets):
+    slots = jnp.dot(jnp.broadcast_to(slot_ref[...], (8, slot_ref.shape[1])).astype(BF), row_tile_ref[...], preferred_element_type=F32)
+    row_ref[...] = slots[:1].astype(jnp.int32) * TPS + token_ref[...]
+
+
+def inverse_density(records, targets, slots):
     rows = 2 * TILES * TPS
     row_tile = (np.arange(2 * TILES)[:, None] == np.arange(rows)[None, :] // TPS).astype(np.float32)
     token = np.tile(ROW_TOKEN, TILES)
@@ -102,11 +105,11 @@
     tap = (np.arange(TAPS)[:, None] == np.arange(CELLS)[None, :] // TPS).astype(np.float32)
     return pl.pallas_call(
         inverse_kernel,
-        out_shape=jax.ShapeDtypeStruct((TAPS, rows), F32),
+        out_shape=(jax.ShapeDtypeStruct((TAPS, rows), F32), jax.ShapeDtypeStruct((1, rows), jnp.int32)),
         compiler_params=pltpu.CompilerParams(vmem_limit_bytes=KERNEL_VMEM),
         cost_estimate=pl.CostEstimate(flops=6 * 1024 * CELLS * 128, bytes_accessed=2000000, transcendentals=0),
         name="inverse_density",
-    )(records, targets, *(jnp.asarray(v, BF) for v in (row_tile, own_cell, tap)))
+    )(records, targets, slots, jnp.asarray(token, jnp.int32)[None], *(jnp.asarray(v, BF) for v in (row_tile, own_cell, tap)))
 
 
 def grid_kernel(swath_ref, pos_ref, center_ref, out_ref):
@@ -316,13 +319,30 @@
     return lax.ppermute(array, "lat", shift(offset, second))
 
 
-def gather_weights(shard):
+def gather(shard, record, swap):
     half = TAPS // 2
     up, down = send(shard, 1, False), send(shard, -1, False)
+    others = [send(record, -offset, False) for offset in OFFSETS[1:]]
+    up, down, *others = lax.optimization_barrier((up, down, *others))
+    record = jnp.stack([record] + others, 0)
     far = [send(up[:half], 1, False), send(down[half:], -1, False)]
+    others = [send(record, -offset, True) for offset in OFFSETS[1:]]
+    *far, others = lax.optimization_barrier((*far, others))
+    record = jnp.stack([record] + others, 0)
     line = jnp.stack([shard, up, down, jnp.concatenate(far, 0)], 0)
     above, below = send(line, 1, True), send(line, -1, True)
-    return [line, above, below, send(above[:2], 1, True), send(below[2:], -1, True)]
+    sib_record = lax.ppermute(record, "lat", swap)
+    weights = [line, above, below, send(above[:2], 1, True), send(below[2:], -1, True)]
+    return weights, record, sib_record
+
+
+def offset_at(index):
+    return jnp.where(index == 0, 0, jnp.where(index == 1, -1, index - 1))
+
+
+def index_of(offset):
+    offset = offset % SIDE
+    return jnp.where(offset == 0, 0, jnp.where(offset == SIDE - 1, 1, offset + 1))
 
 
 def body(
@@ -346,48 +366,47 @@
     swap = [(i, i ^ 1) for i in range(2 * CHIPS)]
 
     shard = jnp.transpose(conv_weight[0].reshape(TAPS, channels, cols), (0, 2, 1))
-    weights = gather_weights(shard)
+    record = tile_records(tile_band[0, :, 0], tile_patch[0], fp_pos)
+    weights, record, sib_record = gather(shard, record, swap)
     sib_swath = lax.ppermute(swath, "lat", swap)
-    band, patch = tile_band[0, :, 0], tile_patch[0]
-    about = jnp.broadcast_to(jnp.stack([band, patch], 1).astype(BF)[:, :, None], fp_pos.shape)
-    pos = jnp.concatenate([fp_pos, about], 1)
-    sib_pos = lax.ppermute(pos, "lat", swap)
-
-    records = lax.all_gather(tile_records(pos), "lat")
+    sib_pos = lax.ppermute(fp_pos, "lat", swap)
     center = jnp.asarray(
         np.concatenate([centers(list(range(TPS)) + [-1] * 4), centers([-1] * 4 + list(ROW_TOKEN[TPS:]))], 0)
     )
-    own = gridded(swath, pos, center)
+    swath, sib_swath, _, _ = lax.optimization_barrier((swath, sib_swath, weights[1], weights[2]))
+    own = gridded(swath, fp_pos, center)
     sib = gridded(sib_swath, sib_pos, center)
-    sib_about = sib_pos[:, 2:, 0].astype(jnp.int32)
-    bands_here = jnp.stack([band, sib_about[:, 0]])
-    patches_here = jnp.stack([patch, sib_about[:, 1]])
-    targets = (bands_here * PATCHES + patches_here).reshape(1, -1).astype(F32)
-    inverse = inverse_density(records.reshape(-1, RECORD), targets)
-
+    records = jnp.stack([record, sib_record]).reshape(2, CHIPS, TILES, RECORD)
+    about = records[:, 0, :, CELLS : CELLS + 2].astype(jnp.int32)
+    bands_here = about[:, :, 0]
+    targets = (bands_here * PATCHES + about[:, :, 1]).reshape(1, -1).astype(F32)
     earlier = jnp.asarray(np.tril(np.ones((TILES, TILES), np.int32), -1))
-
-    def rank_of(named):
-        return jnp.sum((named[:, :, None] == named[:, None, :]).astype(jnp.int32) * earlier, axis=2)
-
+    rank = jnp.sum((bands_here[:, :, None] == bands_here[:, None, :]).astype(jnp.int32) * earlier, axis=2)
     origin = jnp.stack([core, 1 - core])[:, None]
-    slot = (bands_here * SLOTS + 2 * origin + rank_of(bands_here)) * TPS
-    token_rows = jnp.asarray(np.tile(ROW_TOKEN, TILES))
-    rows = (jnp.repeat(slot.reshape(-1), TPS) + token_rows)[None, :].astype(jnp.int32)
-    near = jnp.tile(jnp.asarray(OFFSETS), SIDE)
-    farther = jnp.repeat(jnp.asarray(OFFSETS), SIDE)
+    slots = (bands_here * SLOTS + 2 * origin + rank).reshape(1, -1).astype(F32)
+    inverse, rows = inverse_density(records.reshape(-1, RECORD), targets, slots)
+
+    column = jnp.arange(CHIPS * cols, dtype=jnp.int32)[None, :]
+    near, farther = offset_at(column // cols % SIDE), offset_at(column // cols // SIDE)
     at_y = (chip_y + jnp.where(core == 0, farther, near)) % SIDE
     at_x = (chip_x + jnp.where(core == 0, near, farther)) % SIDE
-    columns = (jnp.repeat((at_y * SIDE + at_x) * cols, cols) + jnp.asarray(np.tile(np.arange(cols), CHIPS)))[None, :]
+    columns = (at_y * SIDE + at_x) * cols + column % cols
     outgoing = embed(own, sib, weights, inverse, columns.astype(jnp.int32), rows)
 
     outgoing = outgoing.reshape(2 * CHIPS, SLOTS * TPS, CHIPS * cols)
     incoming = lax.all_to_all(outgoing, "lat", split_axis=0, concat_axis=0, tiled=True)
-    target = records[:, :, CELLS].astype(jnp.int32)
-    bands, patches = target // PATCHES, target % PATCHES
-    rank = rank_of(bands)
-    mine = (bands == place)[:, :, None] & (rank[:, :, None] == jnp.arange(2)[None, None, :])
-    patch_in = jnp.sum(jnp.where(mine, patches[:, :, None] + 1, 0), axis=1).reshape(-1, 1) - 1
+    mine = records[:, :, :, CELLS].astype(F32) == place.astype(F32)
+    patches = jnp.where(mine, records[:, :, :, CELLS + 1].astype(F32) + 1, 0)
+    before = jnp.einsum("cdt,tu->cdu", mine.astype(F32), jnp.asarray(np.triu(np.ones((TILES, TILES), np.float32), 1)))
+    patch_at = jnp.stack([jnp.sum(jnp.where(before == n, patches, 0), axis=2) for n in range(2)], 2)
+    number = jnp.arange(CHIPS)
+    in_y, in_x = index_of(number // SIDE - chip_y), index_of(number % SIDE - chip_x)
+    x_first, y_first = SIDE * in_y + in_x, SIDE * in_x + in_y
+    order = jnp.stack([jnp.where(core == 0, x_first, y_first), jnp.where(core == 0, y_first, x_first)])
+    hot = (order[:, :, None] == number[None, None, :]).astype(F32)
+    patch_by = jnp.einsum("cnd,cdk->nck", hot, patch_at)
+    patch_by = jnp.where(core == 0, patch_by, patch_by[:, ::-1])
+    patch_in = patch_by.astype(jnp.int32).reshape(-1, 1) - 1
     token_in = jnp.where(patch_in < 0, -1, patch_in + PATCHES * jnp.arange(TPS)[None, :]).reshape(1, -1)
 
     def by_core(array):

time: 140 us -> 139 us (level)
  between operations: 13.9 us -> 0.43 us
  starting transfers between devices: 18.5 us -> 28.3 us
  other arithmetic: 5.28 us -> 10.5 us
  local copies, waits for them, and re-layouts: 19.5 us -> 14.3 us
  blocking collectives: 17.1 us -> 18.6 us
    ppermute x8 -> x14, starting transfers between devices: 11.8 us -> 21.3 us  [send(): return lax.ppermute(array, 'lat', shift(offset, second))]
    all_gather x1 -> x0, waiting for transfers between devices: 5.46 us -> none  [body(): records = lax.all_gather(tile_records(pos), 'lat')]
    ppermute x8 -> x14, waiting for transfers between devices: 12.7 us -> 18.1 us  [send(): return lax.ppermute(array, 'lat', shift(offset, second))]
    another operation x6 -> x7, other arithmetic: 1.65 us -> 6.8 us  [the longest x3 3.53 us: body(): records = jnp.stack([record, sib_record]).reshape(2, CHIPS, TILES, RECORD)]
    reshape x2, local copies, waits for them, and re-layouts: 2.41 us -> 0.19 us  [by_core(): split = array.reshape((CHIPS, 2, cols) + shape)]
    unnamed x64 -> x58, local copies, waits for them, and re-layouts: 8.84 us -> 6.83 us
    all_to_all x1, blocking collectives: 17.1 us -> 18.6 us  [body(): lax.all_to_all(parts.reshape(sources, -1, width + FP), 'src', split_axis=...]
    slice x5 -> x4, local copies, waits for them, and re-layouts: 5.16 us -> 4.07 us  [the longest x1 2.05 us: gather(): below[2:]]
  transfers between devices with their start and end apart: 12 -> 18, of which waited for: 5 -> 4; matrix products, arithmetic and copies ran while one was open for 13% -> 16% of each run, Pallas kernels for 12% -> 12%
where the time goes in v2:
time: 139 us; the launch traced here: 138 us
  Pallas kernels  34 us (24%)
  waiting for transfers between devices  30.8 us (22%)
  starting transfers between devices  28.3 us (20%)
  blocking collectives  18.6 us (13%)
  local copies, waits for them, and re-layouts  14.3 us (10%)
  other arithmetic  10.5 us (8%)
    ppermute x14, starting transfers between devices, send(): return lax.ppermute(array, 'lat', shift(offset, second))  21.3 us
    all_to_all x1, blocking collectives, body(): lax.all_to_all(parts.reshape(sources, -1, width + FP), 'src', split_axis=...  18.6 us
    ppermute x14, waiting for transfers between devices, send(): return lax.ppermute(array, 'lat', shift(offset, second))  18.1 us
    all_to_all x1, waiting for transfers between devices, body(): lax.all_to_all(outgoing, 'lat', split_axis=0, concat_axis=0, tiled=True)  12.8 us
    pallas_call x2, Pallas kernels, gridded(): pl.pallas_call(grid_kernel, in_specs=[pl.BlockSpec(memory_space=pl.ANY),...  12.5 us
    pallas_call x1, Pallas kernels, embed(): pl.pallas_call(embed_kernel, in_specs=[vmem] * (len(large) + 3), out_spec...  12.5 us
    unnamed x58, local copies, waits for them, and re-layouts  6.83 us
    all_to_all x1, starting transfers between devices, body(): lax.all_to_all(outgoing, 'lat', split_axis=0, concat_axis=0, tiled=True)  6.48 us
  transfers between devices with their start and end apart: 18, of which 4 were waited for; matrix products, arithmetic and copies ran while one was open for 16% of the time, Pallas kernels for 12%

profile of v2, /device:TPU:2, one launch (start us, length us, event | category | flops | bytes accessed | tf_op | source)
XLA Modules:
  0.0 137.8 jit_solution(12861954649235579293)
XLA Ops:
  0.0 2.7 %tile_records.1 = bf16[32,256]{1,0:T(8,128)(2,1)} custom-call(s32[32]{0:T(128)} %bitcast.100, s32[32]{0:T(128)} %bitcast.101, bf16[32,2,128]{2,1,0:T(2,128)(2,1)} %bitcast.75, f32[2,192,128]{2,1,0:T(8,128)} %constant.175.clone.center_ref), custom_call_target="tpu_custom_call" | custom-call | flops 12582912 | bytes 300000 | tf_op jit(solution)/shard_map/tile_records/pallas_call | solution.py:75
  2.7 1.5 %collective-permute-start.3 = (bf16[32,256]{1,0:T(8,128)(2,1)}, bf16[32,256]{1,0:T(8,128)(2,1)S(1)}, u32[]{:S(2)}, u32[]{:S(2)}) collective-permute-start(bf16[32,256]{1,0:T(8,128)(2,1)} %tile_records.1), channel_id=1, source_target_pairs={{0,16},{8,72},{16,32},{24,88},{32,48},{40,104},{48,0},{56,120},{64... | collective-permute-start | bytes 49160 | tf_op jit(solution)/shard_map/ppermute | solution.py:319
  5.0 1.3 collective-permute-start.1
  6.3 2.0 %collective-permute-start.2 = (bf16[16,16,616]{2,1,0:T(8,128)(2,1)S(1)}, bf16[16,16,616]{2,1,0:T(8,128)(2,1)S(1)}, u32[]{:S(2)}, u32[]{:S(2)}) collective-permute-start(bf16[16,16,616]{2,1,0:T(8,128)(2,1)S(1)} %bitcast.88), channel_id=1, source_target_pairs={{0,48},{8,200},{16,0},{24,216},{32,16},{40,232},{48,32},{56,248},{... | collective-permute-start | bytes 946184 | tf_op jit(solution)/shard_map/ppermute | solution.py:319
  8.9 2.1 %collective-permute-start.5 = (bf16[32,256]{1,0:T(8,128)(2,1)}, bf16[32,256]{1,0:T(8,128)(2,1)S(1)}, u32[]{:S(2)}, u32[]{:S(2)}) collective-permute-start(bf16[32,256]{1,0:T(8,128)(2,1)} %tile_records.1), channel_id=1, source_target_pairs={{0,32},{8,136},{16,48},{24,152},{32,0},{40,168},{48,16},{56,184},{... | collective-permute-start | bytes 49160 | tf_op jit(solution)/shard_map/ppermute | solution.py:319
  11.5 4.0 %collective-permute-done.5 = bf16[32,256]{1,0:T(8,128)(2,1)S(1)} collective-permute-done((bf16[32,256]{1,0:T(8,128)(2,1)}, bf16[32,256]{1,0:T(8,128)(2,1)S(1)}, u32[]{:S(2)}, u32[]{:S(2)}) %collective-permute-start.5) | collective-permute-done | bytes 16416 | tf_op jit(solution)/shard_map/ppermute | solution.py:319
  15.6 1.4 %fusion.22 = (bf16[1,4,32,256]{3,2,1,0:T(8,128)(2,1)S(1)}, bf16[4,32,256]{2,1,0:T(8,128)(2,1)}) fusion(bf16[1,32,256]{2,1,0:T(8,128)(2,1)S(1)} %bitcast.96, bf16[1,32,256]{2,1,0:T(8,128)(2,1)S(1)} %bitcast.95, bf16[1,32,256]{2,1,0:T(8,128)(2,1)S(1)} %bitcast.94, bf16[1,32,256]{2,1,0:T(8,128)(2,1)} %bitcast.93), kind=kLoop, calls=%fused_computation.96 | loop fusion | flops 98304 | bytes 196608 | tf_op jit(solution)/shard_map/stack | solution.py:331
  17.0 1.8 %collective-permute-start.10 = (bf16[4,32,256]{2,1,0:T(8,128)(2,1)}, bf16[4,32,256]{2,1,0:T(8,128)(2,1)}, u32[]{:S(2)}, u32[]{:S(2)}) collective-permute-start(bf16[4,32,256]{2,1,0:T(8,128)(2,1)} %get-tuple-element.42), channel_id=1, source_target_pairs={{0,128},{8,40},{16,144},{24,56},{32,160},{40,8},{48,176},{56,24},{... | collective-permute-start | bytes 196616 | tf_op jit(solution)/shard_map/ppermute | solution.py:319
  19.2 1.8 %collective-permute-start.7 = (bf16[8,16,616]{2,1,0:T(8,128)(2,1)S(1)}, bf16[8,16,616]{2,1,0:T(8,128)(2,1)S(1)}, u32[]{:S(2)}, u32[]{:S(2)}) collective-permute-start(bf16[8,16,616]{2,1,0:T(8,128)(2,1)S(1)} %slice.28), channel_id=1, source_target_pairs={{0,48},{8,200},{16,0},{24,216},{32,16},{40,232},{48,32},{56,248},{... | collective-permute-start | bytes 473096 | tf_op jit(solution)/shard_map/ppermute | solution.py:319
  24.7 2.6 %collective-permute-start.9 = (bf16[4,32,256]{2,1,0:T(8,128)(2,1)}, bf16[4,32,256]{2,1,0:T(8,128)(2,1)S(1)}, u32[]{:S(2)}, u32[]{:S(2)}) collective-permute-start(bf16[4,32,256]{2,1,0:T(8,128)(2,1)} %get-tuple-element.42), channel_id=1, source_target_pairs={{0,192},{8,56},{16,208},{24,8},{32,224},{40,24},{48,240},{56,40},{... | collective-permute-start | bytes 196616 | tf_op jit(solution)/shard_map/ppermute | solution.py:319
  27.8 1.9 %collective-permute-done.8 = bf16[4,32,256]{2,1,0:T(8,128)(2,1)S(1)} collective-permute-done((bf16[4,32,256]{2,1,0:T(8,128)(2,1)}, bf16[4,32,256]{2,1,0:T(8,128)(2,1)S(1)}, u32[]{:S(2)}, u32[]{:S(2)}) %collective-permute-start.8) | collective-permute-done | bytes 65568 | tf_op jit(solution)/shard_map/ppermute | solution.py:319
  29.7 1.6 %fusion.23 = (bf16[1,4,4,32,256]{4,3,2,1,0:T(8,128)(2,1)}, bf16[4,4,32,256]{3,2,1,0:T(8,128)(2,1)S(1)}) fusion(bf16[1,4,32,256]{3,2,1,0:T(8,128)(2,1)} %bitcast.18, bf16[1,4,32,256]{3,2,1,0:T(8,128)(2,1)S(1)} %bitcast.90, bf16[1,4,32,256]{3,2,1,0:T(8,128)(2,1)S(1)} %bitcast.89, bf16[1,4,32,256]{3,2,1,0:T(8,128)(2,1)S(1)} %get-tuple-element.41), kind=kLoop, calls=%fused_computation.97 | loop fusion | flops 393216 | bytes 786432 | tf_op jit(solution)/shard_map/stack | solution.py:379
  31.9 1.2 pad_maximum_fusion.w0
  33.3 3.2 %collective-permute-start.12 = (bf16[4,16,16,616]{3,2,1,0:T(8,128)(2,1)S(1)}, bf16[4,16,16,616]{3,2,1,0:T(8,128)(2,1)}, u32[]{:S(2)}, u32[]{:S(2)}) collective-permute-start(bf16[4,16,16,616]{3,2,1,0:T(8,128)(2,1)S(1)} %pad_maximum_fusion.w0), channel_id=1, source_target_pairs={{0,192},{8,56},{16,208},{24,8},{32,224},{40,24},{48,240},{56,40},{... | collective-permute-start | bytes 3784712 | tf_op jit(solution)/shard_map/ppermute | solution.py:319
  39.0 1.0 pad_maximum_fusion.1
  40.0 12.1 %collective-permute-done.11.w1 = bf16[4,16,16,616]{3,2,1,0:T(8,128)(2,1)} collective-permute-done((bf16[4,16,16,616]{3,2,1,0:T(8,128)(2,1)S(1)}, bf16[4,16,16,616]{3,2,1,0:T(8,128)(2,1)}, u32[]{:S(2)}, u32[]{:S(2)}) %collective-permute-start.11) | collective-permute-done | bytes 1261600 | tf_op jit(solution)/shard_map/ppermute | solution.py:319
  52.2 2.0 %slice.36 = bf16[2,16,16,616]{3,2,1,0:T(8,128)(2,1)} slice(bf16[4,16,16,616]{3,2,1,0:T(8,128)(2,1)} %collective-permute-done.11.w1), slice={[0:2], [0:16], [0:16], [0:616]} | slice | bytes 1261568 | tf_op jit(solution)/shard_map/slice | solution.py:335
  54.2 2.1 %slice.37 = bf16[2,16,16,616]{3,2,1,0:T(8,128)(2,1)} slice(bf16[4,16,16,616]{3,2,1,0:T(8,128)(2,1)} %collective-permute-done.12.w2), slice={[2:4], [0:16], [0:16], [0:616]} | slice | bytes 1261568 | tf_op jit(solution)/shard_map/slice | solution.py:335
  56.2 3.2 %collective-permute-start.15 = (bf16[2,16,16,616]{3,2,1,0:T(8,128)(2,1)}, bf16[2,16,16,616]{3,2,1,0:T(8,128)(2,1)}, u32[]{:S(2)}, u32[]{:S(2)}) collective-permute-start(bf16[2,16,16,616]{3,2,1,0:T(8,128)(2,1)} %slice.37), channel_id=1, source_target_pairs={{0,192},{8,56},{16,208},{24,8},{32,224},{40,24},{48,240},{56,40},{... | collective-permute-start | bytes 1892360 | tf_op jit(solution)/shard_map/ppermute | solution.py:319
  59.9 1.8 %copy.65 = bf16[2,16,32,1]{2,1,0,3:T(8,128)(2,1)} copy(bf16[2,16,32,1]{3,2,1,0:T(8,128)(2,1)} %get-tuple-element.37) | data formatting | bytes 4096
  61.8 1.3 convert_element_type.38.target_ref
  63.0 1.0 copy-done.2
  64.6 1.2 inverse_density.1
  66.8 2.4 %copy-done = bf16[1,32,616,128]{3,2,1,0:T(8,128)(2,1)S(1)} copy-done((bf16[1,32,616,128]{3,2,1,0:T(8,128)(2,1)S(1)}, bf16[1,32,616,128]{3,2,1,0:T(8,128)(2,1)}, u32[]{:S(2)}) %copy-start) | copy-done | bytes 5046296
  69.2 5.5 %grid_tiles.2.own_ref = bf16[16,384,616]{2,1,0:T(8,128)(2,1)S(1)} custom-call(bf16[32,616,128]{2,1,0:T(8,128)(2,1)S(1)} %bitcast.70, bf16[32,2,128]{2,1,0:T(2,128)(2,1)S(1)} %bitcast.77, f32[4,256,128]{2,1,0:T(8,128)S(1)} %copy-done.1), custom_call_target="tpu_custom_call" | custom-call | flops 2415919104 | bytes 5046272 | tf_op jit(solution)/shard_map/grid_tiles/pallas_call | solution.py:143
  74.7 7.0 %grid_tiles.3.sib_ref = bf16[16,384,616]{2,1,0:T(8,128)(2,1)S(1)} custom-call(bf16[32,616,128]{2,1,0:T(8,128)(2,1)} %collective-permute-done.swath_ref, bf16[32,2,128]{2,1,0:T(2,128)(2,1)S(1)} %collective-permute-done.13.pos_ref, f32[4,256,128]{2,1,0:T(8,128)S(1)} %copy-done.1), custom_call_target="tpu_custom_call" | custom-call | flops 2415919104 | bytes 5046272 | tf_op jit(solution)/shard_map/grid_tiles/pallas_call | solution.py:143
  81.8 12.5 %embed_tiles.1 = bf16[1536,256]{1,0:T(8,128)(2,1)} custom-call(bf16[16,384,616]{2,1,0:T(8,128)(2,1)S(1)} %grid_tiles.2.own_ref, bf16[16,384,616]{2,1,0:T(8,128)(2,1)S(1)} %grid_tiles.3.sib_ref, bf16[4,16,16,616]{3,2,1,0:T(8,128)(2,1)S(1)} %pad_maximum_fusion.w0, bf16[4,16,16,616]{3,2,1,0:T(8,128)(2,1)} %collective-permute-done.11.w1, ...), custom_call_target="tpu_custom_call" | custom-call | flops 9663676416 | bytes 1000000 | tf_op jit(solution)/shard_map/embed_tiles/pallas_call | solution.py:191
  94.3 6.5 %all-to-all-start = ((bf16[32,48,256]{2,1,0:T(8,128)(2,1)}), bf16[32,48,256]{2,1,0:T(8,128)(2,1)S(1)}, u32[]{:S(2)}, u32[]{:S(2)}) async-start(bf16[32,48,256]{2,1,0:T(8,128)(2,1)} %bitcast.29), calls=%async_computation | async-start | bytes 1572864 | tf_op jit(solution)/shard_map/all_to_all | solution.py:397
  101.4 12.8 %all-to-all-done = bf16[32,48,256]{2,1,0:T(8,128)(2,1)S(1)} async-done(((bf16[32,48,256]{2,1,0:T(8,128)(2,1)}), bf16[32,48,256]{2,1,0:T(8,128)(2,1)S(1)}, u32[]{:S(2)}, u32[]{:S(2)}) %all-to-all-start) | async-done | bytes 786464 | tf_op jit(solution)/shard_map/all_to_all | solution.py:397
  114.2 2.9 %attend_source.1 = bf16[128,640]{1,0:T(8,128)(2,1)S(1)} custom-call(bf16[16,2,48,256]{3,2,1,0:T(8,128)(2,1)S(1)} %bitcast.73, s32[1,768]{1,0:T(1,128)S(1)} %select_n.396.row_ref, f32[1,512]{1,0:T(1,128)S(1)} %copy-done.7, f32[1,512]{1,0:T(1,128)S(1)} %copy-done.8, bf16[512,1024]{1,0:T(8,128)(2,1)S(1)} %bitcast.72, f32[4,512]{1,0:T(4,128)S(1)} %copy-done.11), custom_call_target="tpu_custom_call" | custom-call | flops 1572864000 | bytes 3000000 | tf_op jit(solution)/shard_map/attend_source/pallas_call | solution.py:266
  117.1 18.6 %all_to_all.10.parts_ref = bf16[8,16,640]{2,1,0:T(8,128)(2,1)} all-to-all(bf16[8,16,640]{2,1,0:T(8,128)(2,1)S(1)} %bitcast.74), channel_id=1, replica_groups=mesh['lat'=32,'src'=8] {'src'}, dimensions={0} | all-to-all | bytes 327680 | tf_op jit(solution)/shard_map/all_to_all | solution.py:426
  135.7 2.1 %combine_sources.1 = f32[4,4,512]{2,1,0:T(4,128)} custom-call(bf16[8,16,640]{2,1,0:T(8,128)(2,1)} %all_to_all.10.parts_ref, bf16[512,512]{1,0:T(8,128)(2,1)} %weight_ref.1), custom_call_target="tpu_custom_call" | custom-call | flops 33554432 | bytes 800000 | tf_op jit(solution)/shard_map/combine_sources/pallas_call | solution.py:295
  (113 shorter events, 12.4 us)
Async XLA Ops:
  0.0 21.2 %copy-start.12 = (bf16[512,1024]{1,0:T(8,128)(2,1)S(1)}, bf16[512,1024]{1,0:T(8,128)(2,1)}, u32[]{:S(2)}) copy-start(bf16[512,1024]{1,0:T(8,128)(2,1)} %param.26) | copy-start | bytes 3145732
  0.0 66.7 %collective-permute-start = (bf16[32,616,128]{2,1,0:T(8,128)(2,1)}, bf16[32,616,128]{2,1,0:T(8,128)(2,1)}, u32[]{:S(2)}, u32[]{:S(2)}) collective-permute-start(bf16[32,616,128]{2,1,0:T(8,128)(2,1)} %bitcast.69), channel_id=1, source_target_pairs={{0,8},{8,0},{16,24},{24,16},{32,40},{40,32},{48,56},{56,48},{64,72... | collective-permute-start | bytes 15138824 | tf_op jit(solution)/shard_map/ppermute | solution.py:371
  2.7 6.1 %collective-permute-start.3 = (bf16[32,256]{1,0:T(8,128)(2,1)}, bf16[32,256]{1,0:T(8,128)(2,1)S(1)}, u32[]{:S(2)}, u32[]{:S(2)}) collective-permute-start(bf16[32,256]{1,0:T(8,128)(2,1)} %tile_records.1), channel_id=1, source_target_pairs={{0,16},{8,72},{16,32},{24,88},{32,48},{40,104},{48,0},{56,120},{64... | collective-permute-start | bytes 49160 | tf_op jit(solution)/shard_map/ppermute | solution.py:319
  4.2 7.3 %collective-permute-start.4 = (bf16[32,256]{1,0:T(8,128)(2,1)}, bf16[32,256]{1,0:T(8,128)(2,1)S(1)}, u32[]{:S(2)}, u32[]{:S(2)}) collective-permute-start(bf16[32,256]{1,0:T(8,128)(2,1)} %tile_records.1), channel_id=1, source_target_pairs={{0,48},{8,200},{16,0},{24,216},{32,16},{40,232},{48,32},{56,248},{... | collective-permute-start | bytes 49160 | tf_op jit(solution)/shard_map/ppermute | solution.py:319
  5.0 10.5 %collective-permute-start.1 = (bf16[16,16,616]{2,1,0:T(8,128)(2,1)S(1)}, bf16[16,16,616]{2,1,0:T(8,128)(2,1)S(1)}, u32[]{:S(2)}, u32[]{:S(2)}) collective-permute-start(bf16[16,16,616]{2,1,0:T(8,128)(2,1)S(1)} %bitcast.87), channel_id=1, source_target_pairs={{0,16},{8,72},{16,32},{24,88},{32,48},{40,104},{48,0},{56,120},{64... | collective-permute-start | bytes 946184 | tf_op jit(solution)/shard_map/ppermute | solution.py:319
  6.3 9.3 %collective-permute-start.2 = (bf16[16,16,616]{2,1,0:T(8,128)(2,1)S(1)}, bf16[16,16,616]{2,1,0:T(8,128)(2,1)S(1)}, u32[]{:S(2)}, u32[]{:S(2)}) collective-permute-start(bf16[16,16,616]{2,1,0:T(8,128)(2,1)S(1)} %bitcast.88), channel_id=1, source_target_pairs={{0,48},{8,200},{16,0},{24,216},{32,16},{40,232},{48,32},{56,248},{... | collective-permute-start | bytes 946184 | tf_op jit(solution)/shard_map/ppermute | solution.py:319
  8.9 6.7 %collective-permute-start.5 = (bf16[32,256]{1,0:T(8,128)(2,1)}, bf16[32,256]{1,0:T(8,128)(2,1)S(1)}, u32[]{:S(2)}, u32[]{:S(2)}) collective-permute-start(bf16[32,256]{1,0:T(8,128)(2,1)} %tile_records.1), channel_id=1, source_target_pairs={{0,32},{8,136},{16,48},{24,152},{32,0},{40,168},{48,16},{56,184},{... | collective-permute-start | bytes 49160 | tf_op jit(solution)/shard_map/ppermute | solution.py:319
  17.0 7.7 %collective-permute-start.10 = (bf16[4,32,256]{2,1,0:T(8,128)(2,1)}, bf16[4,32,256]{2,1,0:T(8,128)(2,1)}, u32[]{:S(2)}, u32[]{:S(2)}) collective-permute-start(bf16[4,32,256]{2,1,0:T(8,128)(2,1)} %get-tuple-element.42), channel_id=1, source_target_pairs={{0,128},{8,40},{16,144},{24,56},{32,160},{40,8},{48,176},{56,24},{... | collective-permute-start | bytes 196616 | tf_op jit(solution)/shard_map/ppermute | solution.py:319
  18.8 10.9 %copy-start.4 = (bf16[1,32,2,128]{3,2,1,0:T(2,128)(2,1)S(1)}, bf16[1,32,2,128]{3,2,1,0:T(2,128)(2,1)}, u32[]{:S(2)}) copy-start(bf16[1,32,2,128]{3,2,1,0:T(2,128)(2,1)} %param.21) | copy-start | bytes 49156
  18.8 10.9 %collective-permute-start.6 = (bf16[8,16,616]{2,1,0:T(8,128)(2,1)S(1)}, bf16[8,16,616]{2,1,0:T(8,128)(2,1)S(1)}, u32[]{:S(2)}, u32[]{:S(2)}) collective-permute-start(bf16[8,16,616]{2,1,0:T(8,128)(2,1)S(1)} %slice.27), channel_id=1, source_target_pairs={{0,16},{8,72},{16,32},{24,88},{32,48},{40,104},{48,0},{56,120},{64... | collective-permute-start | bytes 473096 | tf_op jit(solution)/shard_map/ppermute | solution.py:319
  19.2 10.5 %collective-permute-start.7 = (bf16[8,16,616]{2,1,0:T(8,128)(2,1)S(1)}, bf16[8,16,616]{2,1,0:T(8,128)(2,1)S(1)}, u32[]{:S(2)}, u32[]{:S(2)}) collective-permute-start(bf16[8,16,616]{2,1,0:T(8,128)(2,1)S(1)} %slice.28), channel_id=1, source_target_pairs={{0,48},{8,200},{16,0},{24,216},{32,16},{40,232},{48,32},{56,248},{... | collective-permute-start | bytes 473096 | tf_op jit(solution)/shard_map/ppermute | solution.py:319
  24.0 7.9 %copy-start.14 = (bf16[16,16,616]{2,1,0:T(8,128)(2,1)S(1)}, bf16[16,16,616]{2,1,0:T(8,128)(2,1)}, u32[]{:S(2)}) copy-start(bf16[16,16,616]{2,1,0:T(8,128)(2,1)} %copy-done.13) | copy-start | bytes 946180
  24.0 7.9 %copy-start.16 = (bf16[16,16,616]{2,1,0:T(8,128)(2,1)S(1)}, bf16[16,16,616]{2,1,0:T(8,128)(2,1)}, u32[]{:S(2)}) copy-start(bf16[16,16,616]{2,1,0:T(8,128)(2,1)} %copy-done.15) | copy-start | bytes 946180
  24.0 5.7 %collective-permute-start.8 = (bf16[4,32,256]{2,1,0:T(8,128)(2,1)}, bf16[4,32,256]{2,1,0:T(8,128)(2,1)S(1)}, u32[]{:S(2)}, u32[]{:S(2)}) collective-permute-start(bf16[4,32,256]{2,1,0:T(8,128)(2,1)} %get-tuple-element.42), channel_id=1, source_target_pairs={{0,64},{8,24},{16,80},{24,40},{32,96},{40,56},{48,112},{56,8},{64,... | collective-permute-start | bytes 196616 | tf_op jit(solution)/shard_map/ppermute | solution.py:319
  24.7 5.0 %collective-permute-start.9 = (bf16[4,32,256]{2,1,0:T(8,128)(2,1)}, bf16[4,32,256]{2,1,0:T(8,128)(2,1)S(1)}, u32[]{:S(2)}, u32[]{:S(2)}) collective-permute-start(bf16[4,32,256]{2,1,0:T(8,128)(2,1)} %get-tuple-element.42), channel_id=1, source_target_pairs={{0,192},{8,56},{16,208},{24,8},{32,224},{40,24},{48,240},{56,40},{... | collective-permute-start | bytes 196616 | tf_op jit(solution)/shard_map/ppermute | solution.py:319
  29.7 45.0 %collective-permute-start.13 = (bf16[32,2,128]{2,1,0:T(2,128)(2,1)S(1)}, bf16[32,2,128]{2,1,0:T(2,128)(2,1)S(1)}, u32[]{:S(2)}, u32[]{:S(2)}) collective-permute-start(bf16[32,2,128]{2,1,0:T(2,128)(2,1)S(1)} %bitcast.76), channel_id=1, source_target_pairs={{0,8},{8,0},{16,24},{24,16},{32,40},{40,32},{48,56},{56,48},{64,72... | collective-permute-start | bytes 49160 | tf_op jit(solution)/shard_map/ppermute | solution.py:372
  31.3 5.1 %collective-permute-start.16 = (bf16[4,4,32,256]{3,2,1,0:T(8,128)(2,1)S(1)}, bf16[4,4,32,256]{3,2,1,0:T(8,128)(2,1)S(1)}, u32[]{:S(2)}, u32[]{:S(2)}) collective-permute-start(bf16[4,4,32,256]{3,2,1,0:T(8,128)(2,1)S(1)} %get-tuple-element.40), channel_id=1, source_target_pairs={{0,8},{8,0},{16,24},{24,16},{32,40},{40,32},{48,56},{56,48},{64,72... | collective-permute-start | bytes 786440 | tf_op jit(solution)/shard_map/ppermute | solution.py:334
  33.2 19.0 %collective-permute-start.11 = (bf16[4,16,16,616]{3,2,1,0:T(8,128)(2,1)S(1)}, bf16[4,16,16,616]{3,2,1,0:T(8,128)(2,1)}, u32[]{:S(2)}, u32[]{:S(2)}) collective-permute-start(bf16[4,16,16,616]{3,2,1,0:T(8,128)(2,1)S(1)} %pad_maximum_fusion.w0), channel_id=1, source_target_pairs={{0,64},{8,24},{16,80},{24,40},{32,96},{40,56},{48,112},{56,8},{64,... | collective-permute-start | bytes 3784712 | tf_op jit(solution)/shard_map/ppermute | solution.py:319
  33.3 20.9 %collective-permute-start.12 = (bf16[4,16,16,616]{3,2,1,0:T(8,128)(2,1)S(1)}, bf16[4,16,16,616]{3,2,1,0:T(8,128)(2,1)}, u32[]{:S(2)}, u32[]{:S(2)}) collective-permute-start(bf16[4,16,16,616]{3,2,1,0:T(8,128)(2,1)S(1)} %pad_maximum_fusion.w0), channel_id=1, source_target_pairs={{0,192},{8,56},{16,208},{24,8},{32,224},{40,24},{48,240},{56,40},{... | collective-permute-start | bytes 3784712 | tf_op jit(solution)/shard_map/ppermute | solution.py:319
  40.0 19.4 %copy-start.21 = (s32[2,32,2]{1,2,0:T(2,128)S(1)}, s32[2,32,2]{1,2,0:T(2,128)}, u32[]{:S(2)}) copy-start(s32[2,32,2]{1,2,0:T(2,128)} %copy-done.20) | copy-start | bytes 1540
  40.0 23.0 %copy-start.3 = (bf16[64,768]{1,0:T(8,128)(2,1)S(1)}, bf16[64,768]{1,0:T(8,128)(2,1)}, u32[]{:S(2)}) copy-start(bf16[64,768]{1,0:T(8,128)(2,1)} %constant.179.clone.row_tile_ref) | copy-start | bytes 294916
  40.0 23.0 %copy-start.5 = (bf16[16,192]{1,0:T(8,128)(2,1)S(1)}, bf16[16,192]{1,0:T(8,128)(2,1)}, u32[]{:S(2)}) copy-start(bf16[16,192]{1,0:T(8,128)(2,1)} %constant.181.clone.tap_ref) | copy-start | bytes 18436
  40.0 23.0 %copy-start.6 = (s32[1,768]{1,0:T(1,128)S(1)}, s32[1,768]{1,0:T(1,128)}, u32[]{:S(2)}) copy-start(s32[1,768]{1,0:T(1,128)} %constant.189.token_ref) | copy-start | bytes 9220
  54.1 12.6 %copy-start.1 = (f32[4,256,128]{2,1,0:T(8,128)S(1)}, f32[4,256,128]{2,1,0:T(8,128)}, u32[]{:S(2)}) copy-start(f32[4,256,128]{2,1,0:T(8,128)} %constant.176.clone.center_ref) | copy-start | bytes 1572868
  54.2 27.6 %collective-permute-start.14 = (bf16[2,16,16,616]{3,2,1,0:T(8,128)(2,1)}, bf16[2,16,16,616]{3,2,1,0:T(8,128)(2,1)}, u32[]{:S(2)}, u32[]{:S(2)}) collective-permute-start(bf16[2,16,16,616]{3,2,1,0:T(8,128)(2,1)} %slice.36), channel_id=1, source_target_pairs={{0,64},{8,24},{16,80},{24,40},{32,96},{40,56},{48,112},{56,8},{64,... | collective-permute-start | bytes 1892360 | tf_op jit(solution)/shard_map/ppermute | solution.py:319
  56.2 25.5 %collective-permute-start.15 = (bf16[2,16,16,616]{3,2,1,0:T(8,128)(2,1)}, bf16[2,16,16,616]{3,2,1,0:T(8,128)(2,1)}, u32[]{:S(2)}, u32[]{:S(2)}) collective-permute-start(bf16[2,16,16,616]{3,2,1,0:T(8,128)(2,1)} %slice.37), channel_id=1, source_target_pairs={{0,192},{8,56},{16,208},{24,8},{32,224},{40,24},{48,240},{56,40},{... | collective-permute-start | bytes 1892360 | tf_op jit(solution)/shard_map/ppermute | solution.py:319
  74.7 7.1 %copy-start.9 = (s32[1,256]{1,0:T(1,128)S(1)}, s32[1,256]{1,0:T(1,128)}, u32[]{:S(2)}) copy-start(s32[1,256]{1,0:T(1,128)} %fusion.8.column_ref) | copy-start | bytes 3076
  94.2 7.0 %copy-start.25 = (s32[12]{0:T(128)S(1)}, s32[12]{0:T(128)}, u32[]{:S(2)}) copy-start(s32[12]{0:T(128)} %iota_multiply_fusion) | copy-start | bytes 148
  94.2 19.9 %copy-start.7 = (f32[1,512]{1,0:T(1,128)S(1)}, f32[1,512]{1,0:T(1,128)}, u32[]{:S(2)}) copy-start(f32[1,512]{1,0:T(1,128)} %broadcast_in_dim_reshape.6.bias_ref) | copy-start | bytes 6148
  94.2 19.9 %copy-start.8 = (f32[1,512]{1,0:T(1,128)S(1)}, f32[1,512]{1,0:T(1,128)}, u32[]{:S(2)}) copy-start(f32[1,512]{1,0:T(1,128)} %broadcast_in_dim_reshape.7.gain_ref) | copy-start | bytes 6148
  94.3 19.9 %copy-start.11 = (f32[4,512]{1,0:T(4,128)S(1)}, f32[4,512]{1,0:T(4,128)}, u32[]{:S(2)}) copy-start(f32[4,512]{1,0:T(4,128)} %latent_ref.1) | copy-start | bytes 24580
  94.3 19.9 %all-to-all-start = ((bf16[32,48,256]{2,1,0:T(8,128)(2,1)}), bf16[32,48,256]{2,1,0:T(8,128)(2,1)S(1)}, u32[]{:S(2)}, u32[]{:S(2)}) async-start(bf16[32,48,256]{2,1,0:T(8,128)(2,1)} %bitcast.29), calls=%async_computation | async-start | bytes 1572864 | tf_op jit(solution)/shard_map/all_to_all | solution.py:397
  (13 other events, 50.9 us)

commit v3 on v2

--- a/solution.py
+++ b/solution.py
@@ -31,6 +31,7 @@
 NT = (((1,), (1,)), ((), ()))
 KERNEL_VMEM = 24 * 2**20
 RECORD = 256
+SMALL = pl.CostEstimate(flops=1000000, bytes_accessed=10000, transcendentals=0)
 
 
 def centers(tokens):
@@ -76,16 +77,26 @@
         record_kernel,
         in_specs=[smem, smem, vmem, vmem],
         out_shape=jax.ShapeDtypeStruct((TILES, RECORD), BF),
-        cost_estimate=pl.CostEstimate(flops=2 * TILES * 8 * FP * CELLS, bytes_accessed=300000, transcendentals=TILES * FP * CELLS),
+        cost_estimate=SMALL,
         name="tile_records",
     )(band, patch, pos, jnp.asarray(centers(range(TPS))))
 
 
-def inverse_kernel(record_ref, target_ref, slot_ref, token_ref, row_tile_ref, own_cell_ref, tap_ref, out_ref, row_ref):
-    about = record_ref[:, CELLS:].astype(F32)
-    same = jnp.where(about[:, :1] * PATCHES + about[:, 1:2] == target_ref[...], 1.0, 0.0).astype(BF)
-    total = lax.dot_general(record_ref[:, :CELLS], same, (((0,), (0,)), ((), ())), preferred_element_type=F32)
-    inverse = 1.0 / (1.0 + total)
+def inverse_kernel(core_ref, own_ref, sib_ref, token_ref, row_tile_ref, own_cell_ref, tap_ref, out_ref, row_ref):
+    here = 2 * TILES
+
+    def as_row(column):
+        return jnp.broadcast_to(column, (column.shape[0], FP)).T[:1]
+
+    about = jnp.concatenate([own_ref[:TILES, CELLS:], sib_ref[:TILES, CELLS:]], 0).astype(F32)
+    band, target = about[:, :1], about[:, :1] * PATCHES + about[:, 1:2]
+    band_row, target_row = as_row(band), as_row(target)
+    total = jnp.ones((CELLS, here), F32)
+    for ref in (own_ref, sib_ref):
+        about = ref[:, CELLS:].astype(F32)
+        same = jnp.where(about[:, :1] * PATCHES + about[:, 1:2] == target_row, 1.0, 0.0).astype(BF)
+        total += lax.dot_general(ref[:, :CELLS], same, (((0,), (0,)), ((), ())), preferred_element_type=F32)
+    inverse = 1.0 / total
     out = jnp.zeros(out_ref.shape, F32)
     for _ in range(3):
         piece = inverse.astype(BF)
@@ -93,23 +104,31 @@
         out += jnp.dot(tap_ref[...], spread, preferred_element_type=F32)
         inverse = inverse - piece.astype(F32)
     out_ref[...] = out
-    slots = jnp.dot(jnp.broadcast_to(slot_ref[...], (8, slot_ref.shape[1])).astype(BF), row_tile_ref[...], preferred_element_type=F32)
+    other = lax.broadcasted_iota(jnp.int32, (here, here), 0)
+    tile = lax.broadcasted_iota(jnp.int32, (here, here), 1)
+    earlier = (other < tile) & ((other < TILES) == (tile < TILES)) & (band == band_row)
+    rank = jnp.sum(jnp.where(earlier, 1.0, 0.0), axis=0, keepdims=True)
+    origin = jnp.where(tile[:1] < TILES, core_ref[0], 1 - core_ref[0]).astype(F32)
+    slots = jnp.broadcast_to(band_row * SLOTS + 2 * origin + rank, (8, here)).astype(BF)
+    slots = jnp.dot(slots, row_tile_ref[...], preferred_element_type=F32)
     row_ref[...] = slots[:1].astype(jnp.int32) * TPS + token_ref[...]
 
 
-def inverse_density(records, targets, slots):
+def inverse_density(core, own, sib):
     rows = 2 * TILES * TPS
     row_tile = (np.arange(2 * TILES)[:, None] == np.arange(rows)[None, :] // TPS).astype(np.float32)
     token = np.tile(ROW_TOKEN, TILES)
     own_cell = (np.arange(CELLS)[:, None] % TPS == token[None, :]).astype(np.float32)
     tap = (np.arange(TAPS)[:, None] == np.arange(CELLS)[None, :] // TPS).astype(np.float32)
+    vmem, smem = pl.BlockSpec(memory_space=pltpu.VMEM), pl.BlockSpec(memory_space=pltpu.SMEM)
     return pl.pallas_call(
         inverse_kernel,
+        in_specs=[smem] + [vmem] * 6,
         out_shape=(jax.ShapeDtypeStruct((TAPS, rows), F32), jax.ShapeDtypeStruct((1, rows), jnp.int32)),
-        compiler_params=pltpu.CompilerParams(vmem_limit_bytes=KERNEL_VMEM),
-        cost_estimate=pl.CostEstimate(flops=6 * 1024 * CELLS * 128, bytes_accessed=2000000, transcendentals=0),
+        compiler_params=pltpu.CompilerParams(vmem_limit_bytes=KERNEL_VMEM // 2),
+        cost_estimate=SMALL,
         name="inverse_density",
-    )(records, targets, slots, jnp.asarray(token, jnp.int32)[None], *(jnp.asarray(v, BF) for v in (row_tile, own_cell, tap)))
+    )(core, own, sib, jnp.asarray(token, jnp.int32)[None], *(jnp.asarray(v, BF) for v in (row_tile, own_cell, tap)))
 
 
 def grid_kernel(swath_ref, pos_ref, center_ref, out_ref):
@@ -140,22 +159,20 @@
 def gridded(swath, pos, center):
     channels = swath.shape[1]
     vmem = pl.BlockSpec(memory_space=pltpu.VMEM)
+    swath = pltpu.with_memory_space_constraint(swath, pltpu.HBM)
     return pl.pallas_call(
         grid_kernel,
         in_specs=[pl.BlockSpec(memory_space=pl.ANY), vmem, vmem],
         out_specs=vmem,
         out_shape=pltpu.VMEM((TAPS, TILES * TPS, channels), BF),
-        compiler_params=pltpu.CompilerParams(vmem_limit_bytes=KERNEL_VMEM),
-        cost_estimate=pl.CostEstimate(
-            flops=2 * (TILES // 2) * TAPS * PAIR * 2 * FP * 768,
-            bytes_accessed=TILES * channels * FP * 2,
-            transcendentals=TILES * FP * 256,
-        ),
+        compiler_params=pltpu.CompilerParams(vmem_limit_bytes=KERNEL_VMEM // 2),
+        cost_estimate=SMALL,
         name="grid_tiles",
     )(swath, pos, center)
 
 
-def embed_kernel(own_ref, sib_ref, w0, w1, w2, w3, w4, inverse_ref, column_ref, row_ref, out_ref, total, spread):
+def embed_kernel(own_ref, sib_ref, *refs):
+    *weight_refs, inverse_ref, column_ref, row_ref, out_ref, total, spread = refs
     channels = own_ref.shape[2]
     slot_rows, half = out_ref.shape[0], own_ref.shape[1]
     part = slot_rows // TAPS
@@ -163,7 +180,7 @@
     total[...] = jnp.zeros_like(total)
 
     def tap(k, carry):
-        weight = jnp.concatenate([w[:, k].reshape(-1, channels) for w in (w0, w1, w2, w3, w4)], 0)
+        weight = jnp.concatenate([w[:, k].reshape(-1, channels) for w in weight_refs], 0)
         scale = jnp.broadcast_to(inverse_ref[pl.ds(k, 1), :], (FP, 2 * half)).T
         scale = jnp.concatenate([scale] * (width // FP), 1)
         for n, ref in enumerate((own_ref, sib_ref)):
@@ -194,7 +211,7 @@
         out_specs=vmem,
         out_shape=jax.ShapeDtypeStruct((slot_rows, width), BF),
         scratch_shapes=[pltpu.VMEM((2 * half, width), F32), pltpu.VMEM((slot_rows, 2 * half), BF)],
-        compiler_params=pltpu.CompilerParams(vmem_limit_bytes=KERNEL_VMEM),
+        compiler_params=pltpu.CompilerParams(vmem_limit_bytes=KERNEL_VMEM // 2),
         cost_estimate=pl.CostEstimate(flops=2 * TAPS * 2 * half * 768 * width * 2, bytes_accessed=1000000, transcendentals=0),
         name="embed_tiles",
     )(*large, inverse, columns, rows)
@@ -319,23 +336,6 @@
     return lax.ppermute(array, "lat", shift(offset, second))
 
 
-def gather(shard, record, swap):
-    half = TAPS // 2
-    up, down = send(shard, 1, False), send(shard, -1, False)
-    others = [send(record, -offset, False) for offset in OFFSETS[1:]]
-    up, down, *others = lax.optimization_barrier((up, down, *others))
-    record = jnp.stack([record] + others, 0)
-    far = [send(up[:half], 1, False), send(down[half:], -1, False)]
-    others = [send(record, -offset, True) for offset in OFFSETS[1:]]
-    *far, others = lax.optimization_barrier((*far, others))
-    record = jnp.stack([record] + others, 0)
-    line = jnp.stack([shard, up, down, jnp.concatenate(far, 0)], 0)
-    above, below = send(line, 1, True), send(line, -1, True)
-    sib_record = lax.ppermute(record, "lat", swap)
-    weights = [line, above, below, send(above[:2], 1, True), send(below[2:], -1, True)]
-    return weights, record, sib_record
-
-
 def offset_at(index):
     return jnp.where(index == 0, 0, jnp.where(index == 1, -1, index - 1))
 
@@ -366,25 +366,35 @@
     swap = [(i, i ^ 1) for i in range(2 * CHIPS)]
 
     shard = jnp.transpose(conv_weight[0].reshape(TAPS, channels, cols), (0, 2, 1))
-    record = tile_records(tile_band[0, :, 0], tile_patch[0], fp_pos)
-    weights, record, sib_record = gather(shard, record, swap)
+    center = jnp.asarray(
+        np.concatenate([centers(list(range(TPS)) + [-1] * 4), centers([-1] * 4 + list(ROW_TOKEN[TPS:]))], 0)
+    )
+    half = TAPS // 2
+    up, down = send(shard, 1, False), send(shard, -1, False)
     sib_swath = lax.ppermute(swath, "lat", swap)
     sib_pos = lax.ppermute(fp_pos, "lat", swap)
-    center = jnp.asarray(
-        np.concatenate([centers(list(range(TPS)) + [-1] * 4), centers([-1] * 4 + list(ROW_TOKEN[TPS:]))], 0)
-    )
-    swath, sib_swath, _, _ = lax.optimization_barrier((swath, sib_swath, weights[1], weights[2]))
+    record = tile_records(tile_band[0, :, 0], tile_patch[0], fp_pos)
+    up, down, record = lax.optimization_barrier((up, down, record))
+    far = [send(up[:half], 1, False), send(down[half:], -1, False)]
+    others = [send(record, -offset, False) for offset in OFFSETS[1:]]
+    *far, record = lax.optimization_barrier((*far, jnp.stack([record] + others, 0)))
+    low = jnp.stack([shard, up], 0)
+    high = jnp.stack([down, jnp.concatenate(far, 0)], 0)
+    above_low, below_high = send(low, 1, True), send(high, -1, True)
+    record = jnp.stack([record] + [send(record, -offset, True) for offset in OFFSETS[1:]], 0)
+    above_low, below_high, low, high, record, swath, sib_swath = lax.optimization_barrier(
+        (above_low, below_high, low, high, record, swath, sib_swath)
+    )
+    corner_low, corner_high = send(above_low, 1, True), send(below_high, -1, True)
+    above_high, below_low = send(high, 1, True), send(low, -1, True)
+    sib_record = lax.ppermute(record, "lat", swap)
     own = gridded(swath, fp_pos, center)
     sib = gridded(sib_swath, sib_pos, center)
-    records = jnp.stack([record, sib_record]).reshape(2, CHIPS, TILES, RECORD)
-    about = records[:, 0, :, CELLS : CELLS + 2].astype(jnp.int32)
-    bands_here = about[:, :, 0]
-    targets = (bands_here * PATCHES + about[:, :, 1]).reshape(1, -1).astype(F32)
-    earlier = jnp.asarray(np.tril(np.ones((TILES, TILES), np.int32), -1))
-    rank = jnp.sum((bands_here[:, :, None] == bands_here[:, None, :]).astype(jnp.int32) * earlier, axis=2)
-    origin = jnp.stack([core, 1 - core])[:, None]
-    slots = (bands_here * SLOTS + 2 * origin + rank).reshape(1, -1).astype(F32)
-    inverse, rows = inverse_density(records.reshape(-1, RECORD), targets, slots)
+    weights = [low, high, above_low, above_high, below_low, below_high, corner_low, corner_high]
+
+    inverse, rows = inverse_density(
+        core[None].astype(jnp.int32), record.reshape(-1, RECORD), sib_record.reshape(-1, RECORD)
+    )
 
     column = jnp.arange(CHIPS * cols, dtype=jnp.int32)[None, :]
     near, farther = offset_at(column // cols % SIDE), offset_at(column // cols // SIDE)
@@ -393,10 +403,15 @@
     columns = (at_y * SIDE + at_x) * cols + column % cols
     outgoing = embed(own, sib, weights, inverse, columns.astype(jnp.int32), rows)
 
+    record, sib_record, conv_bias, norm_gain, kv_weight, outgoing = lax.optimization_barrier(
+        (record, sib_record, conv_bias, norm_gain, kv_weight, outgoing)
+    )
+    about = jnp.stack([record[..., CELLS : CELLS + 2], sib_record[..., CELLS : CELLS + 2]])
+    about = about.reshape(2, CHIPS, TILES, 2).astype(F32)
     outgoing = outgoing.reshape(2 * CHIPS, SLOTS * TPS, CHIPS * cols)
     incoming = lax.all_to_all(outgoing, "lat", split_axis=0, concat_axis=0, tiled=True)
-    mine = records[:, :, :, CELLS].astype(F32) == place.astype(F32)
-    patches = jnp.where(mine, records[:, :, :, CELLS + 1].astype(F32) + 1, 0)
+    mine = about[..., 0] == place.astype(F32)
+    patches = jnp.where(mine, about[..., 1] + 1, 0)
     before = jnp.einsum("cdt,tu->cdu", mine.astype(F32), jnp.asarray(np.triu(np.ones((TILES, TILES), np.float32), 1)))
     patch_at = jnp.stack([jnp.sum(jnp.where(before == n, patches, 0), axis=2) for n in range(2)], 2)
     number = jnp.arange(CHIPS)

time: 139 us -> 117 us (0.84)
  local copies, waits for them, and re-layouts: 14.3 us -> 4.86 us
  other arithmetic: 10.5 us -> 2.91 us
  waiting for transfers between devices: 30.8 us -> 27.2 us
  blocking collectives: 18.6 us -> 17.2 us
    unnamed x58 -> x22, local copies, waits for them, and re-layouts: 6.83 us -> 1.81 us
    another operation x6 -> x5, other arithmetic: 6.22 us -> 1.98 us  [the longest x1 1.07 us: body(): low = jnp.stack([shard, up], 0)]
    slice x4, local copies, waits for them, and re-layouts: 4.07 us -> 0.27 us  [the longest x1 0.14 us: body(): sib_record[..., CELLS:CELLS + 2]]
    all_to_all x1, waiting for transfers between devices: 12.8 us -> 9.66 us  [body(): lax.all_to_all(outgoing, 'lat', split_axis=0, concat_axis=0, tiled=True)]
    ppermute x14 -> x16, waiting for transfers between devices: 18.1 us -> 16.1 us  [send(): return lax.ppermute(array, 'lat', shift(offset, second))]
    pallas_call x2, Pallas kernels: 12.5 us -> 14.1 us  [gridded(): pl.pallas_call(grid_kernel, in_specs=[pl.BlockSpec(memory_space=pl.ANY),...]
    all_to_all x1, blocking collectives: 18.6 us -> 17.2 us  [body(): lax.all_to_all(parts.reshape(sources, -1, width + FP), 'src', split_axis=...]
    ppermute x14 -> x16, starting transfers between devices: 21.3 us -> 22.3 us  [send(): return lax.ppermute(array, 'lat', shift(offset, second))]
  transfers between devices with their start and end apart: 18 -> 20, of which waited for: 4 -> 8; matrix products, arithmetic and copies ran while one was open for 16% -> 5% of each run, Pallas kernels for 12% -> 16%
where the time goes in v3:
time: 117 us; the launch traced here: 116 us
  Pallas kernels  35.3 us (30%)
  starting transfers between devices  27.9 us (24%)
  waiting for transfers between devices  27.2 us (23%)
  blocking collectives  17.2 us (15%)
  local copies, waits for them, and re-layouts  4.86 us (4%)
  other arithmetic  2.91 us (2%)
    ppermute x16, starting transfers between devices, send(): return lax.ppermute(array, 'lat', shift(offset, second))  22.3 us
    all_to_all x1, blocking collectives, body(): lax.all_to_all(parts.reshape(sources, -1, width + FP), 'src', split_axis=...  17.2 us
    ppermute x16, waiting for transfers between devices, send(): return lax.ppermute(array, 'lat', shift(offset, second))  16.1 us
    pallas_call x2, Pallas kernels, gridded(): pl.pallas_call(grid_kernel, in_specs=[pl.BlockSpec(memory_space=pl.ANY),...  14.1 us
    pallas_call x1, Pallas kernels, embed(): pl.pallas_call(embed_kernel, in_specs=[vmem] * (len(large) + 3), out_spec...  12.2 us
    all_to_all x1, waiting for transfers between devices, body(): lax.all_to_all(outgoing, 'lat', split_axis=0, concat_axis=0, tiled=True)  9.66 us
    all_to_all x1, starting transfers between devices, body(): lax.all_to_all(outgoing, 'lat', split_axis=0, concat_axis=0, tiled=True)  5.43 us
    pallas_call x1, Pallas kernels, attend(): pl.pallas_call(attend_kernel, out_shape=jax.ShapeDtypeStruct((PATCHES * L...  2.9 us
  transfers between devices with their start and end apart: 20, of which 8 were waited for; matrix products, arithmetic and copies ran while one was open for 5% of the time, Pallas kernels for 16%

profile of v3, /device:TPU:2, one launch (start us, length us, event | category | flops | bytes accessed | tf_op | source)
XLA Modules:
  0.0 116.0 jit_solution(402118434804013631)
XLA Ops:
  0.0 1.5 %collective-permute-start = (bf16[16,16,616]{2,1,0:T(8,128)(2,1)}, bf16[16,16,616]{2,1,0:T(8,128)(2,1)S(1)}, u32[]{:S(2)}, u32[]{:S(2)}) collective-permute-start(bf16[16,16,616]{2,1,0:T(8,128)(2,1)} %bitcast.78), channel_id=1, source_target_pairs={{0,16},{8,72},{16,32},{24,88},{32,48},{40,104},{48,0},{56,120},{64... | collective-permute-start | bytes 946184 | tf_op jit(solution)/shard_map/ppermute | solution.py:336
  1.5 0.8 collective-permute-start.1
  2.3 2.6 %tile_records.1 = bf16[32,256]{1,0:T(8,128)(2,1)} custom-call(s32[32]{0:T(128)} %bitcast.93, s32[32]{0:T(128)} %bitcast.94, bf16[32,2,128]{2,1,0:T(2,128)(2,1)} %bitcast.68, f32[2,192,128]{2,1,0:T(8,128)} %constant.170.clone.center_ref), custom_call_target="tpu_custom_call" | custom-call | flops 1000000 | bytes 10000 | tf_op jit(solution)/shard_map/tile_records/pallas_call | solution.py:76
  4.9 2.7 %collective-permute-done = bf16[16,16,616]{2,1,0:T(8,128)(2,1)S(1)} collective-permute-done((bf16[16,16,616]{2,1,0:T(8,128)(2,1)}, bf16[16,16,616]{2,1,0:T(8,128)(2,1)S(1)}, u32[]{:S(2)}, u32[]{:S(2)}) %collective-permute-start) | collective-permute-done | bytes 315424 | tf_op jit(solution)/shard_map/ppermute | solution.py:336
  7.5 1.2 %collective-permute-done.1 = bf16[16,16,616]{2,1,0:T(8,128)(2,1)S(1)} collective-permute-done((bf16[16,16,616]{2,1,0:T(8,128)(2,1)}, bf16[16,16,616]{2,1,0:T(8,128)(2,1)S(1)}, u32[]{:S(2)}, u32[]{:S(2)}) %collective-permute-start.1) | collective-permute-done | bytes 315424 | tf_op jit(solution)/shard_map/ppermute | solution.py:336
  8.8 1.4 %collective-permute-start.5 = (bf16[32,256]{1,0:T(8,128)(2,1)}, bf16[32,256]{1,0:T(8,128)(2,1)S(1)}, u32[]{:S(2)}, u32[]{:S(2)}) collective-permute-start(bf16[32,256]{1,0:T(8,128)(2,1)} %tile_records.1), channel_id=1, source_target_pairs={{0,16},{8,72},{16,32},{24,88},{32,48},{40,104},{48,0},{56,120},{64... | collective-permute-start | bytes 49160 | tf_op jit(solution)/shard_map/ppermute | solution.py:336
  10.8 4.1 %collective-permute-start.7 = (bf16[32,256]{1,0:T(8,128)(2,1)}, bf16[32,256]{1,0:T(8,128)(2,1)S(1)}, u32[]{:S(2)}, u32[]{:S(2)}) collective-permute-start(bf16[32,256]{1,0:T(8,128)(2,1)} %tile_records.1), channel_id=1, source_target_pairs={{0,32},{8,136},{16,48},{24,152},{32,0},{40,168},{48,16},{56,184},{... | collective-permute-start | bytes 49160 | tf_op jit(solution)/shard_map/ppermute | solution.py:336
  14.9 0.7 collective-permute-start.3
  15.6 1.5 %collective-permute-start.4 = (bf16[8,16,616]{2,1,0:T(8,128)(2,1)S(1)}, bf16[8,16,616]{2,1,0:T(8,128)(2,1)S(1)}, u32[]{:S(2)}, u32[]{:S(2)}) collective-permute-start(bf16[8,16,616]{2,1,0:T(8,128)(2,1)S(1)} %slice.19), channel_id=1, source_target_pairs={{0,48},{8,200},{16,0},{24,216},{32,16},{40,232},{48,32},{56,248},{... | collective-permute-start | bytes 473096 | tf_op jit(solution)/shard_map/ppermute | solution.py:336
  17.1 1.1 pad_maximum_fusion.refs_0_
  18.3 0.7 pad_maximum_fusion.3
  19.0 2.7 %collective-permute-done.3 = bf16[8,16,616]{2,1,0:T(8,128)(2,1)S(1)} collective-permute-done((bf16[8,16,616]{2,1,0:T(8,128)(2,1)S(1)}, bf16[8,16,616]{2,1,0:T(8,128)(2,1)S(1)}, u32[]{:S(2)}, u32[]{:S(2)}) %collective-permute-start.3) | collective-permute-done | bytes 157728 | tf_op jit(solution)/shard_map/ppermute | solution.py:336
  21.8 1.6 %collective-permute-start.8 = (bf16[2,16,16,616]{3,2,1,0:T(8,128)(2,1)S(1)}, bf16[2,16,16,616]{3,2,1,0:T(8,128)(2,1)}, u32[]{:S(2)}, u32[]{:S(2)}) collective-permute-start(bf16[2,16,16,616]{3,2,1,0:T(8,128)(2,1)S(1)} %pad_maximum_fusion.1.refs_1_), channel_id=1, source_target_pairs={{0,192},{8,56},{16,208},{24,8},{32,224},{40,24},{48,240},{56,40},{... | collective-permute-start | bytes 1892360 | tf_op jit(solution)/shard_map/ppermute | solution.py:336
  23.9 2.8 %collective-permute-start.10 = (bf16[4,32,256]{2,1,0:T(8,128)(2,1)S(1)}, bf16[4,32,256]{2,1,0:T(8,128)(2,1)S(1)}, u32[]{:S(2)}, u32[]{:S(2)}) collective-permute-start(bf16[4,32,256]{2,1,0:T(8,128)(2,1)S(1)} %pad_maximum_fusion.3), channel_id=1, source_target_pairs={{0,192},{8,56},{16,208},{24,8},{32,224},{40,24},{48,240},{56,40},{... | collective-permute-start | bytes 196616 | tf_op jit(solution)/shard_map/ppermute | solution.py:336
  26.7 4.0 %collective-permute-done.9 = bf16[4,32,256]{2,1,0:T(8,128)(2,1)S(1)} collective-permute-done((bf16[4,32,256]{2,1,0:T(8,128)(2,1)S(1)}, bf16[4,32,256]{2,1,0:T(8,128)(2,1)S(1)}, u32[]{:S(2)}, u32[]{:S(2)}) %collective-permute-start.9) | collective-permute-done | bytes 65568 | tf_op jit(solution)/shard_map/ppermute | solution.py:336
  31.0 2.2 %collective-permute-done.10 = bf16[4,32,256]{2,1,0:T(8,128)(2,1)S(1)} collective-permute-done((bf16[4,32,256]{2,1,0:T(8,128)(2,1)S(1)}, bf16[4,32,256]{2,1,0:T(8,128)(2,1)S(1)}, u32[]{:S(2)}, u32[]{:S(2)}) %collective-permute-start.10) | collective-permute-done | bytes 65568 | tf_op jit(solution)/shard_map/ppermute | solution.py:336
  33.2 3.3 %collective-permute-done.11 = bf16[4,32,256]{2,1,0:T(8,128)(2,1)S(1)} collective-permute-done((bf16[4,32,256]{2,1,0:T(8,128)(2,1)S(1)}, bf16[4,32,256]{2,1,0:T(8,128)(2,1)S(1)}, u32[]{:S(2)}, u32[]{:S(2)}) %collective-permute-start.11) | collective-permute-done | bytes 65568 | tf_op jit(solution)/shard_map/ppermute | solution.py:336
  36.7 3.2 %collective-permute-start.16 = (bf16[2,16,16,616]{3,2,1,0:T(8,128)(2,1)S(1)}, bf16[2,16,16,616]{3,2,1,0:T(8,128)(2,1)}, u32[]{:S(2)}, u32[]{:S(2)}) collective-permute-start(bf16[2,16,16,616]{3,2,1,0:T(8,128)(2,1)S(1)} %pad_maximum_fusion.refs_0_), channel_id=1, source_target_pairs={{0,192},{8,56},{16,208},{24,8},{32,224},{40,24},{48,240},{56,40},{... | collective-permute-start | bytes 1892360 | tf_op jit(solution)/shard_map/ppermute | solution.py:336
  39.9 3.2 %collective-permute-start.18 = (bf16[2,16,16,616]{3,2,1,0:T(8,128)(2,1)}, bf16[2,16,16,616]{3,2,1,0:T(8,128)(2,1)}, u32[]{:S(2)}, u32[]{:S(2)}) collective-permute-start(bf16[2,16,16,616]{3,2,1,0:T(8,128)(2,1)} %collective-permute-done.8.refs_5_), channel_id=1, source_target_pairs={{0,192},{8,56},{16,208},{24,8},{32,224},{40,24},{48,240},{56,40},{... | collective-permute-start | bytes 1892360 | tf_op jit(solution)/shard_map/ppermute | solution.py:336
  43.2 1.4 %collective-permute-done.14.pos_ref = bf16[32,2,128]{2,1,0:T(2,128)(2,1)S(1)} collective-permute-done((bf16[32,2,128]{2,1,0:T(2,128)(2,1)}, bf16[32,2,128]{2,1,0:T(2,128)(2,1)S(1)}, u32[]{:S(2)}, u32[]{:S(2)}) %collective-permute-start.14) | collective-permute-done | bytes 16416 | tf_op jit(solution)/shard_map/ppermute | solution.py:375
  44.8 1.0 copy-done
  45.8 0.7 copy-done.4
  46.5 7.0 %grid_tiles.2.own_ref = bf16[16,384,616]{2,1,0:T(8,128)(2,1)S(1)} custom-call(bf16[32,616,128]{2,1,0:T(8,128)(2,1)} %bitcast.72, bf16[32,2,128]{2,1,0:T(2,128)(2,1)S(1)} %bitcast.70, f32[4,256,128]{2,1,0:T(8,128)S(1)} %copy-done), custom_call_target="tpu_custom_call" | custom-call | flops 1000000 | bytes 10000 | tf_op jit(solution)/shard_map/grid_tiles/pallas_call | solution.py:163
  53.6 7.1 %grid_tiles.3.sib_ref = bf16[16,384,616]{2,1,0:T(8,128)(2,1)S(1)} custom-call(bf16[32,616,128]{2,1,0:T(8,128)(2,1)} %collective-permute-done.12.swath_ref, bf16[32,2,128]{2,1,0:T(2,128)(2,1)S(1)} %collective-permute-done.14.pos_ref, f32[4,256,128]{2,1,0:T(8,128)S(1)} %copy-done.1), custom_call_target="tpu_custom_call" | custom-call | flops 1000000 | bytes 10000 | tf_op jit(solution)/shard_map/grid_tiles/pallas_call | solution.py:163
  60.7 1.4 %inverse_density.1 = (f32[16,768]{1,0:T(8,128)S(1)}, s32[1,768]{1,0:T(1,128)S(1)}) custom-call(s32[1]{0:T(128)} %bitcast.19.core_ref, bf16[512,256]{1,0:T(8,128)(2,1)S(1)} %bitcast.63, bf16[512,256]{1,0:T(8,128)(2,1)S(1)} %bitcast.66, s32[1,768]{1,0:T(1,128)S(1)} %copy-done.6, bf16[64,768]{1,0:T(8,128)(2,1)S(1)} %copy-done.3, ...), custom_call_target="tpu_custom_call" | custom-call | flops 1000000 | bytes 10000 | tf_op jit(solution)/shard_map/inverse_density/pallas_call | solution.py:124
  62.2 12.2 %embed_tiles.1 = bf16[1536,256]{1,0:T(8,128)(2,1)} custom-call(bf16[16,384,616]{2,1,0:T(8,128)(2,1)S(1)} %grid_tiles.2.own_ref, bf16[16,384,616]{2,1,0:T(8,128)(2,1)S(1)} %grid_tiles.3.sib_ref, bf16[2,16,16,616]{3,2,1,0:T(8,128)(2,1)S(1)} %pad_maximum_fusion.refs_0_, bf16[2,16,16,616]{3,2,1,0:T(8,128)(2,1)S(1)} %pad_maximum_fusion.1.refs_1_, ...), custom_call_target="tpu_custom_call" | custom-call | flops 9663676416 | bytes 1000000 | tf_op jit(solution)/shard_map/embed_tiles/pallas_call | solution.py:208
  74.9 5.4 %all-to-all-start = ((bf16[32,48,256]{2,1,0:T(8,128)(2,1)}), bf16[32,48,256]{2,1,0:T(8,128)(2,1)S(1)}, u32[]{:S(2)}, u32[]{:S(2)}) async-start(bf16[32,48,256]{2,1,0:T(8,128)(2,1)} %bitcast.22), calls=%async_computation | async-start | bytes 1572864 | tf_op jit(solution)/shard_map/all_to_all | solution.py:412
  80.8 1.3 %copy.32 = bf16[16,2,16,1024]{3,2,0,1:T(8,128)(2,1)S(1)} copy(bf16[16,2,16,1024]{3,2,1,0:T(8,128)(2,1)} %bitcast.73) | data formatting | bytes 2097152 | tf_op jit(solution)/shard_map/reshape | solution.py:429
  84.1 9.7 %all-to-all-done = bf16[32,48,256]{2,1,0:T(8,128)(2,1)S(1)} async-done(((bf16[32,48,256]{2,1,0:T(8,128)(2,1)}), bf16[32,48,256]{2,1,0:T(8,128)(2,1)S(1)}, u32[]{:S(2)}, u32[]{:S(2)}) %all-to-all-start) | async-done | bytes 786464 | tf_op jit(solution)/shard_map/all_to_all | solution.py:412
  93.7 2.9 %attend_source.1 = bf16[128,640]{1,0:T(8,128)(2,1)S(1)} custom-call(bf16[16,2,48,256]{3,2,1,0:T(8,128)(2,1)S(1)} %bitcast.65, s32[1,768]{1,0:T(1,128)S(1)} %select_n.396.row_ref, f32[1,512]{1,0:T(1,128)S(1)} %broadcast_in_dim_reshape.6.bias_ref, f32[1,512]{1,0:T(1,128)S(1)} %broadcast_in_dim_reshape.7.gain_ref, bf16[512,1024]{1,0:T(8,128)(2,1)S(1)} %bitcast.64, ...), custom_call_target="tpu_custom_call" | custom-call | flops 1572864000 | bytes 3000000 | tf_op jit(solution)/shard_map/attend_source/pallas_call | solution.py:283
  96.7 17.2 %all_to_all.10.parts_ref = bf16[8,16,640]{2,1,0:T(8,128)(2,1)} all-to-all(bf16[8,16,640]{2,1,0:T(8,128)(2,1)S(1)} %bitcast.67), channel_id=1, replica_groups=mesh['lat'=32,'src'=8] {'src'}, dimensions={0} | all-to-all | bytes 327680 | tf_op jit(solution)/shard_map/all_to_all | solution.py:441
  113.8 2.1 %combine_sources.1 = f32[4,4,512]{2,1,0:T(4,128)} custom-call(bf16[8,16,640]{2,1,0:T(8,128)(2,1)} %all_to_all.10.parts_ref, bf16[512,512]{1,0:T(8,128)(2,1)} %weight_ref.1), custom_call_target="tpu_custom_call" | custom-call | flops 33554432 | bytes 800000 | tf_op jit(solution)/shard_map/combine_sources/pallas_call | solution.py:312
  (72 shorter events, 4.9 us)
Async XLA Ops:
  0.0 36.6 %collective-permute-start.12 = (bf16[32,616,128]{2,1,0:T(8,128)(2,1)}, bf16[32,616,128]{2,1,0:T(8,128)(2,1)}, u32[]{:S(2)}, u32[]{:S(2)}) collective-permute-start(bf16[32,616,128]{2,1,0:T(8,128)(2,1)} %bitcast.71), channel_id=1, source_target_pairs={{0,8},{8,0},{16,24},{24,16},{32,40},{40,32},{48,56},{56,48},{64,72... | collective-permute-start | bytes 15138824 | tf_op jit(solution)/shard_map/ppermute | solution.py:374
  0.0 7.5 %collective-permute-start = (bf16[16,16,616]{2,1,0:T(8,128)(2,1)}, bf16[16,16,616]{2,1,0:T(8,128)(2,1)S(1)}, u32[]{:S(2)}, u32[]{:S(2)}) collective-permute-start(bf16[16,16,616]{2,1,0:T(8,128)(2,1)} %bitcast.78), channel_id=1, source_target_pairs={{0,16},{8,72},{16,32},{24,88},{32,48},{40,104},{48,0},{56,120},{64... | collective-permute-start | bytes 946184 | tf_op jit(solution)/shard_map/ppermute | solution.py:336
  1.5 7.3 %collective-permute-start.1 = (bf16[16,16,616]{2,1,0:T(8,128)(2,1)}, bf16[16,16,616]{2,1,0:T(8,128)(2,1)S(1)}, u32[]{:S(2)}, u32[]{:S(2)}) collective-permute-start(bf16[16,16,616]{2,1,0:T(8,128)(2,1)} %bitcast.79), channel_id=1, source_target_pairs={{0,48},{8,200},{16,0},{24,216},{32,16},{40,232},{48,32},{56,248},{... | collective-permute-start | bytes 946184 | tf_op jit(solution)/shard_map/ppermute | solution.py:336
  8.8 6.8 %collective-permute-start.5 = (bf16[32,256]{1,0:T(8,128)(2,1)}, bf16[32,256]{1,0:T(8,128)(2,1)S(1)}, u32[]{:S(2)}, u32[]{:S(2)}) collective-permute-start(bf16[32,256]{1,0:T(8,128)(2,1)} %tile_records.1), channel_id=1, source_target_pairs={{0,16},{8,72},{16,32},{24,88},{32,48},{40,104},{48,0},{56,120},{64... | collective-permute-start | bytes 49160 | tf_op jit(solution)/shard_map/ppermute | solution.py:336
  10.2 8.0 %collective-permute-start.6 = (bf16[32,256]{1,0:T(8,128)(2,1)}, bf16[32,256]{1,0:T(8,128)(2,1)S(1)}, u32[]{:S(2)}, u32[]{:S(2)}) collective-permute-start(bf16[32,256]{1,0:T(8,128)(2,1)} %tile_records.1), channel_id=1, source_target_pairs={{0,48},{8,200},{16,0},{24,216},{32,16},{40,232},{48,32},{56,248},{... | collective-permute-start | bytes 49160 | tf_op jit(solution)/shard_map/ppermute | solution.py:336
  10.8 7.5 %collective-permute-start.7 = (bf16[32,256]{1,0:T(8,128)(2,1)}, bf16[32,256]{1,0:T(8,128)(2,1)S(1)}, u32[]{:S(2)}, u32[]{:S(2)}) collective-permute-start(bf16[32,256]{1,0:T(8,128)(2,1)} %tile_records.1), channel_id=1, source_target_pairs={{0,32},{8,136},{16,48},{24,152},{32,0},{40,168},{48,16},{56,184},{... | collective-permute-start | bytes 49160 | tf_op jit(solution)/shard_map/ppermute | solution.py:336
  14.9 6.8 %collective-permute-start.3 = (bf16[8,16,616]{2,1,0:T(8,128)(2,1)S(1)}, bf16[8,16,616]{2,1,0:T(8,128)(2,1)S(1)}, u32[]{:S(2)}, u32[]{:S(2)}) collective-permute-start(bf16[8,16,616]{2,1,0:T(8,128)(2,1)S(1)} %slice.18), channel_id=1, source_target_pairs={{0,16},{8,72},{16,32},{24,88},{32,48},{40,104},{48,0},{56,120},{64... | collective-permute-start | bytes 473096 | tf_op jit(solution)/shard_map/ppermute | solution.py:336
  15.6 6.1 %collective-permute-start.4 = (bf16[8,16,616]{2,1,0:T(8,128)(2,1)S(1)}, bf16[8,16,616]{2,1,0:T(8,128)(2,1)S(1)}, u32[]{:S(2)}, u32[]{:S(2)}) collective-permute-start(bf16[8,16,616]{2,1,0:T(8,128)(2,1)S(1)} %slice.19), channel_id=1, source_target_pairs={{0,48},{8,200},{16,0},{24,216},{32,16},{40,232},{48,32},{56,248},{... | collective-permute-start | bytes 473096 | tf_op jit(solution)/shard_map/ppermute | solution.py:336
  18.2 18.4 %collective-permute-start.2 = (bf16[2,16,16,616]{3,2,1,0:T(8,128)(2,1)S(1)}, bf16[2,16,16,616]{3,2,1,0:T(8,128)(2,1)S(1)}, u32[]{:S(2)}, u32[]{:S(2)}) collective-permute-start(bf16[2,16,16,616]{3,2,1,0:T(8,128)(2,1)S(1)} %pad_maximum_fusion.refs_0_), channel_id=1, source_target_pairs={{0,64},{8,24},{16,80},{24,40},{32,96},{40,56},{48,112},{56,8},{64,... | collective-permute-start | bytes 1892360 | tf_op jit(solution)/shard_map/ppermute | solution.py:336
  19.0 34.5 %copy-start.1 = (f32[4,256,128]{2,1,0:T(8,128)S(1)}, f32[4,256,128]{2,1,0:T(8,128)}, u32[]{:S(2)}) copy-start(f32[4,256,128]{2,1,0:T(8,128)} %constant.169.clone.center_ref) | copy-start | bytes 1572868
  21.8 14.7 %collective-permute-start.8 = (bf16[2,16,16,616]{3,2,1,0:T(8,128)(2,1)S(1)}, bf16[2,16,16,616]{3,2,1,0:T(8,128)(2,1)}, u32[]{:S(2)}, u32[]{:S(2)}) collective-permute-start(bf16[2,16,16,616]{3,2,1,0:T(8,128)(2,1)S(1)} %pad_maximum_fusion.1.refs_1_), channel_id=1, source_target_pairs={{0,192},{8,56},{16,208},{24,8},{32,224},{40,24},{48,240},{56,40},{... | collective-permute-start | bytes 1892360 | tf_op jit(solution)/shard_map/ppermute | solution.py:336
  23.5 7.3 %collective-permute-start.9 = (bf16[4,32,256]{2,1,0:T(8,128)(2,1)S(1)}, bf16[4,32,256]{2,1,0:T(8,128)(2,1)S(1)}, u32[]{:S(2)}, u32[]{:S(2)}) collective-permute-start(bf16[4,32,256]{2,1,0:T(8,128)(2,1)S(1)} %pad_maximum_fusion.3), channel_id=1, source_target_pairs={{0,64},{8,24},{16,80},{24,40},{32,96},{40,56},{48,112},{56,8},{64,... | collective-permute-start | bytes 196616 | tf_op jit(solution)/shard_map/ppermute | solution.py:336
  23.9 9.3 %collective-permute-start.10 = (bf16[4,32,256]{2,1,0:T(8,128)(2,1)S(1)}, bf16[4,32,256]{2,1,0:T(8,128)(2,1)S(1)}, u32[]{:S(2)}, u32[]{:S(2)}) collective-permute-start(bf16[4,32,256]{2,1,0:T(8,128)(2,1)S(1)} %pad_maximum_fusion.3), channel_id=1, source_target_pairs={{0,192},{8,56},{16,208},{24,8},{32,224},{40,24},{48,240},{56,40},{... | collective-permute-start | bytes 196616 | tf_op jit(solution)/shard_map/ppermute | solution.py:336
  30.8 5.8 %collective-permute-start.11 = (bf16[4,32,256]{2,1,0:T(8,128)(2,1)S(1)}, bf16[4,32,256]{2,1,0:T(8,128)(2,1)S(1)}, u32[]{:S(2)}, u32[]{:S(2)}) collective-permute-start(bf16[4,32,256]{2,1,0:T(8,128)(2,1)S(1)} %pad_maximum_fusion.3), channel_id=1, source_target_pairs={{0,128},{8,40},{16,144},{24,56},{32,160},{40,8},{48,176},{56,24},{... | collective-permute-start | bytes 196616 | tf_op jit(solution)/shard_map/ppermute | solution.py:336
  36.6 25.5 %collective-permute-start.15 = (bf16[2,16,16,616]{3,2,1,0:T(8,128)(2,1)S(1)}, bf16[2,16,16,616]{3,2,1,0:T(8,128)(2,1)}, u32[]{:S(2)}, u32[]{:S(2)}) collective-permute-start(bf16[2,16,16,616]{3,2,1,0:T(8,128)(2,1)S(1)} %pad_maximum_fusion.1.refs_1_), channel_id=1, source_target_pairs={{0,64},{8,24},{16,80},{24,40},{32,96},{40,56},{48,112},{56,8},{64,... | collective-permute-start | bytes 1892360 | tf_op jit(solution)/shard_map/ppermute | solution.py:336
  36.7 25.4 %collective-permute-start.16 = (bf16[2,16,16,616]{3,2,1,0:T(8,128)(2,1)S(1)}, bf16[2,16,16,616]{3,2,1,0:T(8,128)(2,1)}, u32[]{:S(2)}, u32[]{:S(2)}) collective-permute-start(bf16[2,16,16,616]{3,2,1,0:T(8,128)(2,1)S(1)} %pad_maximum_fusion.refs_0_), channel_id=1, source_target_pairs={{0,192},{8,56},{16,208},{24,8},{32,224},{40,24},{48,240},{56,40},{... | collective-permute-start | bytes 1892360 | tf_op jit(solution)/shard_map/ppermute | solution.py:336
  39.9 22.2 %collective-permute-start.17 = (bf16[2,16,16,616]{3,2,1,0:T(8,128)(2,1)S(1)}, bf16[2,16,16,616]{3,2,1,0:T(8,128)(2,1)}, u32[]{:S(2)}, u32[]{:S(2)}) collective-permute-start(bf16[2,16,16,616]{3,2,1,0:T(8,128)(2,1)S(1)} %collective-permute-done.2.refs_2_), channel_id=1, source_target_pairs={{0,64},{8,24},{16,80},{24,40},{32,96},{40,56},{48,112},{56,8},{64,... | collective-permute-start | bytes 1892360 | tf_op jit(solution)/shard_map/ppermute | solution.py:336
  39.9 22.2 %collective-permute-start.18 = (bf16[2,16,16,616]{3,2,1,0:T(8,128)(2,1)}, bf16[2,16,16,616]{3,2,1,0:T(8,128)(2,1)}, u32[]{:S(2)}, u32[]{:S(2)}) collective-permute-start(bf16[2,16,16,616]{3,2,1,0:T(8,128)(2,1)} %collective-permute-done.8.refs_5_), channel_id=1, source_target_pairs={{0,192},{8,56},{16,208},{24,8},{32,224},{40,24},{48,240},{56,40},{... | collective-permute-start | bytes 1892360 | tf_op jit(solution)/shard_map/ppermute | solution.py:336
  43.1 1.4 %collective-permute-start.14 = (bf16[32,2,128]{2,1,0:T(2,128)(2,1)}, bf16[32,2,128]{2,1,0:T(2,128)(2,1)S(1)}, u32[]{:S(2)}, u32[]{:S(2)}) collective-permute-start(bf16[32,2,128]{2,1,0:T(2,128)(2,1)} %bitcast.69), channel_id=1, source_target_pairs={{0,8},{8,0},{16,24},{24,16},{32,40},{40,32},{48,56},{56,48},{64,72... | collective-permute-start | bytes 49160 | tf_op jit(solution)/shard_map/ppermute | solution.py:375
  44.5 16.1 %collective-permute-start.13 = (bf16[4,4,32,256]{3,2,1,0:T(8,128)(2,1)S(1)}, bf16[4,4,32,256]{3,2,1,0:T(8,128)(2,1)S(1)}, u32[]{:S(2)}, u32[]{:S(2)}) collective-permute-start(bf16[4,4,32,256]{3,2,1,0:T(8,128)(2,1)S(1)} %pad_maximum_fusion.2), channel_id=1, source_target_pairs={{0,8},{8,0},{16,24},{24,16},{32,40},{40,32},{48,56},{56,48},{64,72... | collective-permute-start | bytes 786440 | tf_op jit(solution)/shard_map/ppermute | solution.py:390
  44.7 1.0 copy-start
  45.8 0.7 copy-start.4
  53.5 7.1 %copy-start.2 = (bf16[192,768]{1,0:T(8,128)(2,1)S(1)}, bf16[192,768]{1,0:T(8,128)(2,1)}, u32[]{:S(2)}) copy-start(bf16[192,768]{1,0:T(8,128)(2,1)} %constant.173.clone.own_cell_ref) | copy-start | bytes 884740
  53.6 7.1 %copy-start.3 = (bf16[64,768]{1,0:T(8,128)(2,1)S(1)}, bf16[64,768]{1,0:T(8,128)(2,1)}, u32[]{:S(2)}) copy-start(bf16[64,768]{1,0:T(8,128)(2,1)} %constant.172.clone.row_tile_ref) | copy-start | bytes 294916
  53.6 7.1 %copy-start.5 = (bf16[16,192]{1,0:T(8,128)(2,1)S(1)}, bf16[16,192]{1,0:T(8,128)(2,1)}, u32[]{:S(2)}) copy-start(bf16[16,192]{1,0:T(8,128)(2,1)} %constant.174.clone.tap_ref) | copy-start | bytes 18436
  53.6 7.1 %copy-start.6 = (s32[1,768]{1,0:T(1,128)S(1)}, s32[1,768]{1,0:T(1,128)}, u32[]{:S(2)}) copy-start(s32[1,768]{1,0:T(1,128)} %constant.182.token_ref) | copy-start | bytes 9220
  62.1 18.3 %copy-start.10 = (bf16[32,32,1]{1,0,2:T(8,128)(2,1)S(1)}, bf16[32,32,1]{1,0,2:T(8,128)(2,1)}, u32[]{:S(2)}) copy-start(bf16[32,32,1]{1,0,2:T(8,128)(2,1)} %constant.285) | copy-start | bytes 6148
  62.1 20.9 %copy-start.9 = (f32[1,512]{1,0:T(1,128)S(1)}, f32[1,512]{1,0:T(1,128)}, u32[]{:S(2)}) copy-start(f32[1,512]{1,0:T(1,128)} %param.22) | copy-start | bytes 6148
  62.1 21.8 %copy-start.8 = (f32[512]{0:T(512)S(1)}, f32[512]{0:T(512)}, u32[]{:S(2)}) copy-start(f32[512]{0:T(512)} %param.23) | copy-start | bytes 6148
  62.1 31.6 %copy-start.7 = (f32[4,512]{1,0:T(4,128)S(1)}, f32[4,512]{1,0:T(4,128)}, u32[]{:S(2)}) copy-start(f32[4,512]{1,0:T(4,128)} %latent_ref.1) | copy-start | bytes 24580
  74.9 18.8 %all-to-all-start = ((bf16[32,48,256]{2,1,0:T(8,128)(2,1)}), bf16[32,48,256]{2,1,0:T(8,128)(2,1)S(1)}, u32[]{:S(2)}, u32[]{:S(2)}) async-start(bf16[32,48,256]{2,1,0:T(8,128)(2,1)} %bitcast.22), calls=%async_computation | async-start | bytes 1572864 | tf_op jit(solution)/shard_map/all_to_all | solution.py:412

commit v4 on v3

--- a/solution.py
+++ b/solution.py
@@ -131,7 +131,7 @@
     )(core, own, sib, jnp.asarray(token, jnp.int32)[None], *(jnp.asarray(v, BF) for v in (row_tile, own_cell, tap)))
 
 
-def grid_kernel(swath_ref, pos_ref, center_ref, out_ref):
+def grid_kernel(swath_ref, pos_ref, center_ref, after_ref, out_ref, done_ref):
     channels = swath_ref.shape[1]
     gap = jnp.zeros((TAPS, 8, FP), F32)
 
@@ -154,21 +154,22 @@
     pltpu.emit_pipeline(
         step, grid=(TILES // 4,), in_specs=[pl.BlockSpec((4, channels, FP), lambda i: (i, 0, 0))]
     )(swath_ref)
-
-
-def gridded(swath, pos, center):
+    done_ref[...] = after_ref[...]
+
+
+def gridded(swath, pos, center, after):
     channels = swath.shape[1]
     vmem = pl.BlockSpec(memory_space=pltpu.VMEM)
     swath = pltpu.with_memory_space_constraint(swath, pltpu.HBM)
     return pl.pallas_call(
         grid_kernel,
-        in_specs=[pl.BlockSpec(memory_space=pl.ANY), vmem, vmem],
-        out_specs=vmem,
-        out_shape=pltpu.VMEM((TAPS, TILES * TPS, channels), BF),
+        in_specs=[pl.BlockSpec(memory_space=pl.ANY), vmem, vmem, vmem],
+        out_specs=(vmem, vmem),
+        out_shape=(pltpu.VMEM((TAPS, TILES * TPS, channels), BF), jax.ShapeDtypeStruct((8, FP), F32)),
         compiler_params=pltpu.CompilerParams(vmem_limit_bytes=KERNEL_VMEM // 2),
         cost_estimate=SMALL,
         name="grid_tiles",
-    )(swath, pos, center)
+    )(swath, pos, center, after)
 
 
 def embed_kernel(own_ref, sib_ref, *refs):
@@ -192,7 +193,7 @@
         spread[pl.ds(base, part), :] = jnp.where(here == row_ref[...], 1.0, 0.0).astype(BF)
         return carry
 
-    lax.fori_loop(0, TAPS, tap, 0)
+    lax.fori_loop(0, TAPS, tap, 0, unroll=4)
     columns = lax.broadcasted_iota(jnp.int32, (width, width), 0)
     order = jnp.where(columns == column_ref[...], 1.0, 0.0).astype(BF)
     tokens = lax.dot_general(total[...].astype(BF), order, NT, preferred_element_type=F32).astype(BF)
@@ -377,19 +378,21 @@
     up, down, record = lax.optimization_barrier((up, down, record))
     far = [send(up[:half], 1, False), send(down[half:], -1, False)]
     others = [send(record, -offset, False) for offset in OFFSETS[1:]]
-    *far, record = lax.optimization_barrier((*far, jnp.stack([record] + others, 0)))
+    *far, record, sib_pos, swath = lax.optimization_barrier(
+        (*far, jnp.stack([record] + others, 0), sib_pos, swath)
+    )
     low = jnp.stack([shard, up], 0)
     high = jnp.stack([down, jnp.concatenate(far, 0)], 0)
     above_low, below_high = send(low, 1, True), send(high, -1, True)
+    above_high, below_low = send(high, 1, True), send(low, -1, True)
     record = jnp.stack([record] + [send(record, -offset, True) for offset in OFFSETS[1:]], 0)
-    above_low, below_high, low, high, record, swath, sib_swath = lax.optimization_barrier(
-        (above_low, below_high, low, high, record, swath, sib_swath)
+    own, after = gridded(swath, fp_pos, center, jnp.zeros((8, FP), F32))
+    above_low, below_high, above_high, below_low, record, sib_swath, after = lax.optimization_barrier(
+        (above_low, below_high, above_high, below_low, record, sib_swath, after)
     )
     corner_low, corner_high = send(above_low, 1, True), send(below_high, -1, True)
-    above_high, below_low = send(high, 1, True), send(low, -1, True)
     sib_record = lax.ppermute(record, "lat", swap)
-    own = gridded(swath, fp_pos, center)
-    sib = gridded(sib_swath, sib_pos, center)
+    sib, _ = gridded(sib_swath, sib_pos, center, after)
     weights = [low, high, above_low, above_high, below_low, below_high, corner_low, corner_high]
 
     inverse, rows = inverse_density(

time: 117 us -> 122 us (1.043)
  local copies, waits for them, and re-layouts: 4.86 us -> 15.1 us
  waiting for transfers between devices: 27.2 us -> 22.2 us
  Pallas kernels: 35.3 us -> 33.4 us
  blocking collectives: 17.2 us -> 18.6 us
    unnamed x22 -> x34, local copies, waits for them, and re-layouts: 1.81 us -> 12 us
    ppermute x16, waiting for transfers between devices: 16.1 us -> 12.8 us  [send(): return lax.ppermute(array, 'lat', shift(offset, second))]
    pallas_call x1, Pallas kernels: 12.2 us -> 9.79 us  [embed(): pl.pallas_call(embed_kernel, in_specs=[vmem] * (len(large) + 3), out_spec...]
    all_to_all x1, starting transfers between devices: 5.43 us -> 7.34 us  [body(): lax.all_to_all(outgoing, 'lat', split_axis=0, concat_axis=0, tiled=True)]
    ppermute x16, starting transfers between devices: 22.3 us -> 20.6 us  [send(): return lax.ppermute(array, 'lat', shift(offset, second))]
    all_to_all x1, blocking collectives: 17.2 us -> 18.6 us  [body(): lax.all_to_all(parts.reshape(sources, -1, width + FP), 'src', split_axis=...]
  transfers between devices with their start and end apart: 20 -> 20, of which waited for: 8 -> 8; matrix products, arithmetic and copies ran while one was open for 5% -> 5% of each run, Pallas kernels for 16% -> 15%
where the time goes in v4:
time: 122 us; the launch traced here: 121 us
  Pallas kernels  33.4 us (27%)
  starting transfers between devices  28.2 us (23%)
  waiting for transfers between devices  22.2 us (18%)
  blocking collectives  18.6 us (15%)
  local copies, waits for them, and re-layouts  15.1 us (12%)
  other arithmetic  2.92 us (2%)
    ppermute x16, starting transfers between devices, send(): return lax.ppermute(array, 'lat', shift(offset, second))  20.6 us
    all_to_all x1, blocking collectives, body(): lax.all_to_all(parts.reshape(sources, -1, width + FP), 'src', split_axis=...  18.6 us
    pallas_call x2, Pallas kernels, gridded(): pl.pallas_call(grid_kernel, in_specs=[pl.BlockSpec(memory_space=pl.ANY),...  14.7 us
    ppermute x16, waiting for transfers between devices, send(): return lax.ppermute(array, 'lat', shift(offset, second))  12.8 us
    unnamed x34, local copies, waits for them, and re-layouts  12 us
    pallas_call x1, Pallas kernels, embed(): pl.pallas_call(embed_kernel, in_specs=[vmem] * (len(large) + 3), out_spec...  9.79 us
    all_to_all x1, waiting for transfers between devices, body(): lax.all_to_all(outgoing, 'lat', split_axis=0, concat_axis=0, tiled=True)  8.93 us
    all_to_all x1, starting transfers between devices, body(): lax.all_to_all(outgoing, 'lat', split_axis=0, concat_axis=0, tiled=True)  7.34 us
  transfers between devices with their start and end apart: 20, of which 8 were waited for; matrix products, arithmetic and copies ran while one was open for 5% of the time, Pallas kernels for 15%

profile of v4, /device:TPU:2, one launch (start us, length us, event | category | flops | bytes accessed | tf_op | source)
XLA Modules:
  0.0 121.1 jit_solution(2174994965516164083)
XLA Ops:
  0.0 1.6 %collective-permute-start = (bf16[16,16,616]{2,1,0:T(8,128)(2,1)}, bf16[16,16,616]{2,1,0:T(8,128)(2,1)S(1)}, u32[]{:S(2)}, u32[]{:S(2)}) collective-permute-start(bf16[16,16,616]{2,1,0:T(8,128)(2,1)} %bitcast.78), channel_id=1, source_target_pairs={{0,16},{8,72},{16,32},{24,88},{32,48},{40,104},{48,0},{56,120},{64... | collective-permute-start | bytes 946184 | tf_op jit(solution)/shard_map/ppermute | solution.py:337
  2.4 2.6 %tile_records.1 = bf16[32,256]{1,0:T(8,128)(2,1)} custom-call(s32[32]{0:T(128)} %bitcast.93, s32[32]{0:T(128)} %bitcast.94, bf16[32,2,128]{2,1,0:T(2,128)(2,1)} %bitcast.68, f32[2,192,128]{2,1,0:T(8,128)} %constant.171.clone.center_ref), custom_call_target="tpu_custom_call" | custom-call | flops 1000000 | bytes 10000 | tf_op jit(solution)/shard_map/tile_records/pallas_call | solution.py:76
  5.0 2.6 %collective-permute-done = bf16[16,16,616]{2,1,0:T(8,128)(2,1)S(1)} collective-permute-done((bf16[16,16,616]{2,1,0:T(8,128)(2,1)}, bf16[16,16,616]{2,1,0:T(8,128)(2,1)S(1)}, u32[]{:S(2)}, u32[]{:S(2)}) %collective-permute-start) | collective-permute-done | bytes 315424 | tf_op jit(solution)/shard_map/ppermute | solution.py:337
  7.5 1.3 %collective-permute-done.1 = bf16[16,16,616]{2,1,0:T(8,128)(2,1)S(1)} collective-permute-done((bf16[16,16,616]{2,1,0:T(8,128)(2,1)}, bf16[16,16,616]{2,1,0:T(8,128)(2,1)S(1)}, u32[]{:S(2)}, u32[]{:S(2)}) %collective-permute-start.1) | collective-permute-done | bytes 315424 | tf_op jit(solution)/shard_map/ppermute | solution.py:337
  8.9 4.0 %collective-permute-start.7 = (bf16[32,256]{1,0:T(8,128)(2,1)}, bf16[32,256]{1,0:T(8,128)(2,1)S(1)}, u32[]{:S(2)}, u32[]{:S(2)}) collective-permute-start(bf16[32,256]{1,0:T(8,128)(2,1)} %tile_records.1), channel_id=1, source_target_pairs={{0,32},{8,136},{16,48},{24,152},{32,0},{40,168},{48,16},{56,184},{... | collective-permute-start | bytes 49160 | tf_op jit(solution)/shard_map/ppermute | solution.py:337
  12.8 2.0 %collective-permute-start.5 = (bf16[32,256]{1,0:T(8,128)(2,1)}, bf16[32,256]{1,0:T(8,128)(2,1)S(1)}, u32[]{:S(2)}, u32[]{:S(2)}) collective-permute-start(bf16[32,256]{1,0:T(8,128)(2,1)} %tile_records.1), channel_id=1, source_target_pairs={{0,16},{8,72},{16,32},{24,88},{32,48},{40,104},{48,0},{56,120},{64... | collective-permute-start | bytes 49160 | tf_op jit(solution)/shard_map/ppermute | solution.py:337
  15.1 2.1 %collective-permute-start.4 = (bf16[8,16,616]{2,1,0:T(8,128)(2,1)S(1)}, bf16[8,16,616]{2,1,0:T(8,128)(2,1)S(1)}, u32[]{:S(2)}, u32[]{:S(2)}) collective-permute-start(bf16[8,16,616]{2,1,0:T(8,128)(2,1)S(1)} %slice.19), channel_id=1, source_target_pairs={{0,48},{8,200},{16,0},{24,216},{32,16},{40,232},{48,32},{56,248},{... | collective-permute-start | bytes 473096 | tf_op jit(solution)/shard_map/ppermute | solution.py:337
  17.1 1.1 pad_maximum_fusion.refs_0_
  20.5 2.5 %collective-permute-start.14 = (bf16[4,32,256]{2,1,0:T(8,128)(2,1)S(1)}, bf16[4,32,256]{2,1,0:T(8,128)(2,1)S(1)}, u32[]{:S(2)}, u32[]{:S(2)}) collective-permute-start(bf16[4,32,256]{2,1,0:T(8,128)(2,1)S(1)} %pad_maximum_fusion.3), channel_id=1, source_target_pairs={{0,128},{8,40},{16,144},{24,56},{32,160},{40,8},{48,176},{56,24},{... | collective-permute-start | bytes 196616 | tf_op jit(solution)/shard_map/ppermute | solution.py:337
  22.9 1.1 collective-permute-start.13
  24.0 1.0 collective-permute-start.12
  25.1 5.5 %collective-permute-done.14 = bf16[4,32,256]{2,1,0:T(8,128)(2,1)S(1)} collective-permute-done((bf16[4,32,256]{2,1,0:T(8,128)(2,1)S(1)}, bf16[4,32,256]{2,1,0:T(8,128)(2,1)S(1)}, u32[]{:S(2)}, u32[]{:S(2)}) %collective-permute-start.14) | collective-permute-done | bytes 65568 | tf_op jit(solution)/shard_map/ppermute | solution.py:337
  30.6 1.3 %collective-permute-start.9 = (bf16[2,16,16,616]{3,2,1,0:T(8,128)(2,1)S(1)}, bf16[2,16,16,616]{3,2,1,0:T(8,128)(2,1)}, u32[]{:S(2)}, u32[]{:S(2)}) collective-permute-start(bf16[2,16,16,616]{3,2,1,0:T(8,128)(2,1)S(1)} %pad_maximum_fusion.1.refs_1_), channel_id=1, source_target_pairs={{0,192},{8,56},{16,208},{24,8},{32,224},{40,24},{48,240},{56,40},{... | collective-permute-start | bytes 1892360 | tf_op jit(solution)/shard_map/ppermute | solution.py:337
  31.9 1.0 collective-permute-start.10
  32.9 1.0 copy-done
  34.7 7.0 %grid_tiles.2 = (bf16[16,384,616]{2,1,0:T(8,128)(2,1)S(1)}, f32[8,128]{1,0:T(8,128)S(1)}) custom-call(bf16[32,616,128]{2,1,0:T(8,128)(2,1)} %bitcast.72, bf16[32,2,128]{2,1,0:T(2,128)(2,1)S(1)} %bitcast.70, f32[4,256,128]{2,1,0:T(8,128)S(1)} %copy-done, f32[8,128]{1,0:T(8,128)S(1)} %broadcast_in_dim.39.after_ref), custom_call_target="tpu_custom_call" | custom-call | flops 1000000 | bytes 10000 | tf_op jit(solution)/shard_map/grid_tiles/pallas_call | solution.py:164
  41.7 3.0 %copy-done.7 = bf16[16,384,616]{2,1,0:T(8,128)(2,1)} copy-done((bf16[16,384,616]{2,1,0:T(8,128)(2,1)}, bf16[16,384,616]{2,1,0:T(8,128)(2,1)S(1)}, u32[]{:S(2)}) %copy-start.7) | copy-done | bytes 7569432
  45.7 2.6 %collective-permute-done.9.refs_5_ = bf16[2,16,16,616]{3,2,1,0:T(8,128)(2,1)} collective-permute-done((bf16[2,16,16,616]{3,2,1,0:T(8,128)(2,1)S(1)}, bf16[2,16,16,616]{3,2,1,0:T(8,128)(2,1)}, u32[]{:S(2)}, u32[]{:S(2)}) %collective-permute-start.9) | collective-permute-done | bytes 630816 | tf_op jit(solution)/shard_map/ppermute | solution.py:337
  48.3 0.9 copy-done.11
  49.2 3.2 %collective-permute-start.18 = (bf16[2,16,16,616]{3,2,1,0:T(8,128)(2,1)}, bf16[2,16,16,616]{3,2,1,0:T(8,128)(2,1)}, u32[]{:S(2)}, u32[]{:S(2)}) collective-permute-start(bf16[2,16,16,616]{3,2,1,0:T(8,128)(2,1)} %collective-permute-done.9.refs_5_), channel_id=1, source_target_pairs={{0,192},{8,56},{16,208},{24,8},{32,224},{40,24},{48,240},{56,40},{... | collective-permute-start | bytes 1892360 | tf_op jit(solution)/shard_map/ppermute | solution.py:337
  52.6 7.6 %grid_tiles.3 = (bf16[16,384,616]{2,1,0:T(8,128)(2,1)S(1)}, f32[8,128]{1,0:T(8,128)}) custom-call(bf16[32,616,128]{2,1,0:T(8,128)(2,1)} %collective-permute-done.15.swath_ref, bf16[32,2,128]{2,1,0:T(2,128)(2,1)S(1)} %collective-permute-done.8.pos_ref, f32[4,256,128]{2,1,0:T(8,128)S(1)} %copy-done.1, f32[8,128]{1,0:T(8,128)S(1)} %get-tuple-element.43.after_ref), custom_call_target="tpu_custom_call" | custom-call | flops 1000000 | bytes 10000 | tf_op jit(solution)/shard_map/grid_tiles/pallas_call | solution.py:164
  60.3 1.4 %inverse_density.1 = (f32[16,768]{1,0:T(8,128)S(1)}, s32[1,768]{1,0:T(1,128)S(1)}) custom-call(s32[1]{0:T(128)} %bitcast.19.core_ref, bf16[512,256]{1,0:T(8,128)(2,1)S(1)} %bitcast.63, bf16[512,256]{1,0:T(8,128)(2,1)S(1)} %bitcast.66, s32[1,768]{1,0:T(1,128)S(1)} %copy-done.6, bf16[64,768]{1,0:T(8,128)(2,1)S(1)} %copy-done.3, ...), custom_call_target="tpu_custom_call" | custom-call | flops 1000000 | bytes 10000 | tf_op jit(solution)/shard_map/inverse_density/pallas_call | solution.py:124
  61.7 3.2 %copy-done.8 = bf16[16,384,616]{2,1,0:T(8,128)(2,1)S(1)} copy-done((bf16[16,384,616]{2,1,0:T(8,128)(2,1)S(1)}, bf16[16,384,616]{2,1,0:T(8,128)(2,1)}, u32[]{:S(2)}) %copy-start.8) | copy-done | bytes 7569432
  64.9 1.1 copy-done.10
  66.0 1.1 copy-done.12
  67.1 9.8 %embed_tiles.1 = bf16[1536,256]{1,0:T(8,128)(2,1)} custom-call(bf16[16,384,616]{2,1,0:T(8,128)(2,1)S(1)} %copy-done.8, bf16[16,384,616]{2,1,0:T(8,128)(2,1)S(1)} %get-tuple-element.44.sib_ref, bf16[2,16,16,616]{3,2,1,0:T(8,128)(2,1)S(1)} %pad_maximum_fusion.refs_0_, bf16[2,16,16,616]{3,2,1,0:T(8,128)(2,1)S(1)} %pad_maximum_fusion.1.refs_1_, ...), custom_call_target="tpu_custom_call" | custom-call | flops 9663676416 | bytes 1000000 | tf_op jit(solution)/shard_map/embed_tiles/pallas_call | solution.py:209
  76.9 7.3 %all-to-all-start = ((bf16[32,48,256]{2,1,0:T(8,128)(2,1)}), bf16[32,48,256]{2,1,0:T(8,128)(2,1)S(1)}, u32[]{:S(2)}, u32[]{:S(2)}) async-start(bf16[32,48,256]{2,1,0:T(8,128)(2,1)} %bitcast.22), calls=%async_computation | async-start | bytes 1572864 | tf_op jit(solution)/shard_map/all_to_all | solution.py:415
  87.2 1.3 %copy.32 = bf16[16,2,16,1024]{3,2,0,1:T(8,128)(2,1)S(1)} copy(bf16[16,2,16,1024]{3,2,1,0:T(8,128)(2,1)} %bitcast.73) | data formatting | bytes 2097152 | tf_op jit(solution)/shard_map/reshape | solution.py:432
  88.6 8.9 %all-to-all-done = bf16[32,48,256]{2,1,0:T(8,128)(2,1)S(1)} async-done(((bf16[32,48,256]{2,1,0:T(8,128)(2,1)}), bf16[32,48,256]{2,1,0:T(8,128)(2,1)S(1)}, u32[]{:S(2)}, u32[]{:S(2)}) %all-to-all-start) | async-done | bytes 786464 | tf_op jit(solution)/shard_map/all_to_all | solution.py:415
  97.5 2.9 %attend_source.1 = bf16[128,640]{1,0:T(8,128)(2,1)S(1)} custom-call(bf16[16,2,48,256]{3,2,1,0:T(8,128)(2,1)S(1)} %bitcast.65, s32[1,768]{1,0:T(1,128)S(1)} %select_n.396.row_ref, f32[1,512]{1,0:T(1,128)S(1)} %broadcast_in_dim_reshape.6.bias_ref, f32[1,512]{1,0:T(1,128)S(1)} %broadcast_in_dim_reshape.7.gain_ref, bf16[512,1024]{1,0:T(8,128)(2,1)S(1)} %bitcast.64, ...), custom_call_target="tpu_custom_call" | custom-call | flops 1572864000 | bytes 3000000 | tf_op jit(solution)/shard_map/attend_source/pallas_call | solution.py:284
  100.4 18.6 %all_to_all.10.parts_ref = bf16[8,16,640]{2,1,0:T(8,128)(2,1)} all-to-all(bf16[8,16,640]{2,1,0:T(8,128)(2,1)S(1)} %bitcast.67), channel_id=1, replica_groups=mesh['lat'=32,'src'=8] {'src'}, dimensions={0} | all-to-all | bytes 327680 | tf_op jit(solution)/shard_map/all_to_all | solution.py:444
  119.0 2.1 %combine_sources.1 = f32[4,4,512]{2,1,0:T(4,128)} custom-call(bf16[8,16,640]{2,1,0:T(8,128)(2,1)} %all_to_all.10.parts_ref, bf16[512,512]{1,0:T(8,128)(2,1)} %weight_ref.1), custom_call_target="tpu_custom_call" | custom-call | flops 33554432 | bytes 800000 | tf_op jit(solution)/shard_map/combine_sources/pallas_call | solution.py:313
  (85 shorter events, 8.1 us)
Async XLA Ops:
  0.0 52.6 %copy-start.1 = (f32[4,256,128]{2,1,0:T(8,128)S(1)}, f32[4,256,128]{2,1,0:T(8,128)}, u32[]{:S(2)}) copy-start(f32[4,256,128]{2,1,0:T(8,128)} %constant.170.clone.center_ref) | copy-start | bytes 1572868
  0.0 49.2 %collective-permute-start.15 = (bf16[32,616,128]{2,1,0:T(8,128)(2,1)}, bf16[32,616,128]{2,1,0:T(8,128)(2,1)}, u32[]{:S(2)}, u32[]{:S(2)}) collective-permute-start(bf16[32,616,128]{2,1,0:T(8,128)(2,1)} %bitcast.71), channel_id=1, source_target_pairs={{0,8},{8,0},{16,24},{24,16},{32,40},{40,32},{48,56},{56,48},{64,72... | collective-permute-start | bytes 15138824 | tf_op jit(solution)/shard_map/ppermute | solution.py:375
  0.0 7.5 %collective-permute-start = (bf16[16,16,616]{2,1,0:T(8,128)(2,1)}, bf16[16,16,616]{2,1,0:T(8,128)(2,1)S(1)}, u32[]{:S(2)}, u32[]{:S(2)}) collective-permute-start(bf16[16,16,616]{2,1,0:T(8,128)(2,1)} %bitcast.78), channel_id=1, source_target_pairs={{0,16},{8,72},{16,32},{24,88},{32,48},{40,104},{48,0},{56,120},{64... | collective-permute-start | bytes 946184 | tf_op jit(solution)/shard_map/ppermute | solution.py:337
  1.6 7.3 %collective-permute-start.1 = (bf16[16,16,616]{2,1,0:T(8,128)(2,1)}, bf16[16,16,616]{2,1,0:T(8,128)(2,1)S(1)}, u32[]{:S(2)}, u32[]{:S(2)}) collective-permute-start(bf16[16,16,616]{2,1,0:T(8,128)(2,1)} %bitcast.79), channel_id=1, source_target_pairs={{0,48},{8,200},{16,0},{24,216},{32,16},{40,232},{48,32},{56,248},{... | collective-permute-start | bytes 946184 | tf_op jit(solution)/shard_map/ppermute | solution.py:337
  8.9 6.2 %collective-permute-start.7 = (bf16[32,256]{1,0:T(8,128)(2,1)}, bf16[32,256]{1,0:T(8,128)(2,1)S(1)}, u32[]{:S(2)}, u32[]{:S(2)}) collective-permute-start(bf16[32,256]{1,0:T(8,128)(2,1)} %tile_records.1), channel_id=1, source_target_pairs={{0,32},{8,136},{16,48},{24,152},{32,0},{40,168},{48,16},{56,184},{... | collective-permute-start | bytes 49160 | tf_op jit(solution)/shard_map/ppermute | solution.py:337
  12.8 5.4 %collective-permute-start.6 = (bf16[32,256]{1,0:T(8,128)(2,1)}, bf16[32,256]{1,0:T(8,128)(2,1)S(1)}, u32[]{:S(2)}, u32[]{:S(2)}) collective-permute-start(bf16[32,256]{1,0:T(8,128)(2,1)} %tile_records.1), channel_id=1, source_target_pairs={{0,48},{8,200},{16,0},{24,216},{32,16},{40,232},{48,32},{56,248},{... | collective-permute-start | bytes 49160 | tf_op jit(solution)/shard_map/ppermute | solution.py:337
  12.8 5.5 %collective-permute-start.5 = (bf16[32,256]{1,0:T(8,128)(2,1)}, bf16[32,256]{1,0:T(8,128)(2,1)S(1)}, u32[]{:S(2)}, u32[]{:S(2)}) collective-permute-start(bf16[32,256]{1,0:T(8,128)(2,1)} %tile_records.1), channel_id=1, source_target_pairs={{0,16},{8,72},{16,32},{24,88},{32,48},{40,104},{48,0},{56,120},{64... | collective-permute-start | bytes 49160 | tf_op jit(solution)/shard_map/ppermute | solution.py:337
  14.9 45.4 %copy-start.2 = (bf16[192,768]{1,0:T(8,128)(2,1)S(1)}, bf16[192,768]{1,0:T(8,128)(2,1)}, u32[]{:S(2)}) copy-start(bf16[192,768]{1,0:T(8,128)(2,1)} %constant.174.clone.own_cell_ref) | copy-start | bytes 884740
  14.9 45.3 %copy-start.3 = (bf16[64,768]{1,0:T(8,128)(2,1)S(1)}, bf16[64,768]{1,0:T(8,128)(2,1)}, u32[]{:S(2)}) copy-start(bf16[64,768]{1,0:T(8,128)(2,1)} %constant.173.clone.row_tile_ref) | copy-start | bytes 294916
  14.9 45.3 %copy-start.5 = (bf16[16,192]{1,0:T(8,128)(2,1)S(1)}, bf16[16,192]{1,0:T(8,128)(2,1)}, u32[]{:S(2)}) copy-start(bf16[16,192]{1,0:T(8,128)(2,1)} %constant.175.clone.tap_ref) | copy-start | bytes 18436
  14.9 45.3 %copy-start.6 = (s32[1,768]{1,0:T(1,128)S(1)}, s32[1,768]{1,0:T(1,128)}, u32[]{:S(2)}) copy-start(s32[1,768]{1,0:T(1,128)} %constant.183.token_ref) | copy-start | bytes 9220
  14.9 5.4 %collective-permute-start.3 = (bf16[8,16,616]{2,1,0:T(8,128)(2,1)S(1)}, bf16[8,16,616]{2,1,0:T(8,128)(2,1)S(1)}, u32[]{:S(2)}, u32[]{:S(2)}) collective-permute-start(bf16[8,16,616]{2,1,0:T(8,128)(2,1)S(1)} %slice.18), channel_id=1, source_target_pairs={{0,16},{8,72},{16,32},{24,88},{32,48},{40,104},{48,0},{56,120},{64... | collective-permute-start | bytes 473096 | tf_op jit(solution)/shard_map/ppermute | solution.py:337
  15.1 5.4 %collective-permute-start.4 = (bf16[8,16,616]{2,1,0:T(8,128)(2,1)S(1)}, bf16[8,16,616]{2,1,0:T(8,128)(2,1)S(1)}, u32[]{:S(2)}, u32[]{:S(2)}) collective-permute-start(bf16[8,16,616]{2,1,0:T(8,128)(2,1)S(1)} %slice.19), channel_id=1, source_target_pairs={{0,48},{8,200},{16,0},{24,216},{32,16},{40,232},{48,32},{56,248},{... | collective-permute-start | bytes 473096 | tf_op jit(solution)/shard_map/ppermute | solution.py:337
  18.2 1.5 %collective-permute-start.8 = (bf16[32,2,128]{2,1,0:T(2,128)(2,1)}, bf16[32,2,128]{2,1,0:T(2,128)(2,1)S(1)}, u32[]{:S(2)}, u32[]{:S(2)}) collective-permute-start(bf16[32,2,128]{2,1,0:T(2,128)(2,1)} %bitcast.69), channel_id=1, source_target_pairs={{0,8},{8,0},{16,24},{24,16},{32,40},{40,32},{48,56},{56,48},{64,72... | collective-permute-start | bytes 49160 | tf_op jit(solution)/shard_map/ppermute | solution.py:376
  18.3 26.5 %collective-permute-start.2 = (bf16[2,16,16,616]{3,2,1,0:T(8,128)(2,1)S(1)}, bf16[2,16,16,616]{3,2,1,0:T(8,128)(2,1)S(1)}, u32[]{:S(2)}, u32[]{:S(2)}) collective-permute-start(bf16[2,16,16,616]{3,2,1,0:T(8,128)(2,1)S(1)} %pad_maximum_fusion.refs_0_), channel_id=1, source_target_pairs={{0,64},{8,24},{16,80},{24,40},{32,96},{40,56},{48,112},{56,8},{64,... | collective-permute-start | bytes 1892360 | tf_op jit(solution)/shard_map/ppermute | solution.py:337
  20.5 10.1 %collective-permute-start.14 = (bf16[4,32,256]{2,1,0:T(8,128)(2,1)S(1)}, bf16[4,32,256]{2,1,0:T(8,128)(2,1)S(1)}, u32[]{:S(2)}, u32[]{:S(2)}) collective-permute-start(bf16[4,32,256]{2,1,0:T(8,128)(2,1)S(1)} %pad_maximum_fusion.3), channel_id=1, source_target_pairs={{0,128},{8,40},{16,144},{24,56},{32,160},{40,8},{48,176},{56,24},{... | collective-permute-start | bytes 196616 | tf_op jit(solution)/shard_map/ppermute | solution.py:337
  22.9 7.7 %collective-permute-start.13 = (bf16[4,32,256]{2,1,0:T(8,128)(2,1)S(1)}, bf16[4,32,256]{2,1,0:T(8,128)(2,1)S(1)}, u32[]{:S(2)}, u32[]{:S(2)}) collective-permute-start(bf16[4,32,256]{2,1,0:T(8,128)(2,1)S(1)} %pad_maximum_fusion.3), channel_id=1, source_target_pairs={{0,192},{8,56},{16,208},{24,8},{32,224},{40,24},{48,240},{56,40},{... | collective-permute-start | bytes 196616 | tf_op jit(solution)/shard_map/ppermute | solution.py:337
  24.0 7.9 %collective-permute-start.12 = (bf16[4,32,256]{2,1,0:T(8,128)(2,1)S(1)}, bf16[4,32,256]{2,1,0:T(8,128)(2,1)S(1)}, u32[]{:S(2)}, u32[]{:S(2)}) collective-permute-start(bf16[4,32,256]{2,1,0:T(8,128)(2,1)S(1)} %pad_maximum_fusion.3), channel_id=1, source_target_pairs={{0,64},{8,24},{16,80},{24,40},{32,96},{40,56},{48,112},{56,8},{64,... | collective-permute-start | bytes 196616 | tf_op jit(solution)/shard_map/ppermute | solution.py:337
  30.6 14.2 %collective-permute-start.11 = (bf16[2,16,16,616]{3,2,1,0:T(8,128)(2,1)S(1)}, bf16[2,16,16,616]{3,2,1,0:T(8,128)(2,1)S(1)}, u32[]{:S(2)}, u32[]{:S(2)}) collective-permute-start(bf16[2,16,16,616]{3,2,1,0:T(8,128)(2,1)S(1)} %pad_maximum_fusion.refs_0_), channel_id=1, source_target_pairs={{0,192},{8,56},{16,208},{24,8},{32,224},{40,24},{48,240},{56,40},{... | collective-permute-start | bytes 1892360 | tf_op jit(solution)/shard_map/ppermute | solution.py:337
  30.6 17.7 %collective-permute-start.9 = (bf16[2,16,16,616]{3,2,1,0:T(8,128)(2,1)S(1)}, bf16[2,16,16,616]{3,2,1,0:T(8,128)(2,1)}, u32[]{:S(2)}, u32[]{:S(2)}) collective-permute-start(bf16[2,16,16,616]{3,2,1,0:T(8,128)(2,1)S(1)} %pad_maximum_fusion.1.refs_1_), channel_id=1, source_target_pairs={{0,192},{8,56},{16,208},{24,8},{32,224},{40,24},{48,240},{56,40},{... | collective-permute-start | bytes 1892360 | tf_op jit(solution)/shard_map/ppermute | solution.py:337
  31.9 16.4 %collective-permute-start.10 = (bf16[2,16,16,616]{3,2,1,0:T(8,128)(2,1)S(1)}, bf16[2,16,16,616]{3,2,1,0:T(8,128)(2,1)S(1)}, u32[]{:S(2)}, u32[]{:S(2)}) collective-permute-start(bf16[2,16,16,616]{3,2,1,0:T(8,128)(2,1)S(1)} %pad_maximum_fusion.1.refs_1_), channel_id=1, source_target_pairs={{0,64},{8,24},{16,80},{24,40},{32,96},{40,56},{48,112},{56,8},{64,... | collective-permute-start | bytes 1892360 | tf_op jit(solution)/shard_map/ppermute | solution.py:337
  41.7 3.1 %copy-start.7 = (bf16[16,384,616]{2,1,0:T(8,128)(2,1)}, bf16[16,384,616]{2,1,0:T(8,128)(2,1)S(1)}, u32[]{:S(2)}) copy-start(bf16[16,384,616]{2,1,0:T(8,128)(2,1)S(1)} %get-tuple-element.40.own_ref) | copy-start | bytes 22708228
  49.2 12.4 %collective-permute-start.17 = (bf16[2,16,16,616]{3,2,1,0:T(8,128)(2,1)S(1)}, bf16[2,16,16,616]{3,2,1,0:T(8,128)(2,1)}, u32[]{:S(2)}, u32[]{:S(2)}) collective-permute-start(bf16[2,16,16,616]{3,2,1,0:T(8,128)(2,1)S(1)} %collective-permute-done.2.refs_2_), channel_id=1, source_target_pairs={{0,64},{8,24},{16,80},{24,40},{32,96},{40,56},{48,112},{56,8},{64,... | collective-permute-start | bytes 1892360 | tf_op jit(solution)/shard_map/ppermute | solution.py:337
  49.2 12.4 %collective-permute-start.18 = (bf16[2,16,16,616]{3,2,1,0:T(8,128)(2,1)}, bf16[2,16,16,616]{3,2,1,0:T(8,128)(2,1)}, u32[]{:S(2)}, u32[]{:S(2)}) collective-permute-start(bf16[2,16,16,616]{3,2,1,0:T(8,128)(2,1)} %collective-permute-done.9.refs_5_), channel_id=1, source_target_pairs={{0,192},{8,56},{16,208},{24,8},{32,224},{40,24},{48,240},{56,40},{... | collective-permute-start | bytes 1892360 | tf_op jit(solution)/shard_map/ppermute | solution.py:337
  52.5 7.8 %collective-permute-start.16 = (bf16[4,4,32,256]{3,2,1,0:T(8,128)(2,1)S(1)}, bf16[4,4,32,256]{3,2,1,0:T(8,128)(2,1)S(1)}, u32[]{:S(2)}, u32[]{:S(2)}) collective-permute-start(bf16[4,4,32,256]{3,2,1,0:T(8,128)(2,1)S(1)} %pad_maximum_fusion.2), channel_id=1, source_target_pairs={{0,8},{8,0},{16,24},{24,16},{32,40},{40,32},{48,56},{56,48},{64,72... | collective-permute-start | bytes 786440 | tf_op jit(solution)/shard_map/ppermute | solution.py:394
  61.7 3.2 %copy-start.8 = (bf16[16,384,616]{2,1,0:T(8,128)(2,1)S(1)}, bf16[16,384,616]{2,1,0:T(8,128)(2,1)}, u32[]{:S(2)}) copy-start(bf16[16,384,616]{2,1,0:T(8,128)(2,1)} %copy-done.7) | copy-start | bytes 22708228
  64.9 1.1 copy-start.10
  67.1 17.8 %copy-start.16 = (bf16[32,32,1]{1,0,2:T(8,128)(2,1)S(1)}, bf16[32,32,1]{1,0,2:T(8,128)(2,1)}, u32[]{:S(2)}) copy-start(bf16[32,32,1]{1,0,2:T(8,128)(2,1)} %constant.286) | copy-start | bytes 6148
  67.1 19.1 %copy-start.15 = (f32[1,512]{1,0:T(1,128)S(1)}, f32[1,512]{1,0:T(1,128)}, u32[]{:S(2)}) copy-start(f32[1,512]{1,0:T(1,128)} %param.22) | copy-start | bytes 6148
  67.1 20.0 %copy-start.14 = (f32[512]{0:T(512)S(1)}, f32[512]{0:T(512)}, u32[]{:S(2)}) copy-start(f32[512]{0:T(512)} %param.23) | copy-start | bytes 6148
  67.1 30.4 %copy-start.13 = (f32[4,512]{1,0:T(4,128)S(1)}, f32[4,512]{1,0:T(4,128)}, u32[]{:S(2)}) copy-start(f32[4,512]{1,0:T(4,128)} %latent_ref.1) | copy-start | bytes 24580
  76.9 20.7 %all-to-all-start = ((bf16[32,48,256]{2,1,0:T(8,128)(2,1)}), bf16[32,48,256]{2,1,0:T(8,128)(2,1)S(1)}, u32[]{:S(2)}, u32[]{:S(2)}) async-start(bf16[32,48,256]{2,1,0:T(8,128)(2,1)} %bitcast.22), calls=%async_computation | async-start | bytes 1572864 | tf_op jit(solution)/shard_map/all_to_all | solution.py:415
  (5 other events, 4.6 us)

commit v5 on v3

--- a/solution.py
+++ b/solution.py
@@ -31,6 +31,7 @@
 NT = (((1,), (1,)), ((), ()))
 KERNEL_VMEM = 24 * 2**20
 RECORD = 256
+STEP = 16
 SMALL = pl.CostEstimate(flops=1000000, bytes_accessed=10000, transcendentals=0)
 
 
@@ -137,22 +138,24 @@
 
     def step(tiles_ref):
         i = pl.program_id(0)
-        blocks = []
-        for pair in range(2):
-            first, second = 4 * i + 2 * pair, 4 * i + 2 * pair + 1
-            left = weights_at(pos_ref[first].astype(F32), center_ref, 0).reshape(TAPS, 16, FP)
-            right = weights_at(pos_ref[second].astype(F32), center_ref, 2).reshape(TAPS, 16, FP)
-            left = jnp.concatenate([left, gap], 1).reshape(TAPS * PAIR, FP)
-            right = jnp.concatenate([gap, right], 1).reshape(TAPS * PAIR, FP)
-            table = jnp.concatenate([left, right], 1).astype(BF)
-            data = jnp.concatenate([tiles_ref[2 * pair], tiles_ref[2 * pair + 1]], 1)
-            total = lax.dot_general(table, data, NT, preferred_element_type=F32)
-            blocks.append(total.reshape(TAPS, PAIR, channels))
-        base = pl.multiple_of(i * 2 * PAIR, 2 * PAIR)
-        out_ref[:, pl.ds(base, 2 * PAIR), :] = jnp.concatenate(blocks, 1).astype(BF)
+        for quad in range(STEP // 4):
+            blocks = []
+            for pair in range(2):
+                place = 4 * quad + 2 * pair
+                first, second = STEP * i + place, STEP * i + place + 1
+                left = weights_at(pos_ref[first].astype(F32), center_ref, 0).reshape(TAPS, 16, FP)
+                right = weights_at(pos_ref[second].astype(F32), center_ref, 2).reshape(TAPS, 16, FP)
+                left = jnp.concatenate([left, gap], 1).reshape(TAPS * PAIR, FP)
+                right = jnp.concatenate([gap, right], 1).reshape(TAPS * PAIR, FP)
+                table = jnp.concatenate([left, right], 1).astype(BF)
+                data = jnp.concatenate([tiles_ref[place], tiles_ref[place + 1]], 1)
+                total = lax.dot_general(table, data, NT, preferred_element_type=F32)
+                blocks.append(total.reshape(TAPS, PAIR, channels))
+            base = pl.multiple_of((STEP // 4 * i + quad) * 2 * PAIR, 2 * PAIR)
+            out_ref[:, pl.ds(base, 2 * PAIR), :] = jnp.concatenate(blocks, 1).astype(BF)
 
     pltpu.emit_pipeline(
-        step, grid=(TILES // 4,), in_specs=[pl.BlockSpec((4, channels, FP), lambda i: (i, 0, 0))]
+        step, grid=(TILES // STEP,), in_specs=[pl.BlockSpec((STEP, channels, FP), lambda i: (i, 0, 0))]
     )(swath_ref)
 
 
@@ -192,7 +195,7 @@
         spread[pl.ds(base, part), :] = jnp.where(here == row_ref[...], 1.0, 0.0).astype(BF)
         return carry
 
-    lax.fori_loop(0, TAPS, tap, 0)
+    lax.fori_loop(0, TAPS, tap, 0, unroll=8)
     columns = lax.broadcasted_iota(jnp.int32, (width, width), 0)
     order = jnp.where(columns == column_ref[...], 1.0, 0.0).astype(BF)
     tokens = lax.dot_general(total[...].astype(BF), order, NT, preferred_element_type=F32).astype(BF)
@@ -377,7 +380,7 @@
     up, down, record = lax.optimization_barrier((up, down, record))
     far = [send(up[:half], 1, False), send(down[half:], -1, False)]
     others = [send(record, -offset, False) for offset in OFFSETS[1:]]
-    *far, record = lax.optimization_barrier((*far, jnp.stack([record] + others, 0)))
+    *far, record, sib_pos = lax.optimization_barrier((*far, jnp.stack([record] + others, 0), sib_pos))
     low = jnp.stack([shard, up], 0)
     high = jnp.stack([down, jnp.concatenate(far, 0)], 0)
     above_low, below_high = send(low, 1, True), send(high, -1, True)

time: 117 us -> 109 us (0.932)
  Pallas kernels: 35.3 us -> 27.5 us
  starting transfers between devices: 27.9 us -> 29.5 us
  waiting for transfers between devices: 27.2 us -> 25.7 us
    pallas_call x2, Pallas kernels: 14.1 us -> 9.21 us  [gridded(): pl.pallas_call(grid_kernel, in_specs=[pl.BlockSpec(memory_space=pl.ANY),...]
    pallas_call x1, Pallas kernels: 12.2 us -> 9.35 us  [embed(): pl.pallas_call(embed_kernel, in_specs=[vmem] * (len(large) + 3), out_spec...]
    all_to_all x1, starting transfers between devices: 5.43 us -> 7.03 us  [body(): lax.all_to_all(outgoing, 'lat', split_axis=0, concat_axis=0, tiled=True)]
  transfers between devices with their start and end apart: 20 -> 20, of which waited for: 8 -> 9; matrix products, arithmetic and copies ran while one was open for 5% -> 5% of each run, Pallas kernels for 16% -> 12%
where the time goes in v5:
time: 109 us
  starting transfers between devices  29.5 us (27%)
  Pallas kernels  27.5 us (25%)
  waiting for transfers between devices  25.7 us (24%)
  blocking collectives  17.4 us (16%)
  local copies, waits for them, and re-layouts  4.86 us (4%)
  other arithmetic  2.91 us (3%)
    ppermute x16, starting transfers between devices, send(): return lax.ppermute(array, 'lat', shift(offset, second))  22.3 us
    all_to_all x1, blocking collectives, body(): lax.all_to_all(parts.reshape(sources, -1, width + FP), 'src', split_axis=...  17.4 us
    ppermute x16, waiting for transfers between devices, send(): return lax.ppermute(array, 'lat', shift(offset, second))  15.6 us
    all_to_all x1, waiting for transfers between devices, body(): lax.all_to_all(outgoing, 'lat', split_axis=0, concat_axis=0, tiled=True)  9.55 us
    pallas_call x1, Pallas kernels, embed(): pl.pallas_call(embed_kernel, in_specs=[vmem] * (len(large) + 3), out_spec...  9.35 us
    pallas_call x2, Pallas kernels, gridded(): pl.pallas_call(grid_kernel, in_specs=[pl.BlockSpec(memory_space=pl.ANY),...  9.21 us
    all_to_all x1, starting transfers between devices, body(): lax.all_to_all(outgoing, 'lat', split_axis=0, concat_axis=0, tiled=True)  7.03 us
    pallas_call x1, Pallas kernels, attend(): pl.pallas_call(attend_kernel, out_shape=jax.ShapeDtypeStruct((PATCHES * L...  2.89 us
  transfers between devices with their start and end apart: 20, of which 9 were waited for; matrix products, arithmetic and copies ran while one was open for 5% of the time, Pallas kernels for 12%

profile of v5, /device:TPU:2, one launch (start us, length us, event | category | flops | bytes accessed | tf_op | source)
XLA Modules:
  0.0 108.6 jit_solution(9097756988669159617)
XLA Ops:
  0.0 1.5 %collective-permute-start = (bf16[16,16,616]{2,1,0:T(8,128)(2,1)}, bf16[16,16,616]{2,1,0:T(8,128)(2,1)S(1)}, u32[]{:S(2)}, u32[]{:S(2)}) collective-permute-start(bf16[16,16,616]{2,1,0:T(8,128)(2,1)} %bitcast.78), channel_id=1, source_target_pairs={{0,16},{8,72},{16,32},{24,88},{32,48},{40,104},{48,0},{56,120},{64... | collective-permute-start | bytes 946184 | tf_op jit(solution)/shard_map/ppermute | solution.py:339
  1.5 0.8 collective-permute-start.1
  2.3 2.6 %tile_records.1 = bf16[32,256]{1,0:T(8,128)(2,1)} custom-call(s32[32]{0:T(128)} %bitcast.93, s32[32]{0:T(128)} %bitcast.94, bf16[32,2,128]{2,1,0:T(2,128)(2,1)} %bitcast.68, f32[2,192,128]{2,1,0:T(8,128)} %constant.170.clone.center_ref), custom_call_target="tpu_custom_call" | custom-call | flops 1000000 | bytes 10000 | tf_op jit(solution)/shard_map/tile_records/pallas_call | solution.py:77
  4.9 2.7 %collective-permute-done = bf16[16,16,616]{2,1,0:T(8,128)(2,1)S(1)} collective-permute-done((bf16[16,16,616]{2,1,0:T(8,128)(2,1)}, bf16[16,16,616]{2,1,0:T(8,128)(2,1)S(1)}, u32[]{:S(2)}, u32[]{:S(2)}) %collective-permute-start) | collective-permute-done | bytes 315424 | tf_op jit(solution)/shard_map/ppermute | solution.py:339
  7.5 1.2 %collective-permute-done.1 = bf16[16,16,616]{2,1,0:T(8,128)(2,1)S(1)} collective-permute-done((bf16[16,16,616]{2,1,0:T(8,128)(2,1)}, bf16[16,16,616]{2,1,0:T(8,128)(2,1)S(1)}, u32[]{:S(2)}, u32[]{:S(2)}) %collective-permute-start.1) | collective-permute-done | bytes 315424 | tf_op jit(solution)/shard_map/ppermute | solution.py:339
  8.8 1.4 %collective-permute-start.5 = (bf16[32,256]{1,0:T(8,128)(2,1)}, bf16[32,256]{1,0:T(8,128)(2,1)S(1)}, u32[]{:S(2)}, u32[]{:S(2)}) collective-permute-start(bf16[32,256]{1,0:T(8,128)(2,1)} %tile_records.1), channel_id=1, source_target_pairs={{0,16},{8,72},{16,32},{24,88},{32,48},{40,104},{48,0},{56,120},{64... | collective-permute-start | bytes 49160 | tf_op jit(solution)/shard_map/ppermute | solution.py:339
  10.8 4.1 %collective-permute-start.7 = (bf16[32,256]{1,0:T(8,128)(2,1)}, bf16[32,256]{1,0:T(8,128)(2,1)S(1)}, u32[]{:S(2)}, u32[]{:S(2)}) collective-permute-start(bf16[32,256]{1,0:T(8,128)(2,1)} %tile_records.1), channel_id=1, source_target_pairs={{0,32},{8,136},{16,48},{24,152},{32,0},{40,168},{48,16},{56,184},{... | collective-permute-start | bytes 49160 | tf_op jit(solution)/shard_map/ppermute | solution.py:339
  14.9 0.7 collective-permute-start.3
  15.6 1.5 %collective-permute-start.4 = (bf16[8,16,616]{2,1,0:T(8,128)(2,1)S(1)}, bf16[8,16,616]{2,1,0:T(8,128)(2,1)S(1)}, u32[]{:S(2)}, u32[]{:S(2)}) collective-permute-start(bf16[8,16,616]{2,1,0:T(8,128)(2,1)S(1)} %slice.19), channel_id=1, source_target_pairs={{0,48},{8,200},{16,0},{24,216},{32,16},{40,232},{48,32},{56,248},{... | collective-permute-start | bytes 473096 | tf_op jit(solution)/shard_map/ppermute | solution.py:339
  17.1 1.1 pad_maximum_fusion.refs_0_
  18.4 0.7 pad_maximum_fusion.3
  20.3 0.7 collective-permute-done.4
  21.2 1.6 %collective-permute-start.9 = (bf16[2,16,16,616]{3,2,1,0:T(8,128)(2,1)S(1)}, bf16[2,16,16,616]{3,2,1,0:T(8,128)(2,1)}, u32[]{:S(2)}, u32[]{:S(2)}) collective-permute-start(bf16[2,16,16,616]{3,2,1,0:T(8,128)(2,1)S(1)} %pad_maximum_fusion.1.refs_1_), channel_id=1, source_target_pairs={{0,192},{8,56},{16,208},{24,8},{32,224},{40,24},{48,240},{56,40},{... | collective-permute-start | bytes 1892360 | tf_op jit(solution)/shard_map/ppermute | solution.py:339
  23.3 2.8 %collective-permute-start.11 = (bf16[4,32,256]{2,1,0:T(8,128)(2,1)S(1)}, bf16[4,32,256]{2,1,0:T(8,128)(2,1)S(1)}, u32[]{:S(2)}, u32[]{:S(2)}) collective-permute-start(bf16[4,32,256]{2,1,0:T(8,128)(2,1)S(1)} %pad_maximum_fusion.3), channel_id=1, source_target_pairs={{0,192},{8,56},{16,208},{24,8},{32,224},{40,24},{48,240},{56,40},{... | collective-permute-start | bytes 196616 | tf_op jit(solution)/shard_map/ppermute | solution.py:339
  26.0 4.8 %collective-permute-done.10 = bf16[4,32,256]{2,1,0:T(8,128)(2,1)S(1)} collective-permute-done((bf16[4,32,256]{2,1,0:T(8,128)(2,1)S(1)}, bf16[4,32,256]{2,1,0:T(8,128)(2,1)S(1)}, u32[]{:S(2)}, u32[]{:S(2)}) %collective-permute-start.10) | collective-permute-done | bytes 65568 | tf_op jit(solution)/shard_map/ppermute | solution.py:339
  31.1 1.4 %collective-permute-done.11 = bf16[4,32,256]{2,1,0:T(8,128)(2,1)S(1)} collective-permute-done((bf16[4,32,256]{2,1,0:T(8,128)(2,1)S(1)}, bf16[4,32,256]{2,1,0:T(8,128)(2,1)S(1)}, u32[]{:S(2)}, u32[]{:S(2)}) %collective-permute-start.11) | collective-permute-done | bytes 65568 | tf_op jit(solution)/shard_map/ppermute | solution.py:339
  32.5 4.1 %collective-permute-done.12 = bf16[4,32,256]{2,1,0:T(8,128)(2,1)S(1)} collective-permute-done((bf16[4,32,256]{2,1,0:T(8,128)(2,1)S(1)}, bf16[4,32,256]{2,1,0:T(8,128)(2,1)S(1)}, u32[]{:S(2)}, u32[]{:S(2)}) %collective-permute-start.12) | collective-permute-done | bytes 65568 | tf_op jit(solution)/shard_map/ppermute | solution.py:339
  36.8 3.2 %collective-permute-start.16 = (bf16[2,16,16,616]{3,2,1,0:T(8,128)(2,1)S(1)}, bf16[2,16,16,616]{3,2,1,0:T(8,128)(2,1)}, u32[]{:S(2)}, u32[]{:S(2)}) collective-permute-start(bf16[2,16,16,616]{3,2,1,0:T(8,128)(2,1)S(1)} %pad_maximum_fusion.refs_0_), channel_id=1, source_target_pairs={{0,192},{8,56},{16,208},{24,8},{32,224},{40,24},{48,240},{56,40},{... | collective-permute-start | bytes 1892360 | tf_op jit(solution)/shard_map/ppermute | solution.py:339
  40.0 3.2 %collective-permute-start.18 = (bf16[2,16,16,616]{3,2,1,0:T(8,128)(2,1)}, bf16[2,16,16,616]{3,2,1,0:T(8,128)(2,1)}, u32[]{:S(2)}, u32[]{:S(2)}) collective-permute-start(bf16[2,16,16,616]{3,2,1,0:T(8,128)(2,1)} %collective-permute-done.9.refs_5_), channel_id=1, source_target_pairs={{0,192},{8,56},{16,208},{24,8},{32,224},{40,24},{48,240},{56,40},{... | collective-permute-start | bytes 1892360 | tf_op jit(solution)/shard_map/ppermute | solution.py:339
  43.5 1.0 copy-done
  44.5 0.7 copy-done.4
  45.2 4.6 %grid_tiles.2.own_ref = bf16[16,384,616]{2,1,0:T(8,128)(2,1)S(1)} custom-call(bf16[32,616,128]{2,1,0:T(8,128)(2,1)} %bitcast.72, bf16[32,2,128]{2,1,0:T(2,128)(2,1)S(1)} %bitcast.70, f32[4,256,128]{2,1,0:T(8,128)S(1)} %copy-done), custom_call_target="tpu_custom_call" | custom-call | flops 1000000 | bytes 10000 | tf_op jit(solution)/shard_map/grid_tiles/pallas_call | solution.py:166
  49.9 4.6 %grid_tiles.3.sib_ref = bf16[16,384,616]{2,1,0:T(8,128)(2,1)S(1)} custom-call(bf16[32,616,128]{2,1,0:T(8,128)(2,1)} %collective-permute-done.13.swath_ref, bf16[32,2,128]{2,1,0:T(2,128)(2,1)S(1)} %collective-permute-done.8.pos_ref, f32[4,256,128]{2,1,0:T(8,128)S(1)} %copy-done.1), custom_call_target="tpu_custom_call" | custom-call | flops 1000000 | bytes 10000 | tf_op jit(solution)/shard_map/grid_tiles/pallas_call | solution.py:166
  54.5 1.3 %inverse_density.1 = (f32[16,768]{1,0:T(8,128)S(1)}, s32[1,768]{1,0:T(1,128)S(1)}) custom-call(s32[1]{0:T(128)} %bitcast.19.core_ref, bf16[512,256]{1,0:T(8,128)(2,1)S(1)} %bitcast.63, bf16[512,256]{1,0:T(8,128)(2,1)S(1)} %bitcast.66, s32[1,768]{1,0:T(1,128)S(1)} %copy-done.6, bf16[64,768]{1,0:T(8,128)(2,1)S(1)} %copy-done.3, ...), custom_call_target="tpu_custom_call" | custom-call | flops 1000000 | bytes 10000 | tf_op jit(solution)/shard_map/inverse_density/pallas_call | solution.py:125
  56.0 9.3 %embed_tiles.1 = bf16[1536,256]{1,0:T(8,128)(2,1)} custom-call(bf16[16,384,616]{2,1,0:T(8,128)(2,1)S(1)} %grid_tiles.2.own_ref, bf16[16,384,616]{2,1,0:T(8,128)(2,1)S(1)} %grid_tiles.3.sib_ref, bf16[2,16,16,616]{3,2,1,0:T(8,128)(2,1)S(1)} %pad_maximum_fusion.refs_0_, bf16[2,16,16,616]{3,2,1,0:T(8,128)(2,1)S(1)} %pad_maximum_fusion.1.refs_1_, ...), custom_call_target="tpu_custom_call" | custom-call | flops 9663676416 | bytes 1000000 | tf_op jit(solution)/shard_map/embed_tiles/pallas_call | solution.py:211
  65.9 7.0 %all-to-all-start = ((bf16[32,48,256]{2,1,0:T(8,128)(2,1)}), bf16[32,48,256]{2,1,0:T(8,128)(2,1)S(1)}, u32[]{:S(2)}, u32[]{:S(2)}) async-start(bf16[32,48,256]{2,1,0:T(8,128)(2,1)} %bitcast.22), calls=%async_computation | async-start | bytes 1572864 | tf_op jit(solution)/shard_map/all_to_all | solution.py:415
  73.4 1.3 %copy.32 = bf16[16,2,16,1024]{3,2,0,1:T(8,128)(2,1)S(1)} copy(bf16[16,2,16,1024]{3,2,1,0:T(8,128)(2,1)} %bitcast.73) | data formatting | bytes 2097152 | tf_op jit(solution)/shard_map/reshape | solution.py:432
  75.6 0.7 reduce.7
  76.7 9.5 %all-to-all-done = bf16[32,48,256]{2,1,0:T(8,128)(2,1)S(1)} async-done(((bf16[32,48,256]{2,1,0:T(8,128)(2,1)}), bf16[32,48,256]{2,1,0:T(8,128)(2,1)S(1)}, u32[]{:S(2)}, u32[]{:S(2)}) %all-to-all-start) | async-done | bytes 786464 | tf_op jit(solution)/shard_map/all_to_all | solution.py:415
  86.2 2.9 %attend_source.1 = bf16[128,640]{1,0:T(8,128)(2,1)S(1)} custom-call(bf16[16,2,48,256]{3,2,1,0:T(8,128)(2,1)S(1)} %bitcast.65, s32[1,768]{1,0:T(1,128)S(1)} %select_n.396.row_ref, f32[1,512]{1,0:T(1,128)S(1)} %broadcast_in_dim_reshape.6.bias_ref, f32[1,512]{1,0:T(1,128)S(1)} %broadcast_in_dim_reshape.7.gain_ref, bf16[512,1024]{1,0:T(8,128)(2,1)S(1)} %bitcast.64, ...), custom_call_target="tpu_custom_call" | custom-call | flops 1572864000 | bytes 3000000 | tf_op jit(solution)/shard_map/attend_source/pallas_call | solution.py:286
  89.1 17.4 %all_to_all.10.parts_ref = bf16[8,16,640]{2,1,0:T(8,128)(2,1)} all-to-all(bf16[8,16,640]{2,1,0:T(8,128)(2,1)S(1)} %bitcast.67), channel_id=1, replica_groups=mesh['lat'=32,'src'=8] {'src'}, dimensions={0} | all-to-all | bytes 327680 | tf_op jit(solution)/shard_map/all_to_all | solution.py:444
  106.5 2.1 %combine_sources.1 = f32[4,4,512]{2,1,0:T(4,128)} custom-call(bf16[8,16,640]{2,1,0:T(8,128)(2,1)} %all_to_all.10.parts_ref, bf16[512,512]{1,0:T(8,128)(2,1)} %weight_ref.1), custom_call_target="tpu_custom_call" | custom-call | flops 33554432 | bytes 800000 | tf_op jit(solution)/shard_map/combine_sources/pallas_call | solution.py:315
  (72 shorter events, 5.4 us)
Async XLA Ops:
  0.0 36.7 %collective-permute-start.13 = (bf16[32,616,128]{2,1,0:T(8,128)(2,1)}, bf16[32,616,128]{2,1,0:T(8,128)(2,1)}, u32[]{:S(2)}, u32[]{:S(2)}) collective-permute-start(bf16[32,616,128]{2,1,0:T(8,128)(2,1)} %bitcast.71), channel_id=1, source_target_pairs={{0,8},{8,0},{16,24},{24,16},{32,40},{40,32},{48,56},{56,48},{64,72... | collective-permute-start | bytes 15138824 | tf_op jit(solution)/shard_map/ppermute | solution.py:377
  0.0 7.5 %collective-permute-start = (bf16[16,16,616]{2,1,0:T(8,128)(2,1)}, bf16[16,16,616]{2,1,0:T(8,128)(2,1)S(1)}, u32[]{:S(2)}, u32[]{:S(2)}) collective-permute-start(bf16[16,16,616]{2,1,0:T(8,128)(2,1)} %bitcast.78), channel_id=1, source_target_pairs={{0,16},{8,72},{16,32},{24,88},{32,48},{40,104},{48,0},{56,120},{64... | collective-permute-start | bytes 946184 | tf_op jit(solution)/shard_map/ppermute | solution.py:339
  1.5 7.3 %collective-permute-start.1 = (bf16[16,16,616]{2,1,0:T(8,128)(2,1)}, bf16[16,16,616]{2,1,0:T(8,128)(2,1)S(1)}, u32[]{:S(2)}, u32[]{:S(2)}) collective-permute-start(bf16[16,16,616]{2,1,0:T(8,128)(2,1)} %bitcast.79), channel_id=1, source_target_pairs={{0,48},{8,200},{16,0},{24,216},{32,16},{40,232},{48,32},{56,248},{... | collective-permute-start | bytes 946184 | tf_op jit(solution)/shard_map/ppermute | solution.py:339
  8.8 6.8 %collective-permute-start.5 = (bf16[32,256]{1,0:T(8,128)(2,1)}, bf16[32,256]{1,0:T(8,128)(2,1)S(1)}, u32[]{:S(2)}, u32[]{:S(2)}) collective-permute-start(bf16[32,256]{1,0:T(8,128)(2,1)} %tile_records.1), channel_id=1, source_target_pairs={{0,16},{8,72},{16,32},{24,88},{32,48},{40,104},{48,0},{56,120},{64... | collective-permute-start | bytes 49160 | tf_op jit(solution)/shard_map/ppermute | solution.py:339
  10.2 8.0 %collective-permute-start.6 = (bf16[32,256]{1,0:T(8,128)(2,1)}, bf16[32,256]{1,0:T(8,128)(2,1)S(1)}, u32[]{:S(2)}, u32[]{:S(2)}) collective-permute-start(bf16[32,256]{1,0:T(8,128)(2,1)} %tile_records.1), channel_id=1, source_target_pairs={{0,48},{8,200},{16,0},{24,216},{32,16},{40,232},{48,32},{56,248},{... | collective-permute-start | bytes 49160 | tf_op jit(solution)/shard_map/ppermute | solution.py:339
  10.8 7.5 %collective-permute-start.7 = (bf16[32,256]{1,0:T(8,128)(2,1)}, bf16[32,256]{1,0:T(8,128)(2,1)S(1)}, u32[]{:S(2)}, u32[]{:S(2)}) collective-permute-start(bf16[32,256]{1,0:T(8,128)(2,1)} %tile_records.1), channel_id=1, source_target_pairs={{0,32},{8,136},{16,48},{24,152},{32,0},{40,168},{48,16},{56,184},{... | collective-permute-start | bytes 49160 | tf_op jit(solution)/shard_map/ppermute | solution.py:339
  14.9 5.4 %collective-permute-start.3 = (bf16[8,16,616]{2,1,0:T(8,128)(2,1)S(1)}, bf16[8,16,616]{2,1,0:T(8,128)(2,1)S(1)}, u32[]{:S(2)}, u32[]{:S(2)}) collective-permute-start(bf16[8,16,616]{2,1,0:T(8,128)(2,1)S(1)} %slice.18), channel_id=1, source_target_pairs={{0,16},{8,72},{16,32},{24,88},{32,48},{40,104},{48,0},{56,120},{64... | collective-permute-start | bytes 473096 | tf_op jit(solution)/shard_map/ppermute | solution.py:339
  15.6 5.4 %collective-permute-start.4 = (bf16[8,16,616]{2,1,0:T(8,128)(2,1)S(1)}, bf16[8,16,616]{2,1,0:T(8,128)(2,1)S(1)}, u32[]{:S(2)}, u32[]{:S(2)}) collective-permute-start(bf16[8,16,616]{2,1,0:T(8,128)(2,1)S(1)} %slice.19), channel_id=1, source_target_pairs={{0,48},{8,200},{16,0},{24,216},{32,16},{40,232},{48,32},{56,248},{... | collective-permute-start | bytes 473096 | tf_op jit(solution)/shard_map/ppermute | solution.py:339
  18.2 1.5 %collective-permute-start.8 = (bf16[32,2,128]{2,1,0:T(2,128)(2,1)}, bf16[32,2,128]{2,1,0:T(2,128)(2,1)S(1)}, u32[]{:S(2)}, u32[]{:S(2)}) collective-permute-start(bf16[32,2,128]{2,1,0:T(2,128)(2,1)} %bitcast.69), channel_id=1, source_target_pairs={{0,8},{8,0},{16,24},{24,16},{32,40},{40,32},{48,56},{56,48},{64,72... | collective-permute-start | bytes 49160 | tf_op jit(solution)/shard_map/ppermute | solution.py:378
  18.3 18.4 %collective-permute-start.2 = (bf16[2,16,16,616]{3,2,1,0:T(8,128)(2,1)S(1)}, bf16[2,16,16,616]{3,2,1,0:T(8,128)(2,1)S(1)}, u32[]{:S(2)}, u32[]{:S(2)}) collective-permute-start(bf16[2,16,16,616]{3,2,1,0:T(8,128)(2,1)S(1)} %pad_maximum_fusion.refs_0_), channel_id=1, source_target_pairs={{0,64},{8,24},{16,80},{24,40},{32,96},{40,56},{48,112},{56,8},{64,... | collective-permute-start | bytes 1892360 | tf_op jit(solution)/shard_map/ppermute | solution.py:339
  19.1 30.7 %copy-start.1 = (f32[4,256,128]{2,1,0:T(8,128)S(1)}, f32[4,256,128]{2,1,0:T(8,128)}, u32[]{:S(2)}) copy-start(f32[4,256,128]{2,1,0:T(8,128)} %constant.169.clone.center_ref) | copy-start | bytes 1572868
  21.2 15.5 %collective-permute-start.9 = (bf16[2,16,16,616]{3,2,1,0:T(8,128)(2,1)S(1)}, bf16[2,16,16,616]{3,2,1,0:T(8,128)(2,1)}, u32[]{:S(2)}, u32[]{:S(2)}) collective-permute-start(bf16[2,16,16,616]{3,2,1,0:T(8,128)(2,1)S(1)} %pad_maximum_fusion.1.refs_1_), channel_id=1, source_target_pairs={{0,192},{8,56},{16,208},{24,8},{32,224},{40,24},{48,240},{56,40},{... | collective-permute-start | bytes 1892360 | tf_op jit(solution)/shard_map/ppermute | solution.py:339
  22.8 8.1 %collective-permute-start.10 = (bf16[4,32,256]{2,1,0:T(8,128)(2,1)S(1)}, bf16[4,32,256]{2,1,0:T(8,128)(2,1)S(1)}, u32[]{:S(2)}, u32[]{:S(2)}) collective-permute-start(bf16[4,32,256]{2,1,0:T(8,128)(2,1)S(1)} %pad_maximum_fusion.3), channel_id=1, source_target_pairs={{0,64},{8,24},{16,80},{24,40},{32,96},{40,56},{48,112},{56,8},{64,... | collective-permute-start | bytes 196616 | tf_op jit(solution)/shard_map/ppermute | solution.py:339
  23.3 9.3 %collective-permute-start.11 = (bf16[4,32,256]{2,1,0:T(8,128)(2,1)S(1)}, bf16[4,32,256]{2,1,0:T(8,128)(2,1)S(1)}, u32[]{:S(2)}, u32[]{:S(2)}) collective-permute-start(bf16[4,32,256]{2,1,0:T(8,128)(2,1)S(1)} %pad_maximum_fusion.3), channel_id=1, source_target_pairs={{0,192},{8,56},{16,208},{24,8},{32,224},{40,24},{48,240},{56,40},{... | collective-permute-start | bytes 196616 | tf_op jit(solution)/shard_map/ppermute | solution.py:339
  30.9 5.8 %collective-permute-start.12 = (bf16[4,32,256]{2,1,0:T(8,128)(2,1)S(1)}, bf16[4,32,256]{2,1,0:T(8,128)(2,1)S(1)}, u32[]{:S(2)}, u32[]{:S(2)}) collective-permute-start(bf16[4,32,256]{2,1,0:T(8,128)(2,1)S(1)} %pad_maximum_fusion.3), channel_id=1, source_target_pairs={{0,128},{8,40},{16,144},{24,56},{32,160},{40,8},{48,176},{56,24},{... | collective-permute-start | bytes 196616 | tf_op jit(solution)/shard_map/ppermute | solution.py:339
  36.7 19.2 %collective-permute-start.15 = (bf16[2,16,16,616]{3,2,1,0:T(8,128)(2,1)S(1)}, bf16[2,16,16,616]{3,2,1,0:T(8,128)(2,1)}, u32[]{:S(2)}, u32[]{:S(2)}) collective-permute-start(bf16[2,16,16,616]{3,2,1,0:T(8,128)(2,1)S(1)} %pad_maximum_fusion.1.refs_1_), channel_id=1, source_target_pairs={{0,64},{8,24},{16,80},{24,40},{32,96},{40,56},{48,112},{56,8},{64,... | collective-permute-start | bytes 1892360 | tf_op jit(solution)/shard_map/ppermute | solution.py:339
  36.8 19.1 %collective-permute-start.16 = (bf16[2,16,16,616]{3,2,1,0:T(8,128)(2,1)S(1)}, bf16[2,16,16,616]{3,2,1,0:T(8,128)(2,1)}, u32[]{:S(2)}, u32[]{:S(2)}) collective-permute-start(bf16[2,16,16,616]{3,2,1,0:T(8,128)(2,1)S(1)} %pad_maximum_fusion.refs_0_), channel_id=1, source_target_pairs={{0,192},{8,56},{16,208},{24,8},{32,224},{40,24},{48,240},{56,40},{... | collective-permute-start | bytes 1892360 | tf_op jit(solution)/shard_map/ppermute | solution.py:339
  40.0 15.9 %collective-permute-start.17 = (bf16[2,16,16,616]{3,2,1,0:T(8,128)(2,1)S(1)}, bf16[2,16,16,616]{3,2,1,0:T(8,128)(2,1)}, u32[]{:S(2)}, u32[]{:S(2)}) collective-permute-start(bf16[2,16,16,616]{3,2,1,0:T(8,128)(2,1)S(1)} %collective-permute-done.2.refs_2_), channel_id=1, source_target_pairs={{0,64},{8,24},{16,80},{24,40},{32,96},{40,56},{48,112},{56,8},{64,... | collective-permute-start | bytes 1892360 | tf_op jit(solution)/shard_map/ppermute | solution.py:339
  40.0 15.9 %collective-permute-start.18 = (bf16[2,16,16,616]{3,2,1,0:T(8,128)(2,1)}, bf16[2,16,16,616]{3,2,1,0:T(8,128)(2,1)}, u32[]{:S(2)}, u32[]{:S(2)}) collective-permute-start(bf16[2,16,16,616]{3,2,1,0:T(8,128)(2,1)} %collective-permute-done.9.refs_5_), channel_id=1, source_target_pairs={{0,192},{8,56},{16,208},{24,8},{32,224},{40,24},{48,240},{56,40},{... | collective-permute-start | bytes 1892360 | tf_op jit(solution)/shard_map/ppermute | solution.py:339
  43.3 11.2 %collective-permute-start.14 = (bf16[4,4,32,256]{3,2,1,0:T(8,128)(2,1)S(1)}, bf16[4,4,32,256]{3,2,1,0:T(8,128)(2,1)S(1)}, u32[]{:S(2)}, u32[]{:S(2)}) collective-permute-start(bf16[4,4,32,256]{3,2,1,0:T(8,128)(2,1)S(1)} %pad_maximum_fusion.2), channel_id=1, source_target_pairs={{0,8},{8,0},{16,24},{24,16},{32,40},{40,32},{48,56},{56,48},{64,72... | collective-permute-start | bytes 786440 | tf_op jit(solution)/shard_map/ppermute | solution.py:393
  43.4 1.0 copy-start
  44.5 0.7 copy-start.4
  49.8 4.7 %copy-start.2 = (bf16[192,768]{1,0:T(8,128)(2,1)S(1)}, bf16[192,768]{1,0:T(8,128)(2,1)}, u32[]{:S(2)}) copy-start(bf16[192,768]{1,0:T(8,128)(2,1)} %constant.173.clone.own_cell_ref) | copy-start | bytes 884740
  49.8 4.7 %copy-start.3 = (bf16[64,768]{1,0:T(8,128)(2,1)S(1)}, bf16[64,768]{1,0:T(8,128)(2,1)}, u32[]{:S(2)}) copy-start(bf16[64,768]{1,0:T(8,128)(2,1)} %constant.172.clone.row_tile_ref) | copy-start | bytes 294916
  49.8 4.7 %copy-start.5 = (bf16[16,192]{1,0:T(8,128)(2,1)S(1)}, bf16[16,192]{1,0:T(8,128)(2,1)}, u32[]{:S(2)}) copy-start(bf16[16,192]{1,0:T(8,128)(2,1)} %constant.174.clone.tap_ref) | copy-start | bytes 18436
  49.8 4.7 %copy-start.6 = (s32[1,768]{1,0:T(1,128)S(1)}, s32[1,768]{1,0:T(1,128)}, u32[]{:S(2)}) copy-start(s32[1,768]{1,0:T(1,128)} %constant.182.token_ref) | copy-start | bytes 9220
  55.9 17.0 %copy-start.10 = (bf16[32,32,1]{1,0,2:T(8,128)(2,1)S(1)}, bf16[32,32,1]{1,0,2:T(8,128)(2,1)}, u32[]{:S(2)}) copy-start(bf16[32,32,1]{1,0,2:T(8,128)(2,1)} %constant.285) | copy-start | bytes 6148
  55.9 19.7 %copy-start.9 = (f32[1,512]{1,0:T(1,128)S(1)}, f32[1,512]{1,0:T(1,128)}, u32[]{:S(2)}) copy-start(f32[1,512]{1,0:T(1,128)} %param.22) | copy-start | bytes 6148
  56.0 20.5 %copy-start.8 = (f32[512]{0:T(512)S(1)}, f32[512]{0:T(512)}, u32[]{:S(2)}) copy-start(f32[512]{0:T(512)} %param.23) | copy-start | bytes 6148
  56.0 30.3 %copy-start.7 = (f32[4,512]{1,0:T(4,128)S(1)}, f32[4,512]{1,0:T(4,128)}, u32[]{:S(2)}) copy-start(f32[4,512]{1,0:T(4,128)} %latent_ref.1) | copy-start | bytes 24580
  65.9 20.3 %all-to-all-start = ((bf16[32,48,256]{2,1,0:T(8,128)(2,1)}), bf16[32,48,256]{2,1,0:T(8,128)(2,1)S(1)}, u32[]{:S(2)}, u32[]{:S(2)}) async-start(bf16[32,48,256]{2,1,0:T(8,128)(2,1)} %bitcast.22), calls=%async_computation | async-start | bytes 1572864 | tf_op jit(solution)/shard_map/all_to_all | solution.py:415

commit v6 on v5

--- a/solution.py
+++ b/solution.py
@@ -380,7 +380,9 @@
     up, down, record = lax.optimization_barrier((up, down, record))
     far = [send(up[:half], 1, False), send(down[half:], -1, False)]
     others = [send(record, -offset, False) for offset in OFFSETS[1:]]
-    *far, record, sib_pos = lax.optimization_barrier((*far, jnp.stack([record] + others, 0), sib_pos))
+    *far, record, sib_pos, sib_swath = lax.optimization_barrier(
+        (*far, jnp.stack([record] + others, 0), sib_pos, sib_swath)
+    )
     low = jnp.stack([shard, up], 0)
     high = jnp.stack([down, jnp.concatenate(far, 0)], 0)
     above_low, below_high = send(low, 1, True), send(high, -1, True)

time: 109 us -> 108 us (level)
  waiting for transfers between devices: 25.7 us -> 21.8 us
  starting transfers between devices: 29.5 us -> 31.2 us
  blocking collectives: 17.4 us -> 18.6 us
    ppermute x16, waiting for transfers between devices: 15.6 us -> 11.7 us  [send(): return lax.ppermute(array, 'lat', shift(offset, second))]
    all_to_all x1, starting transfers between devices: 7.03 us -> 8.42 us  [body(): lax.all_to_all(outgoing, 'lat', split_axis=0, concat_axis=0, tiled=True)]
    all_to_all x1, blocking collectives: 17.4 us -> 18.6 us  [body(): lax.all_to_all(parts.reshape(sources, -1, width + FP), 'src', split_axis=...]
  transfers between devices with their start and end apart: 20 -> 20, of which waited for: 9 -> 8; matrix products, arithmetic and copies ran while one was open for 5% -> 5% of each run, Pallas kernels for 12% -> 12%
where the time goes in v6:
time: 108 us
  starting transfers between devices  31.2 us (29%)
  Pallas kernels  27.5 us (25%)
  waiting for transfers between devices  21.8 us (20%)
  blocking collectives  18.6 us (17%)
  local copies, waits for them, and re-layouts  4.86 us (5%)
  other arithmetic  2.91 us (3%)
    ppermute x16, starting transfers between devices, send(): return lax.ppermute(array, 'lat', shift(offset, second))  22.5 us
    all_to_all x1, blocking collectives, body(): lax.all_to_all(parts.reshape(sources, -1, width + FP), 'src', split_axis=...  18.6 us
    ppermute x16, waiting for transfers between devices, send(): return lax.ppermute(array, 'lat', shift(offset, second))  11.7 us
    all_to_all x1, waiting for transfers between devices, body(): lax.all_to_all(outgoing, 'lat', split_axis=0, concat_axis=0, tiled=True)  9.55 us
    pallas_call x1, Pallas kernels, embed(): pl.pallas_call(embed_kernel, in_specs=[vmem] * (len(large) + 3), out_spec...  9.35 us
    pallas_call x2, Pallas kernels, gridded(): pl.pallas_call(grid_kernel, in_specs=[pl.BlockSpec(memory_space=pl.ANY),...  9.21 us
    all_to_all x1, starting transfers between devices, body(): lax.all_to_all(outgoing, 'lat', split_axis=0, concat_axis=0, tiled=True)  8.42 us
    pallas_call x1, Pallas kernels, attend(): pl.pallas_call(attend_kernel, out_shape=jax.ShapeDtypeStruct((PATCHES * L...  2.89 us
  transfers between devices with their start and end apart: 20, of which 8 were waited for; matrix products, arithmetic and copies ran while one was open for 5% of the time, Pallas kernels for 12%

profile of v6, /device:TPU:2, one launch (start us, length us, event | category | flops | bytes accessed | tf_op | source)
XLA Modules:
  0.0 107.6 jit_solution(16293783036290574460)
XLA Ops:
  0.0 1.5 %collective-permute-start = (bf16[16,16,616]{2,1,0:T(8,128)(2,1)}, bf16[16,16,616]{2,1,0:T(8,128)(2,1)S(1)}, u32[]{:S(2)}, u32[]{:S(2)}) collective-permute-start(bf16[16,16,616]{2,1,0:T(8,128)(2,1)} %bitcast.78), channel_id=1, source_target_pairs={{0,16},{8,72},{16,32},{24,88},{32,48},{40,104},{48,0},{56,120},{64... | collective-permute-start | bytes 946184 | tf_op jit(solution)/shard_map/ppermute | solution.py:339
  1.5 0.8 collective-permute-start.1
  2.3 2.6 %tile_records.1 = bf16[32,256]{1,0:T(8,128)(2,1)} custom-call(s32[32]{0:T(128)} %bitcast.93, s32[32]{0:T(128)} %bitcast.94, bf16[32,2,128]{2,1,0:T(2,128)(2,1)} %bitcast.68, f32[2,192,128]{2,1,0:T(8,128)} %constant.170.clone.center_ref), custom_call_target="tpu_custom_call" | custom-call | flops 1000000 | bytes 10000 | tf_op jit(solution)/shard_map/tile_records/pallas_call | solution.py:77
  4.9 2.7 %collective-permute-done = bf16[16,16,616]{2,1,0:T(8,128)(2,1)S(1)} collective-permute-done((bf16[16,16,616]{2,1,0:T(8,128)(2,1)}, bf16[16,16,616]{2,1,0:T(8,128)(2,1)S(1)}, u32[]{:S(2)}, u32[]{:S(2)}) %collective-permute-start) | collective-permute-done | bytes 315424 | tf_op jit(solution)/shard_map/ppermute | solution.py:339
  7.5 1.2 %collective-permute-done.1 = bf16[16,16,616]{2,1,0:T(8,128)(2,1)S(1)} collective-permute-done((bf16[16,16,616]{2,1,0:T(8,128)(2,1)}, bf16[16,16,616]{2,1,0:T(8,128)(2,1)S(1)}, u32[]{:S(2)}, u32[]{:S(2)}) %collective-permute-start.1) | collective-permute-done | bytes 315424 | tf_op jit(solution)/shard_map/ppermute | solution.py:339
  8.8 1.4 %collective-permute-start.5 = (bf16[32,256]{1,0:T(8,128)(2,1)}, bf16[32,256]{1,0:T(8,128)(2,1)S(1)}, u32[]{:S(2)}, u32[]{:S(2)}) collective-permute-start(bf16[32,256]{1,0:T(8,128)(2,1)} %tile_records.1), channel_id=1, source_target_pairs={{0,16},{8,72},{16,32},{24,88},{32,48},{40,104},{48,0},{56,120},{64... | collective-permute-start | bytes 49160 | tf_op jit(solution)/shard_map/ppermute | solution.py:339
  10.8 4.1 %collective-permute-start.7 = (bf16[32,256]{1,0:T(8,128)(2,1)}, bf16[32,256]{1,0:T(8,128)(2,1)S(1)}, u32[]{:S(2)}, u32[]{:S(2)}) collective-permute-start(bf16[32,256]{1,0:T(8,128)(2,1)} %tile_records.1), channel_id=1, source_target_pairs={{0,32},{8,136},{16,48},{24,152},{32,0},{40,168},{48,16},{56,184},{... | collective-permute-start | bytes 49160 | tf_op jit(solution)/shard_map/ppermute | solution.py:339
  14.9 0.7 collective-permute-start.3
  15.6 1.5 %collective-permute-start.4 = (bf16[8,16,616]{2,1,0:T(8,128)(2,1)S(1)}, bf16[8,16,616]{2,1,0:T(8,128)(2,1)S(1)}, u32[]{:S(2)}, u32[]{:S(2)}) collective-permute-start(bf16[8,16,616]{2,1,0:T(8,128)(2,1)S(1)} %slice.19), channel_id=1, source_target_pairs={{0,48},{8,200},{16,0},{24,216},{32,16},{40,232},{48,32},{56,248},{... | collective-permute-start | bytes 473096 | tf_op jit(solution)/shard_map/ppermute | solution.py:339
  17.1 1.1 pad_maximum_fusion.refs_0_
  18.4 0.7 pad_maximum_fusion.3
  20.3 0.7 collective-permute-done.4
  21.2 1.6 %collective-permute-start.10 = (bf16[2,16,16,616]{3,2,1,0:T(8,128)(2,1)S(1)}, bf16[2,16,16,616]{3,2,1,0:T(8,128)(2,1)}, u32[]{:S(2)}, u32[]{:S(2)}) collective-permute-start(bf16[2,16,16,616]{3,2,1,0:T(8,128)(2,1)S(1)} %pad_maximum_fusion.1.refs_1_), channel_id=1, source_target_pairs={{0,192},{8,56},{16,208},{24,8},{32,224},{40,24},{48,240},{56,40},{... | collective-permute-start | bytes 1892360 | tf_op jit(solution)/shard_map/ppermute | solution.py:339
  23.3 2.8 %collective-permute-start.12 = (bf16[4,32,256]{2,1,0:T(8,128)(2,1)S(1)}, bf16[4,32,256]{2,1,0:T(8,128)(2,1)S(1)}, u32[]{:S(2)}, u32[]{:S(2)}) collective-permute-start(bf16[4,32,256]{2,1,0:T(8,128)(2,1)S(1)} %pad_maximum_fusion.3), channel_id=1, source_target_pairs={{0,192},{8,56},{16,208},{24,8},{32,224},{40,24},{48,240},{56,40},{... | collective-permute-start | bytes 196616 | tf_op jit(solution)/shard_map/ppermute | solution.py:339
  26.0 4.8 %collective-permute-done.11 = bf16[4,32,256]{2,1,0:T(8,128)(2,1)S(1)} collective-permute-done((bf16[4,32,256]{2,1,0:T(8,128)(2,1)S(1)}, bf16[4,32,256]{2,1,0:T(8,128)(2,1)S(1)}, u32[]{:S(2)}, u32[]{:S(2)}) %collective-permute-start.11) | collective-permute-done | bytes 65568 | tf_op jit(solution)/shard_map/ppermute | solution.py:339
  30.9 1.7 %collective-permute-done.12 = bf16[4,32,256]{2,1,0:T(8,128)(2,1)S(1)} collective-permute-done((bf16[4,32,256]{2,1,0:T(8,128)(2,1)S(1)}, bf16[4,32,256]{2,1,0:T(8,128)(2,1)S(1)}, u32[]{:S(2)}, u32[]{:S(2)}) %collective-permute-start.12) | collective-permute-done | bytes 65568 | tf_op jit(solution)/shard_map/ppermute | solution.py:339
  32.6 1.9 %collective-permute-start.15 = (bf16[2,16,16,616]{3,2,1,0:T(8,128)(2,1)S(1)}, bf16[2,16,16,616]{3,2,1,0:T(8,128)(2,1)}, u32[]{:S(2)}, u32[]{:S(2)}) collective-permute-start(bf16[2,16,16,616]{3,2,1,0:T(8,128)(2,1)S(1)} %pad_maximum_fusion.1.refs_1_), channel_id=1, source_target_pairs={{0,64},{8,24},{16,80},{24,40},{32,96},{40,56},{48,112},{56,8},{64,... | collective-permute-start | bytes 1892360 | tf_op jit(solution)/shard_map/ppermute | solution.py:339
  34.5 1.9 %collective-permute-start.16 = (bf16[2,16,16,616]{3,2,1,0:T(8,128)(2,1)S(1)}, bf16[2,16,16,616]{3,2,1,0:T(8,128)(2,1)}, u32[]{:S(2)}, u32[]{:S(2)}) collective-permute-start(bf16[2,16,16,616]{3,2,1,0:T(8,128)(2,1)S(1)} %pad_maximum_fusion.refs_0_), channel_id=1, source_target_pairs={{0,192},{8,56},{16,208},{24,8},{32,224},{40,24},{48,240},{56,40},{... | collective-permute-start | bytes 1892360 | tf_op jit(solution)/shard_map/ppermute | solution.py:339
  36.5 3.1 %collective-permute-start.18 = (bf16[2,16,16,616]{3,2,1,0:T(8,128)(2,1)}, bf16[2,16,16,616]{3,2,1,0:T(8,128)(2,1)}, u32[]{:S(2)}, u32[]{:S(2)}) collective-permute-start(bf16[2,16,16,616]{3,2,1,0:T(8,128)(2,1)} %collective-permute-done.10.refs_5_), channel_id=1, source_target_pairs={{0,192},{8,56},{16,208},{24,8},{32,224},{40,24},{48,240},{56,40},{... | collective-permute-start | bytes 1892360 | tf_op jit(solution)/shard_map/ppermute | solution.py:339
  39.8 1.0 copy-done
  40.9 0.7 copy-done.4
  41.6 4.6 %grid_tiles.2.own_ref = bf16[16,384,616]{2,1,0:T(8,128)(2,1)S(1)} custom-call(bf16[32,616,128]{2,1,0:T(8,128)(2,1)} %bitcast.72, bf16[32,2,128]{2,1,0:T(2,128)(2,1)S(1)} %bitcast.70, f32[4,256,128]{2,1,0:T(8,128)S(1)} %copy-done), custom_call_target="tpu_custom_call" | custom-call | flops 1000000 | bytes 10000 | tf_op jit(solution)/shard_map/grid_tiles/pallas_call | solution.py:166
  46.2 4.6 %grid_tiles.3.sib_ref = bf16[16,384,616]{2,1,0:T(8,128)(2,1)S(1)} custom-call(bf16[32,616,128]{2,1,0:T(8,128)(2,1)} %collective-permute-done.9.swath_ref, bf16[32,2,128]{2,1,0:T(2,128)(2,1)S(1)} %collective-permute-done.8.pos_ref, f32[4,256,128]{2,1,0:T(8,128)S(1)} %copy-done.1), custom_call_target="tpu_custom_call" | custom-call | flops 1000000 | bytes 10000 | tf_op jit(solution)/shard_map/grid_tiles/pallas_call | solution.py:166
  50.9 1.4 %inverse_density.1 = (f32[16,768]{1,0:T(8,128)S(1)}, s32[1,768]{1,0:T(1,128)S(1)}) custom-call(s32[1]{0:T(128)} %bitcast.19.core_ref, bf16[512,256]{1,0:T(8,128)(2,1)S(1)} %bitcast.63, bf16[512,256]{1,0:T(8,128)(2,1)S(1)} %bitcast.66, s32[1,768]{1,0:T(1,128)S(1)} %copy-done.6, bf16[64,768]{1,0:T(8,128)(2,1)S(1)} %copy-done.3, ...), custom_call_target="tpu_custom_call" | custom-call | flops 1000000 | bytes 10000 | tf_op jit(solution)/shard_map/inverse_density/pallas_call | solution.py:125
  52.4 9.3 %embed_tiles.1 = bf16[1536,256]{1,0:T(8,128)(2,1)} custom-call(bf16[16,384,616]{2,1,0:T(8,128)(2,1)S(1)} %grid_tiles.2.own_ref, bf16[16,384,616]{2,1,0:T(8,128)(2,1)S(1)} %grid_tiles.3.sib_ref, bf16[2,16,16,616]{3,2,1,0:T(8,128)(2,1)S(1)} %pad_maximum_fusion.refs_0_, bf16[2,16,16,616]{3,2,1,0:T(8,128)(2,1)S(1)} %pad_maximum_fusion.1.refs_1_, ...), custom_call_target="tpu_custom_call" | custom-call | flops 9663676416 | bytes 1000000 | tf_op jit(solution)/shard_map/embed_tiles/pallas_call | solution.py:211
  62.3 8.4 %all-to-all-start = ((bf16[32,48,256]{2,1,0:T(8,128)(2,1)}), bf16[32,48,256]{2,1,0:T(8,128)(2,1)S(1)}, u32[]{:S(2)}, u32[]{:S(2)}) async-start(bf16[32,48,256]{2,1,0:T(8,128)(2,1)} %bitcast.22), calls=%async_computation | async-start | bytes 1572864 | tf_op jit(solution)/shard_map/all_to_all | solution.py:417
  71.1 1.3 %copy.32 = bf16[16,2,16,1024]{3,2,0,1:T(8,128)(2,1)S(1)} copy(bf16[16,2,16,1024]{3,2,1,0:T(8,128)(2,1)} %bitcast.73) | data formatting | bytes 2097152 | tf_op jit(solution)/shard_map/reshape | solution.py:434
  73.4 0.7 reduce.7
  74.4 9.5 %all-to-all-done = bf16[32,48,256]{2,1,0:T(8,128)(2,1)S(1)} async-done(((bf16[32,48,256]{2,1,0:T(8,128)(2,1)}), bf16[32,48,256]{2,1,0:T(8,128)(2,1)S(1)}, u32[]{:S(2)}, u32[]{:S(2)}) %all-to-all-start) | async-done | bytes 786464 | tf_op jit(solution)/shard_map/all_to_all | solution.py:417
  84.0 2.9 %attend_source.1 = bf16[128,640]{1,0:T(8,128)(2,1)S(1)} custom-call(bf16[16,2,48,256]{3,2,1,0:T(8,128)(2,1)S(1)} %bitcast.65, s32[1,768]{1,0:T(1,128)S(1)} %select_n.396.row_ref, f32[1,512]{1,0:T(1,128)S(1)} %broadcast_in_dim_reshape.6.bias_ref, f32[1,512]{1,0:T(1,128)S(1)} %broadcast_in_dim_reshape.7.gain_ref, bf16[512,1024]{1,0:T(8,128)(2,1)S(1)} %bitcast.64, ...), custom_call_target="tpu_custom_call" | custom-call | flops 1572864000 | bytes 3000000 | tf_op jit(solution)/shard_map/attend_source/pallas_call | solution.py:286
  86.9 18.6 %all_to_all.10.parts_ref = bf16[8,16,640]{2,1,0:T(8,128)(2,1)} all-to-all(bf16[8,16,640]{2,1,0:T(8,128)(2,1)S(1)} %bitcast.67), channel_id=1, replica_groups=mesh['lat'=32,'src'=8] {'src'}, dimensions={0} | all-to-all | bytes 327680 | tf_op jit(solution)/shard_map/all_to_all | solution.py:446
  105.5 2.1 %combine_sources.1 = f32[4,4,512]{2,1,0:T(4,128)} custom-call(bf16[8,16,640]{2,1,0:T(8,128)(2,1)} %all_to_all.10.parts_ref, bf16[512,512]{1,0:T(8,128)(2,1)} %weight_ref.1), custom_call_target="tpu_custom_call" | custom-call | flops 33554432 | bytes 800000 | tf_op jit(solution)/shard_map/combine_sources/pallas_call | solution.py:315
  (72 shorter events, 5.2 us)
Async XLA Ops:
  0.0 21.0 %collective-permute-start.9 = (bf16[32,616,128]{2,1,0:T(8,128)(2,1)}, bf16[32,616,128]{2,1,0:T(8,128)(2,1)}, u32[]{:S(2)}, u32[]{:S(2)}) collective-permute-start(bf16[32,616,128]{2,1,0:T(8,128)(2,1)} %bitcast.71), channel_id=1, source_target_pairs={{0,8},{8,0},{16,24},{24,16},{32,40},{40,32},{48,56},{56,48},{64,72... | collective-permute-start | bytes 15138824 | tf_op jit(solution)/shard_map/ppermute | solution.py:377
  0.0 7.5 %collective-permute-start = (bf16[16,16,616]{2,1,0:T(8,128)(2,1)}, bf16[16,16,616]{2,1,0:T(8,128)(2,1)S(1)}, u32[]{:S(2)}, u32[]{:S(2)}) collective-permute-start(bf16[16,16,616]{2,1,0:T(8,128)(2,1)} %bitcast.78), channel_id=1, source_target_pairs={{0,16},{8,72},{16,32},{24,88},{32,48},{40,104},{48,0},{56,120},{64... | collective-permute-start | bytes 946184 | tf_op jit(solution)/shard_map/ppermute | solution.py:339
  1.5 7.3 %collective-permute-start.1 = (bf16[16,16,616]{2,1,0:T(8,128)(2,1)}, bf16[16,16,616]{2,1,0:T(8,128)(2,1)S(1)}, u32[]{:S(2)}, u32[]{:S(2)}) collective-permute-start(bf16[16,16,616]{2,1,0:T(8,128)(2,1)} %bitcast.79), channel_id=1, source_target_pairs={{0,48},{8,200},{16,0},{24,216},{32,16},{40,232},{48,32},{56,248},{... | collective-permute-start | bytes 946184 | tf_op jit(solution)/shard_map/ppermute | solution.py:339
  8.8 6.8 %collective-permute-start.5 = (bf16[32,256]{1,0:T(8,128)(2,1)}, bf16[32,256]{1,0:T(8,128)(2,1)S(1)}, u32[]{:S(2)}, u32[]{:S(2)}) collective-permute-start(bf16[32,256]{1,0:T(8,128)(2,1)} %tile_records.1), channel_id=1, source_target_pairs={{0,16},{8,72},{16,32},{24,88},{32,48},{40,104},{48,0},{56,120},{64... | collective-permute-start | bytes 49160 | tf_op jit(solution)/shard_map/ppermute | solution.py:339
  10.2 8.0 %collective-permute-start.6 = (bf16[32,256]{1,0:T(8,128)(2,1)}, bf16[32,256]{1,0:T(8,128)(2,1)S(1)}, u32[]{:S(2)}, u32[]{:S(2)}) collective-permute-start(bf16[32,256]{1,0:T(8,128)(2,1)} %tile_records.1), channel_id=1, source_target_pairs={{0,48},{8,200},{16,0},{24,216},{32,16},{40,232},{48,32},{56,248},{... | collective-permute-start | bytes 49160 | tf_op jit(solution)/shard_map/ppermute | solution.py:339
  10.8 7.5 %collective-permute-start.7 = (bf16[32,256]{1,0:T(8,128)(2,1)}, bf16[32,256]{1,0:T(8,128)(2,1)S(1)}, u32[]{:S(2)}, u32[]{:S(2)}) collective-permute-start(bf16[32,256]{1,0:T(8,128)(2,1)} %tile_records.1), channel_id=1, source_target_pairs={{0,32},{8,136},{16,48},{24,152},{32,0},{40,168},{48,16},{56,184},{... | collective-permute-start | bytes 49160 | tf_op jit(solution)/shard_map/ppermute | solution.py:339
  14.9 5.4 %collective-permute-start.3 = (bf16[8,16,616]{2,1,0:T(8,128)(2,1)S(1)}, bf16[8,16,616]{2,1,0:T(8,128)(2,1)S(1)}, u32[]{:S(2)}, u32[]{:S(2)}) collective-permute-start(bf16[8,16,616]{2,1,0:T(8,128)(2,1)S(1)} %slice.18), channel_id=1, source_target_pairs={{0,16},{8,72},{16,32},{24,88},{32,48},{40,104},{48,0},{56,120},{64... | collective-permute-start | bytes 473096 | tf_op jit(solution)/shard_map/ppermute | solution.py:339
  15.6 5.4 %collective-permute-start.4 = (bf16[8,16,616]{2,1,0:T(8,128)(2,1)S(1)}, bf16[8,16,616]{2,1,0:T(8,128)(2,1)S(1)}, u32[]{:S(2)}, u32[]{:S(2)}) collective-permute-start(bf16[8,16,616]{2,1,0:T(8,128)(2,1)S(1)} %slice.19), channel_id=1, source_target_pairs={{0,48},{8,200},{16,0},{24,216},{32,16},{40,232},{48,32},{56,248},{... | collective-permute-start | bytes 473096 | tf_op jit(solution)/shard_map/ppermute | solution.py:339
  18.2 1.5 %collective-permute-start.8 = (bf16[32,2,128]{2,1,0:T(2,128)(2,1)}, bf16[32,2,128]{2,1,0:T(2,128)(2,1)S(1)}, u32[]{:S(2)}, u32[]{:S(2)}) collective-permute-start(bf16[32,2,128]{2,1,0:T(2,128)(2,1)} %bitcast.69), channel_id=1, source_target_pairs={{0,8},{8,0},{16,24},{24,16},{32,40},{40,32},{48,56},{56,48},{64,72... | collective-permute-start | bytes 49160 | tf_op jit(solution)/shard_map/ppermute | solution.py:378
  18.3 14.3 %collective-permute-start.2 = (bf16[2,16,16,616]{3,2,1,0:T(8,128)(2,1)S(1)}, bf16[2,16,16,616]{3,2,1,0:T(8,128)(2,1)S(1)}, u32[]{:S(2)}, u32[]{:S(2)}) collective-permute-start(bf16[2,16,16,616]{3,2,1,0:T(8,128)(2,1)S(1)} %pad_maximum_fusion.refs_0_), channel_id=1, source_target_pairs={{0,64},{8,24},{16,80},{24,40},{32,96},{40,56},{48,112},{56,8},{64,... | collective-permute-start | bytes 1892360 | tf_op jit(solution)/shard_map/ppermute | solution.py:339
  19.1 27.1 %copy-start.1 = (f32[4,256,128]{2,1,0:T(8,128)S(1)}, f32[4,256,128]{2,1,0:T(8,128)}, u32[]{:S(2)}) copy-start(f32[4,256,128]{2,1,0:T(8,128)} %constant.169.clone.center_ref) | copy-start | bytes 1572868
  21.2 11.4 %collective-permute-start.10 = (bf16[2,16,16,616]{3,2,1,0:T(8,128)(2,1)S(1)}, bf16[2,16,16,616]{3,2,1,0:T(8,128)(2,1)}, u32[]{:S(2)}, u32[]{:S(2)}) collective-permute-start(bf16[2,16,16,616]{3,2,1,0:T(8,128)(2,1)S(1)} %pad_maximum_fusion.1.refs_1_), channel_id=1, source_target_pairs={{0,192},{8,56},{16,208},{24,8},{32,224},{40,24},{48,240},{56,40},{... | collective-permute-start | bytes 1892360 | tf_op jit(solution)/shard_map/ppermute | solution.py:339
  22.8 8.1 %collective-permute-start.11 = (bf16[4,32,256]{2,1,0:T(8,128)(2,1)S(1)}, bf16[4,32,256]{2,1,0:T(8,128)(2,1)S(1)}, u32[]{:S(2)}, u32[]{:S(2)}) collective-permute-start(bf16[4,32,256]{2,1,0:T(8,128)(2,1)S(1)} %pad_maximum_fusion.3), channel_id=1, source_target_pairs={{0,64},{8,24},{16,80},{24,40},{32,96},{40,56},{48,112},{56,8},{64,... | collective-permute-start | bytes 196616 | tf_op jit(solution)/shard_map/ppermute | solution.py:339
  23.3 9.3 %collective-permute-start.12 = (bf16[4,32,256]{2,1,0:T(8,128)(2,1)S(1)}, bf16[4,32,256]{2,1,0:T(8,128)(2,1)S(1)}, u32[]{:S(2)}, u32[]{:S(2)}) collective-permute-start(bf16[4,32,256]{2,1,0:T(8,128)(2,1)S(1)} %pad_maximum_fusion.3), channel_id=1, source_target_pairs={{0,192},{8,56},{16,208},{24,8},{32,224},{40,24},{48,240},{56,40},{... | collective-permute-start | bytes 196616 | tf_op jit(solution)/shard_map/ppermute | solution.py:339
  26.0 6.5 %collective-permute-start.13 = (bf16[4,32,256]{2,1,0:T(8,128)(2,1)S(1)}, bf16[4,32,256]{2,1,0:T(8,128)(2,1)S(1)}, u32[]{:S(2)}, u32[]{:S(2)}) collective-permute-start(bf16[4,32,256]{2,1,0:T(8,128)(2,1)S(1)} %pad_maximum_fusion.3), channel_id=1, source_target_pairs={{0,128},{8,40},{16,144},{24,56},{32,160},{40,8},{48,176},{56,24},{... | collective-permute-start | bytes 196616 | tf_op jit(solution)/shard_map/ppermute | solution.py:339
  32.6 19.7 %collective-permute-start.15 = (bf16[2,16,16,616]{3,2,1,0:T(8,128)(2,1)S(1)}, bf16[2,16,16,616]{3,2,1,0:T(8,128)(2,1)}, u32[]{:S(2)}, u32[]{:S(2)}) collective-permute-start(bf16[2,16,16,616]{3,2,1,0:T(8,128)(2,1)S(1)} %pad_maximum_fusion.1.refs_1_), channel_id=1, source_target_pairs={{0,64},{8,24},{16,80},{24,40},{32,96},{40,56},{48,112},{56,8},{64,... | collective-permute-start | bytes 1892360 | tf_op jit(solution)/shard_map/ppermute | solution.py:339
  34.5 17.8 %collective-permute-start.16 = (bf16[2,16,16,616]{3,2,1,0:T(8,128)(2,1)S(1)}, bf16[2,16,16,616]{3,2,1,0:T(8,128)(2,1)}, u32[]{:S(2)}, u32[]{:S(2)}) collective-permute-start(bf16[2,16,16,616]{3,2,1,0:T(8,128)(2,1)S(1)} %pad_maximum_fusion.refs_0_), channel_id=1, source_target_pairs={{0,192},{8,56},{16,208},{24,8},{32,224},{40,24},{48,240},{56,40},{... | collective-permute-start | bytes 1892360 | tf_op jit(solution)/shard_map/ppermute | solution.py:339
  36.4 15.9 %collective-permute-start.17 = (bf16[2,16,16,616]{3,2,1,0:T(8,128)(2,1)S(1)}, bf16[2,16,16,616]{3,2,1,0:T(8,128)(2,1)}, u32[]{:S(2)}, u32[]{:S(2)}) collective-permute-start(bf16[2,16,16,616]{3,2,1,0:T(8,128)(2,1)S(1)} %collective-permute-done.2.refs_2_), channel_id=1, source_target_pairs={{0,64},{8,24},{16,80},{24,40},{32,96},{40,56},{48,112},{56,8},{64,... | collective-permute-start | bytes 1892360 | tf_op jit(solution)/shard_map/ppermute | solution.py:339
  36.5 15.8 %collective-permute-start.18 = (bf16[2,16,16,616]{3,2,1,0:T(8,128)(2,1)}, bf16[2,16,16,616]{3,2,1,0:T(8,128)(2,1)}, u32[]{:S(2)}, u32[]{:S(2)}) collective-permute-start(bf16[2,16,16,616]{3,2,1,0:T(8,128)(2,1)} %collective-permute-done.10.refs_5_), channel_id=1, source_target_pairs={{0,192},{8,56},{16,208},{24,8},{32,224},{40,24},{48,240},{56,40},{... | collective-permute-start | bytes 1892360 | tf_op jit(solution)/shard_map/ppermute | solution.py:339
  39.7 11.2 %collective-permute-start.14 = (bf16[4,4,32,256]{3,2,1,0:T(8,128)(2,1)S(1)}, bf16[4,4,32,256]{3,2,1,0:T(8,128)(2,1)S(1)}, u32[]{:S(2)}, u32[]{:S(2)}) collective-permute-start(bf16[4,4,32,256]{3,2,1,0:T(8,128)(2,1)S(1)} %pad_maximum_fusion.2), channel_id=1, source_target_pairs={{0,8},{8,0},{16,24},{24,16},{32,40},{40,32},{48,56},{56,48},{64,72... | collective-permute-start | bytes 786440 | tf_op jit(solution)/shard_map/ppermute | solution.py:395
  39.8 1.0 copy-start
  40.9 0.7 copy-start.4
  46.2 4.7 %copy-start.2 = (bf16[192,768]{1,0:T(8,128)(2,1)S(1)}, bf16[192,768]{1,0:T(8,128)(2,1)}, u32[]{:S(2)}) copy-start(bf16[192,768]{1,0:T(8,128)(2,1)} %constant.173.clone.own_cell_ref) | copy-start | bytes 884740
  46.2 4.7 %copy-start.3 = (bf16[64,768]{1,0:T(8,128)(2,1)S(1)}, bf16[64,768]{1,0:T(8,128)(2,1)}, u32[]{:S(2)}) copy-start(bf16[64,768]{1,0:T(8,128)(2,1)} %constant.172.clone.row_tile_ref) | copy-start | bytes 294916
  46.2 4.7 %copy-start.5 = (bf16[16,192]{1,0:T(8,128)(2,1)S(1)}, bf16[16,192]{1,0:T(8,128)(2,1)}, u32[]{:S(2)}) copy-start(bf16[16,192]{1,0:T(8,128)(2,1)} %constant.174.clone.tap_ref) | copy-start | bytes 18436
  46.2 4.7 %copy-start.6 = (s32[1,768]{1,0:T(1,128)S(1)}, s32[1,768]{1,0:T(1,128)}, u32[]{:S(2)}) copy-start(s32[1,768]{1,0:T(1,128)} %constant.182.token_ref) | copy-start | bytes 9220
  52.3 18.4 %copy-start.10 = (bf16[32,32,1]{1,0,2:T(8,128)(2,1)S(1)}, bf16[32,32,1]{1,0,2:T(8,128)(2,1)}, u32[]{:S(2)}) copy-start(bf16[32,32,1]{1,0,2:T(8,128)(2,1)} %constant.285) | copy-start | bytes 6148
  52.3 21.1 %copy-start.9 = (f32[1,512]{1,0:T(1,128)S(1)}, f32[1,512]{1,0:T(1,128)}, u32[]{:S(2)}) copy-start(f32[1,512]{1,0:T(1,128)} %param.22) | copy-start | bytes 6148
  52.3 21.9 %copy-start.8 = (f32[512]{0:T(512)S(1)}, f32[512]{0:T(512)}, u32[]{:S(2)}) copy-start(f32[512]{0:T(512)} %param.23) | copy-start | bytes 6148
  52.4 31.6 %copy-start.7 = (f32[4,512]{1,0:T(4,128)S(1)}, f32[4,512]{1,0:T(4,128)}, u32[]{:S(2)}) copy-start(f32[4,512]{1,0:T(4,128)} %latent_ref.1) | copy-start | bytes 24580
  62.3 21.7 %all-to-all-start = ((bf16[32,48,256]{2,1,0:T(8,128)(2,1)}), bf16[32,48,256]{2,1,0:T(8,128)(2,1)S(1)}, u32[]{:S(2)}, u32[]{:S(2)}) async-start(bf16[32,48,256]{2,1,0:T(8,128)(2,1)} %bitcast.22), calls=%async_computation | async-start | bytes 1572864 | tf_op jit(solution)/shard_map/all_to_all | solution.py:417

commit v7 on v6

--- a/solution.py
+++ b/solution.py
@@ -377,7 +377,7 @@
     sib_swath = lax.ppermute(swath, "lat", swap)
     sib_pos = lax.ppermute(fp_pos, "lat", swap)
     record = tile_records(tile_band[0, :, 0], tile_patch[0], fp_pos)
-    up, down, record = lax.optimization_barrier((up, down, record))
+    up, down = lax.optimization_barrier((up, down))
     far = [send(up[:half], 1, False), send(down[half:], -1, False)]
     others = [send(record, -offset, False) for offset in OFFSETS[1:]]
     *far, record, sib_pos, sib_swath = lax.optimization_barrier(

time: 108 us -> 105 us (0.972)
  waiting for transfers between devices: 21.8 us -> 18.7 us
    ppermute x16, waiting for transfers between devices: 11.7 us -> 9.15 us  [send(): return lax.ppermute(array, 'lat', shift(offset, second))]
  transfers between devices with their start and end apart: 20 -> 20, of which waited for: 8 -> 6; matrix products, arithmetic and copies ran while one was open for 5% -> 5% of each run, Pallas kernels for 12% -> 13%
where the time goes in v7:
time: 105 us
  starting transfers between devices  31.7 us (30%)
  Pallas kernels  27.5 us (26%)
  waiting for transfers between devices  18.7 us (18%)
  blocking collectives  18.4 us (18%)
  local copies, waits for them, and re-layouts  4.86 us (5%)
  other arithmetic  2.91 us (3%)
    ppermute x16, starting transfers between devices, send(): return lax.ppermute(array, 'lat', shift(offset, second))  23 us
    all_to_all x1, blocking collectives, body(): lax.all_to_all(parts.reshape(sources, -1, width + FP), 'src', split_axis=...  18.4 us
    all_to_all x1, waiting for transfers between devices, body(): lax.all_to_all(outgoing, 'lat', split_axis=0, concat_axis=0, tiled=True)  9.55 us
    pallas_call x1, Pallas kernels, embed(): pl.pallas_call(embed_kernel, in_specs=[vmem] * (len(large) + 3), out_spec...  9.33 us
    pallas_call x2, Pallas kernels, gridded(): pl.pallas_call(grid_kernel, in_specs=[pl.BlockSpec(memory_space=pl.ANY),...  9.21 us
    ppermute x16, waiting for transfers between devices, send(): return lax.ppermute(array, 'lat', shift(offset, second))  9.15 us
    all_to_all x1, starting transfers between devices, body(): lax.all_to_all(outgoing, 'lat', split_axis=0, concat_axis=0, tiled=True)  8.68 us
    pallas_call x1, Pallas kernels, attend(): pl.pallas_call(attend_kernel, out_shape=jax.ShapeDtypeStruct((PATCHES * L...  2.89 us
  transfers between devices with their start and end apart: 20, of which 6 were waited for; matrix products, arithmetic and copies ran while one was open for 5% of the time, Pallas kernels for 13%

profile of v7, /device:TPU:2, one launch (start us, length us, event | category | flops | bytes accessed | tf_op | source)
XLA Modules:
  0.0 104.9 jit_solution(1206601412491297349)
XLA Ops:
  0.0 1.5 %collective-permute-start = (bf16[16,16,616]{2,1,0:T(8,128)(2,1)}, bf16[16,16,616]{2,1,0:T(8,128)(2,1)S(1)}, u32[]{:S(2)}, u32[]{:S(2)}) collective-permute-start(bf16[16,16,616]{2,1,0:T(8,128)(2,1)} %bitcast.78), channel_id=1, source_target_pairs={{0,16},{8,72},{16,32},{24,88},{32,48},{40,104},{48,0},{56,120},{64... | collective-permute-start | bytes 946184 | tf_op jit(solution)/shard_map/ppermute | solution.py:339
  1.5 0.8 collective-permute-start.1
  2.3 2.6 %tile_records.1 = bf16[32,256]{1,0:T(8,128)(2,1)} custom-call(s32[32]{0:T(128)} %bitcast.93, s32[32]{0:T(128)} %bitcast.94, bf16[32,2,128]{2,1,0:T(2,128)(2,1)} %bitcast.68, f32[2,192,128]{2,1,0:T(8,128)} %constant.170.clone.center_ref), custom_call_target="tpu_custom_call" | custom-call | flops 1000000 | bytes 10000 | tf_op jit(solution)/shard_map/tile_records/pallas_call | solution.py:77
  4.9 1.2 %collective-permute-start.5 = (bf16[32,256]{1,0:T(8,128)(2,1)}, bf16[32,256]{1,0:T(8,128)(2,1)S(1)}, u32[]{:S(2)}, u32[]{:S(2)}) collective-permute-start(bf16[32,256]{1,0:T(8,128)(2,1)} %tile_records.1), channel_id=1, source_target_pairs={{0,16},{8,72},{16,32},{24,88},{32,48},{40,104},{48,0},{56,120},{64... | collective-permute-start | bytes 49160 | tf_op jit(solution)/shard_map/ppermute | solution.py:339
  6.1 2.0 %collective-permute-start.6 = (bf16[32,256]{1,0:T(8,128)(2,1)}, bf16[32,256]{1,0:T(8,128)(2,1)S(1)}, u32[]{:S(2)}, u32[]{:S(2)}) collective-permute-start(bf16[32,256]{1,0:T(8,128)(2,1)} %tile_records.1), channel_id=1, source_target_pairs={{0,48},{8,200},{16,0},{24,216},{32,16},{40,232},{48,32},{56,248},{... | collective-permute-start | bytes 49160 | tf_op jit(solution)/shard_map/ppermute | solution.py:339
  8.1 2.1 %collective-permute-start.7 = (bf16[32,256]{1,0:T(8,128)(2,1)}, bf16[32,256]{1,0:T(8,128)(2,1)S(1)}, u32[]{:S(2)}, u32[]{:S(2)}) collective-permute-start(bf16[32,256]{1,0:T(8,128)(2,1)} %tile_records.1), channel_id=1, source_target_pairs={{0,32},{8,136},{16,48},{24,152},{32,0},{40,168},{48,16},{56,184},{... | collective-permute-start | bytes 49160 | tf_op jit(solution)/shard_map/ppermute | solution.py:339
  10.3 2.7 %collective-permute-start.3 = (bf16[8,16,616]{2,1,0:T(8,128)(2,1)S(1)}, bf16[8,16,616]{2,1,0:T(8,128)(2,1)S(1)}, u32[]{:S(2)}, u32[]{:S(2)}) collective-permute-start(bf16[8,16,616]{2,1,0:T(8,128)(2,1)S(1)} %slice.18), channel_id=1, source_target_pairs={{0,16},{8,72},{16,32},{24,88},{32,48},{40,104},{48,0},{56,120},{64... | collective-permute-start | bytes 473096 | tf_op jit(solution)/shard_map/ppermute | solution.py:339
  13.6 0.7 pad_maximum_fusion.3
  14.3 1.1 %pad_maximum_fusion.refs_0_ = bf16[2,16,16,616]{3,2,1,0:T(8,128)(2,1)S(1)} fusion(bf16[1,16,16,616]{3,2,1,0:T(8,128)(2,1)S(1)} %bitcast.75, bf16[1,16,16,616]{3,2,1,0:T(8,128)(2,1)} %bitcast.80), kind=kLoop, calls=%fused_computation.1 | loop fusion | flops 315392 | bytes 1261568 | tf_op jit(solution)/shard_map/stack | solution.py:386
  15.4 0.8 collective-permute-start.2
  16.6 1.7 %collective-permute-done.4 = bf16[8,16,616]{2,1,0:T(8,128)(2,1)S(1)} collective-permute-done((bf16[8,16,616]{2,1,0:T(8,128)(2,1)S(1)}, bf16[8,16,616]{2,1,0:T(8,128)(2,1)S(1)}, u32[]{:S(2)}, u32[]{:S(2)}) %collective-permute-start.4) | collective-permute-done | bytes 157728 | tf_op jit(solution)/shard_map/ppermute | solution.py:339
  18.4 1.4 %collective-permute-start.10 = (bf16[2,16,16,616]{3,2,1,0:T(8,128)(2,1)S(1)}, bf16[2,16,16,616]{3,2,1,0:T(8,128)(2,1)}, u32[]{:S(2)}, u32[]{:S(2)}) collective-permute-start(bf16[2,16,16,616]{3,2,1,0:T(8,128)(2,1)S(1)} %pad_maximum_fusion.1.refs_1_), channel_id=1, source_target_pairs={{0,192},{8,56},{16,208},{24,8},{32,224},{40,24},{48,240},{56,40},{... | collective-permute-start | bytes 1892360 | tf_op jit(solution)/shard_map/ppermute | solution.py:339
  19.8 0.7 collective-permute-start.11
  20.5 2.5 %collective-permute-start.12 = (bf16[4,32,256]{2,1,0:T(8,128)(2,1)S(1)}, bf16[4,32,256]{2,1,0:T(8,128)(2,1)S(1)}, u32[]{:S(2)}, u32[]{:S(2)}) collective-permute-start(bf16[4,32,256]{2,1,0:T(8,128)(2,1)S(1)} %pad_maximum_fusion.3), channel_id=1, source_target_pairs={{0,192},{8,56},{16,208},{24,8},{32,224},{40,24},{48,240},{56,40},{... | collective-permute-start | bytes 196616 | tf_op jit(solution)/shard_map/ppermute | solution.py:339
  23.0 4.9 %collective-permute-done.11 = bf16[4,32,256]{2,1,0:T(8,128)(2,1)S(1)} collective-permute-done((bf16[4,32,256]{2,1,0:T(8,128)(2,1)S(1)}, bf16[4,32,256]{2,1,0:T(8,128)(2,1)S(1)}, u32[]{:S(2)}, u32[]{:S(2)}) %collective-permute-start.11) | collective-permute-done | bytes 65568 | tf_op jit(solution)/shard_map/ppermute | solution.py:339
  28.0 1.8 %collective-permute-done.12 = bf16[4,32,256]{2,1,0:T(8,128)(2,1)S(1)} collective-permute-done((bf16[4,32,256]{2,1,0:T(8,128)(2,1)S(1)}, bf16[4,32,256]{2,1,0:T(8,128)(2,1)S(1)}, u32[]{:S(2)}, u32[]{:S(2)}) %collective-permute-start.12) | collective-permute-done | bytes 65568 | tf_op jit(solution)/shard_map/ppermute | solution.py:339
  29.9 1.6 %collective-permute-start.15 = (bf16[2,16,16,616]{3,2,1,0:T(8,128)(2,1)S(1)}, bf16[2,16,16,616]{3,2,1,0:T(8,128)(2,1)}, u32[]{:S(2)}, u32[]{:S(2)}) collective-permute-start(bf16[2,16,16,616]{3,2,1,0:T(8,128)(2,1)S(1)} %pad_maximum_fusion.1.refs_1_), channel_id=1, source_target_pairs={{0,64},{8,24},{16,80},{24,40},{32,96},{40,56},{48,112},{56,8},{64,... | collective-permute-start | bytes 1892360 | tf_op jit(solution)/shard_map/ppermute | solution.py:339
  31.5 2.1 %collective-permute-start.16 = (bf16[2,16,16,616]{3,2,1,0:T(8,128)(2,1)S(1)}, bf16[2,16,16,616]{3,2,1,0:T(8,128)(2,1)}, u32[]{:S(2)}, u32[]{:S(2)}) collective-permute-start(bf16[2,16,16,616]{3,2,1,0:T(8,128)(2,1)S(1)} %pad_maximum_fusion.refs_0_), channel_id=1, source_target_pairs={{0,192},{8,56},{16,208},{24,8},{32,224},{40,24},{48,240},{56,40},{... | collective-permute-start | bytes 1892360 | tf_op jit(solution)/shard_map/ppermute | solution.py:339
  33.6 3.2 %collective-permute-start.18 = (bf16[2,16,16,616]{3,2,1,0:T(8,128)(2,1)}, bf16[2,16,16,616]{3,2,1,0:T(8,128)(2,1)}, u32[]{:S(2)}, u32[]{:S(2)}) collective-permute-start(bf16[2,16,16,616]{3,2,1,0:T(8,128)(2,1)} %collective-permute-done.10.refs_5_), channel_id=1, source_target_pairs={{0,192},{8,56},{16,208},{24,8},{32,224},{40,24},{48,240},{56,40},{... | collective-permute-start | bytes 1892360 | tf_op jit(solution)/shard_map/ppermute | solution.py:339
  37.0 1.0 copy-done
  38.1 0.7 copy-done.4
  38.8 4.6 %grid_tiles.2.own_ref = bf16[16,384,616]{2,1,0:T(8,128)(2,1)S(1)} custom-call(bf16[32,616,128]{2,1,0:T(8,128)(2,1)} %bitcast.72, bf16[32,2,128]{2,1,0:T(2,128)(2,1)S(1)} %bitcast.70, f32[4,256,128]{2,1,0:T(8,128)S(1)} %copy-done), custom_call_target="tpu_custom_call" | custom-call | flops 1000000 | bytes 10000 | tf_op jit(solution)/shard_map/grid_tiles/pallas_call | solution.py:166
  43.4 4.6 %grid_tiles.3.sib_ref = bf16[16,384,616]{2,1,0:T(8,128)(2,1)S(1)} custom-call(bf16[32,616,128]{2,1,0:T(8,128)(2,1)} %collective-permute-done.9.swath_ref, bf16[32,2,128]{2,1,0:T(2,128)(2,1)S(1)} %collective-permute-done.8.pos_ref, f32[4,256,128]{2,1,0:T(8,128)S(1)} %copy-done.1), custom_call_target="tpu_custom_call" | custom-call | flops 1000000 | bytes 10000 | tf_op jit(solution)/shard_map/grid_tiles/pallas_call | solution.py:166
  48.1 1.4 %inverse_density.1 = (f32[16,768]{1,0:T(8,128)S(1)}, s32[1,768]{1,0:T(1,128)S(1)}) custom-call(s32[1]{0:T(128)} %bitcast.19.core_ref, bf16[512,256]{1,0:T(8,128)(2,1)S(1)} %bitcast.63, bf16[512,256]{1,0:T(8,128)(2,1)S(1)} %bitcast.66, s32[1,768]{1,0:T(1,128)S(1)} %copy-done.6, bf16[64,768]{1,0:T(8,128)(2,1)S(1)} %copy-done.3, ...), custom_call_target="tpu_custom_call" | custom-call | flops 1000000 | bytes 10000 | tf_op jit(solution)/shard_map/inverse_density/pallas_call | solution.py:125
  49.6 9.3 %embed_tiles.1 = bf16[1536,256]{1,0:T(8,128)(2,1)} custom-call(bf16[16,384,616]{2,1,0:T(8,128)(2,1)S(1)} %grid_tiles.2.own_ref, bf16[16,384,616]{2,1,0:T(8,128)(2,1)S(1)} %grid_tiles.3.sib_ref, bf16[2,16,16,616]{3,2,1,0:T(8,128)(2,1)S(1)} %pad_maximum_fusion.refs_0_, bf16[2,16,16,616]{3,2,1,0:T(8,128)(2,1)S(1)} %pad_maximum_fusion.1.refs_1_, ...), custom_call_target="tpu_custom_call" | custom-call | flops 9663676416 | bytes 1000000 | tf_op jit(solution)/shard_map/embed_tiles/pallas_call | solution.py:211
  59.4 8.7 %all-to-all-start = ((bf16[32,48,256]{2,1,0:T(8,128)(2,1)}), bf16[32,48,256]{2,1,0:T(8,128)(2,1)S(1)}, u32[]{:S(2)}, u32[]{:S(2)}) async-start(bf16[32,48,256]{2,1,0:T(8,128)(2,1)} %bitcast.22), calls=%async_computation | async-start | bytes 1572864 | tf_op jit(solution)/shard_map/all_to_all | solution.py:417
  68.6 1.3 %copy.32 = bf16[16,2,16,1024]{3,2,0,1:T(8,128)(2,1)S(1)} copy(bf16[16,2,16,1024]{3,2,1,0:T(8,128)(2,1)} %bitcast.73) | data formatting | bytes 2097152 | tf_op jit(solution)/shard_map/reshape | solution.py:434
  70.8 0.7 reduce.7
  71.9 9.6 %all-to-all-done = bf16[32,48,256]{2,1,0:T(8,128)(2,1)S(1)} async-done(((bf16[32,48,256]{2,1,0:T(8,128)(2,1)}), bf16[32,48,256]{2,1,0:T(8,128)(2,1)S(1)}, u32[]{:S(2)}, u32[]{:S(2)}) %all-to-all-start) | async-done | bytes 786464 | tf_op jit(solution)/shard_map/all_to_all | solution.py:417
  81.4 2.9 %attend_source.1 = bf16[128,640]{1,0:T(8,128)(2,1)S(1)} custom-call(bf16[16,2,48,256]{3,2,1,0:T(8,128)(2,1)S(1)} %bitcast.65, s32[1,768]{1,0:T(1,128)S(1)} %select_n.396.row_ref, f32[1,512]{1,0:T(1,128)S(1)} %broadcast_in_dim_reshape.6.bias_ref, f32[1,512]{1,0:T(1,128)S(1)} %broadcast_in_dim_reshape.7.gain_ref, bf16[512,1024]{1,0:T(8,128)(2,1)S(1)} %bitcast.64, ...), custom_call_target="tpu_custom_call" | custom-call | flops 1572864000 | bytes 3000000 | tf_op jit(solution)/shard_map/attend_source/pallas_call | solution.py:286
  84.3 18.4 %all_to_all.10.parts_ref = bf16[8,16,640]{2,1,0:T(8,128)(2,1)} all-to-all(bf16[8,16,640]{2,1,0:T(8,128)(2,1)S(1)} %bitcast.67), channel_id=1, replica_groups=mesh['lat'=32,'src'=8] {'src'}, dimensions={0} | all-to-all | bytes 327680 | tf_op jit(solution)/shard_map/all_to_all | solution.py:446
  102.7 2.1 %combine_sources.1 = f32[4,4,512]{2,1,0:T(4,128)} custom-call(bf16[8,16,640]{2,1,0:T(8,128)(2,1)} %all_to_all.10.parts_ref, bf16[512,512]{1,0:T(8,128)(2,1)} %weight_ref.1), custom_call_target="tpu_custom_call" | custom-call | flops 33554432 | bytes 800000 | tf_op jit(solution)/shard_map/combine_sources/pallas_call | solution.py:315
  (72 shorter events, 3.7 us)
Async XLA Ops:
  0.0 18.3 %collective-permute-start.9 = (bf16[32,616,128]{2,1,0:T(8,128)(2,1)}, bf16[32,616,128]{2,1,0:T(8,128)(2,1)}, u32[]{:S(2)}, u32[]{:S(2)}) collective-permute-start(bf16[32,616,128]{2,1,0:T(8,128)(2,1)} %bitcast.71), channel_id=1, source_target_pairs={{0,8},{8,0},{16,24},{24,16},{32,40},{40,32},{48,56},{56,48},{64,72... | collective-permute-start | bytes 15138824 | tf_op jit(solution)/shard_map/ppermute | solution.py:377
  0.0 8.1 %collective-permute-start = (bf16[16,16,616]{2,1,0:T(8,128)(2,1)}, bf16[16,16,616]{2,1,0:T(8,128)(2,1)S(1)}, u32[]{:S(2)}, u32[]{:S(2)}) collective-permute-start(bf16[16,16,616]{2,1,0:T(8,128)(2,1)} %bitcast.78), channel_id=1, source_target_pairs={{0,16},{8,72},{16,32},{24,88},{32,48},{40,104},{48,0},{56,120},{64... | collective-permute-start | bytes 946184 | tf_op jit(solution)/shard_map/ppermute | solution.py:339
  1.5 8.7 %collective-permute-start.1 = (bf16[16,16,616]{2,1,0:T(8,128)(2,1)}, bf16[16,16,616]{2,1,0:T(8,128)(2,1)S(1)}, u32[]{:S(2)}, u32[]{:S(2)}) collective-permute-start(bf16[16,16,616]{2,1,0:T(8,128)(2,1)} %bitcast.79), channel_id=1, source_target_pairs={{0,48},{8,200},{16,0},{24,216},{32,16},{40,232},{48,32},{56,248},{... | collective-permute-start | bytes 946184 | tf_op jit(solution)/shard_map/ppermute | solution.py:339
  4.9 5.4 %collective-permute-start.5 = (bf16[32,256]{1,0:T(8,128)(2,1)}, bf16[32,256]{1,0:T(8,128)(2,1)S(1)}, u32[]{:S(2)}, u32[]{:S(2)}) collective-permute-start(bf16[32,256]{1,0:T(8,128)(2,1)} %tile_records.1), channel_id=1, source_target_pairs={{0,16},{8,72},{16,32},{24,88},{32,48},{40,104},{48,0},{56,120},{64... | collective-permute-start | bytes 49160 | tf_op jit(solution)/shard_map/ppermute | solution.py:339
  6.1 6.8 %collective-permute-start.6 = (bf16[32,256]{1,0:T(8,128)(2,1)}, bf16[32,256]{1,0:T(8,128)(2,1)S(1)}, u32[]{:S(2)}, u32[]{:S(2)}) collective-permute-start(bf16[32,256]{1,0:T(8,128)(2,1)} %tile_records.1), channel_id=1, source_target_pairs={{0,48},{8,200},{16,0},{24,216},{32,16},{40,232},{48,32},{56,248},{... | collective-permute-start | bytes 49160 | tf_op jit(solution)/shard_map/ppermute | solution.py:339
  8.1 5.5 %collective-permute-start.7 = (bf16[32,256]{1,0:T(8,128)(2,1)}, bf16[32,256]{1,0:T(8,128)(2,1)S(1)}, u32[]{:S(2)}, u32[]{:S(2)}) collective-permute-start(bf16[32,256]{1,0:T(8,128)(2,1)} %tile_records.1), channel_id=1, source_target_pairs={{0,32},{8,136},{16,48},{24,152},{32,0},{40,168},{48,16},{56,184},{... | collective-permute-start | bytes 49160 | tf_op jit(solution)/shard_map/ppermute | solution.py:339
  10.2 6.0 %collective-permute-start.8 = (bf16[32,2,128]{2,1,0:T(2,128)(2,1)}, bf16[32,2,128]{2,1,0:T(2,128)(2,1)S(1)}, u32[]{:S(2)}, u32[]{:S(2)}) collective-permute-start(bf16[32,2,128]{2,1,0:T(2,128)(2,1)} %bitcast.69), channel_id=1, source_target_pairs={{0,8},{8,0},{16,24},{24,16},{32,40},{40,32},{48,56},{56,48},{64,72... | collective-permute-start | bytes 49160 | tf_op jit(solution)/shard_map/ppermute | solution.py:378
  10.3 6.3 %collective-permute-start.3 = (bf16[8,16,616]{2,1,0:T(8,128)(2,1)S(1)}, bf16[8,16,616]{2,1,0:T(8,128)(2,1)S(1)}, u32[]{:S(2)}, u32[]{:S(2)}) collective-permute-start(bf16[8,16,616]{2,1,0:T(8,128)(2,1)S(1)} %slice.18), channel_id=1, source_target_pairs={{0,16},{8,72},{16,32},{24,88},{32,48},{40,104},{48,0},{56,120},{64... | collective-permute-start | bytes 473096 | tf_op jit(solution)/shard_map/ppermute | solution.py:339
  13.0 5.3 %collective-permute-start.4 = (bf16[8,16,616]{2,1,0:T(8,128)(2,1)S(1)}, bf16[8,16,616]{2,1,0:T(8,128)(2,1)S(1)}, u32[]{:S(2)}, u32[]{:S(2)}) collective-permute-start(bf16[8,16,616]{2,1,0:T(8,128)(2,1)S(1)} %slice.19), channel_id=1, source_target_pairs={{0,48},{8,200},{16,0},{24,216},{32,16},{40,232},{48,32},{56,248},{... | collective-permute-start | bytes 473096 | tf_op jit(solution)/shard_map/ppermute | solution.py:339
  15.4 28.0 %copy-start.1 = (f32[4,256,128]{2,1,0:T(8,128)S(1)}, f32[4,256,128]{2,1,0:T(8,128)}, u32[]{:S(2)}) copy-start(f32[4,256,128]{2,1,0:T(8,128)} %constant.169.clone.center_ref) | copy-start | bytes 1572868
  15.4 14.5 %collective-permute-start.2 = (bf16[2,16,16,616]{3,2,1,0:T(8,128)(2,1)S(1)}, bf16[2,16,16,616]{3,2,1,0:T(8,128)(2,1)S(1)}, u32[]{:S(2)}, u32[]{:S(2)}) collective-permute-start(bf16[2,16,16,616]{3,2,1,0:T(8,128)(2,1)S(1)} %pad_maximum_fusion.refs_0_), channel_id=1, source_target_pairs={{0,64},{8,24},{16,80},{24,40},{32,96},{40,56},{48,112},{56,8},{64,... | collective-permute-start | bytes 1892360 | tf_op jit(solution)/shard_map/ppermute | solution.py:339
  18.4 11.4 %collective-permute-start.10 = (bf16[2,16,16,616]{3,2,1,0:T(8,128)(2,1)S(1)}, bf16[2,16,16,616]{3,2,1,0:T(8,128)(2,1)}, u32[]{:S(2)}, u32[]{:S(2)}) collective-permute-start(bf16[2,16,16,616]{3,2,1,0:T(8,128)(2,1)S(1)} %pad_maximum_fusion.1.refs_1_), channel_id=1, source_target_pairs={{0,192},{8,56},{16,208},{24,8},{32,224},{40,24},{48,240},{56,40},{... | collective-permute-start | bytes 1892360 | tf_op jit(solution)/shard_map/ppermute | solution.py:339
  19.8 8.2 %collective-permute-start.11 = (bf16[4,32,256]{2,1,0:T(8,128)(2,1)S(1)}, bf16[4,32,256]{2,1,0:T(8,128)(2,1)S(1)}, u32[]{:S(2)}, u32[]{:S(2)}) collective-permute-start(bf16[4,32,256]{2,1,0:T(8,128)(2,1)S(1)} %pad_maximum_fusion.3), channel_id=1, source_target_pairs={{0,64},{8,24},{16,80},{24,40},{32,96},{40,56},{48,112},{56,8},{64,... | collective-permute-start | bytes 196616 | tf_op jit(solution)/shard_map/ppermute | solution.py:339
  20.5 9.3 %collective-permute-start.12 = (bf16[4,32,256]{2,1,0:T(8,128)(2,1)S(1)}, bf16[4,32,256]{2,1,0:T(8,128)(2,1)S(1)}, u32[]{:S(2)}, u32[]{:S(2)}) collective-permute-start(bf16[4,32,256]{2,1,0:T(8,128)(2,1)S(1)} %pad_maximum_fusion.3), channel_id=1, source_target_pairs={{0,192},{8,56},{16,208},{24,8},{32,224},{40,24},{48,240},{56,40},{... | collective-permute-start | bytes 196616 | tf_op jit(solution)/shard_map/ppermute | solution.py:339
  23.0 6.8 %collective-permute-start.13 = (bf16[4,32,256]{2,1,0:T(8,128)(2,1)S(1)}, bf16[4,32,256]{2,1,0:T(8,128)(2,1)S(1)}, u32[]{:S(2)}, u32[]{:S(2)}) collective-permute-start(bf16[4,32,256]{2,1,0:T(8,128)(2,1)S(1)} %pad_maximum_fusion.3), channel_id=1, source_target_pairs={{0,128},{8,40},{16,144},{24,56},{32,160},{40,8},{48,176},{56,24},{... | collective-permute-start | bytes 196616 | tf_op jit(solution)/shard_map/ppermute | solution.py:339
  29.9 19.6 %collective-permute-start.15 = (bf16[2,16,16,616]{3,2,1,0:T(8,128)(2,1)S(1)}, bf16[2,16,16,616]{3,2,1,0:T(8,128)(2,1)}, u32[]{:S(2)}, u32[]{:S(2)}) collective-permute-start(bf16[2,16,16,616]{3,2,1,0:T(8,128)(2,1)S(1)} %pad_maximum_fusion.1.refs_1_), channel_id=1, source_target_pairs={{0,64},{8,24},{16,80},{24,40},{32,96},{40,56},{48,112},{56,8},{64,... | collective-permute-start | bytes 1892360 | tf_op jit(solution)/shard_map/ppermute | solution.py:339
  31.5 18.0 %collective-permute-start.16 = (bf16[2,16,16,616]{3,2,1,0:T(8,128)(2,1)S(1)}, bf16[2,16,16,616]{3,2,1,0:T(8,128)(2,1)}, u32[]{:S(2)}, u32[]{:S(2)}) collective-permute-start(bf16[2,16,16,616]{3,2,1,0:T(8,128)(2,1)S(1)} %pad_maximum_fusion.refs_0_), channel_id=1, source_target_pairs={{0,192},{8,56},{16,208},{24,8},{32,224},{40,24},{48,240},{56,40},{... | collective-permute-start | bytes 1892360 | tf_op jit(solution)/shard_map/ppermute | solution.py:339
  33.6 15.9 %collective-permute-start.17 = (bf16[2,16,16,616]{3,2,1,0:T(8,128)(2,1)S(1)}, bf16[2,16,16,616]{3,2,1,0:T(8,128)(2,1)}, u32[]{:S(2)}, u32[]{:S(2)}) collective-permute-start(bf16[2,16,16,616]{3,2,1,0:T(8,128)(2,1)S(1)} %collective-permute-done.2.refs_2_), channel_id=1, source_target_pairs={{0,64},{8,24},{16,80},{24,40},{32,96},{40,56},{48,112},{56,8},{64,... | collective-permute-start | bytes 1892360 | tf_op jit(solution)/shard_map/ppermute | solution.py:339
  33.6 15.9 %collective-permute-start.18 = (bf16[2,16,16,616]{3,2,1,0:T(8,128)(2,1)}, bf16[2,16,16,616]{3,2,1,0:T(8,128)(2,1)}, u32[]{:S(2)}, u32[]{:S(2)}) collective-permute-start(bf16[2,16,16,616]{3,2,1,0:T(8,128)(2,1)} %collective-permute-done.10.refs_5_), channel_id=1, source_target_pairs={{0,192},{8,56},{16,208},{24,8},{32,224},{40,24},{48,240},{56,40},{... | collective-permute-start | bytes 1892360 | tf_op jit(solution)/shard_map/ppermute | solution.py:339
  36.9 11.2 %collective-permute-start.14 = (bf16[4,4,32,256]{3,2,1,0:T(8,128)(2,1)S(1)}, bf16[4,4,32,256]{3,2,1,0:T(8,128)(2,1)S(1)}, u32[]{:S(2)}, u32[]{:S(2)}) collective-permute-start(bf16[4,4,32,256]{3,2,1,0:T(8,128)(2,1)S(1)} %pad_maximum_fusion.2), channel_id=1, source_target_pairs={{0,8},{8,0},{16,24},{24,16},{32,40},{40,32},{48,56},{56,48},{64,72... | collective-permute-start | bytes 786440 | tf_op jit(solution)/shard_map/ppermute | solution.py:395
  37.0 1.0 copy-start
  38.1 0.7 copy-start.4
  43.4 4.7 %copy-start.2 = (bf16[192,768]{1,0:T(8,128)(2,1)S(1)}, bf16[192,768]{1,0:T(8,128)(2,1)}, u32[]{:S(2)}) copy-start(bf16[192,768]{1,0:T(8,128)(2,1)} %constant.173.clone.own_cell_ref) | copy-start | bytes 884740
  43.4 4.7 %copy-start.3 = (bf16[64,768]{1,0:T(8,128)(2,1)S(1)}, bf16[64,768]{1,0:T(8,128)(2,1)}, u32[]{:S(2)}) copy-start(bf16[64,768]{1,0:T(8,128)(2,1)} %constant.172.clone.row_tile_ref) | copy-start | bytes 294916
  43.4 4.7 %copy-start.5 = (bf16[16,192]{1,0:T(8,128)(2,1)S(1)}, bf16[16,192]{1,0:T(8,128)(2,1)}, u32[]{:S(2)}) copy-start(bf16[16,192]{1,0:T(8,128)(2,1)} %constant.174.clone.tap_ref) | copy-start | bytes 18436
  43.4 4.7 %copy-start.6 = (s32[1,768]{1,0:T(1,128)S(1)}, s32[1,768]{1,0:T(1,128)}, u32[]{:S(2)}) copy-start(s32[1,768]{1,0:T(1,128)} %constant.182.token_ref) | copy-start | bytes 9220
  49.5 18.6 %copy-start.10 = (bf16[32,32,1]{1,0,2:T(8,128)(2,1)S(1)}, bf16[32,32,1]{1,0,2:T(8,128)(2,1)}, u32[]{:S(2)}) copy-start(bf16[32,32,1]{1,0,2:T(8,128)(2,1)} %constant.285) | copy-start | bytes 6148
  49.5 21.3 %copy-start.9 = (f32[1,512]{1,0:T(1,128)S(1)}, f32[1,512]{1,0:T(1,128)}, u32[]{:S(2)}) copy-start(f32[1,512]{1,0:T(1,128)} %param.22) | copy-start | bytes 6148
  49.5 22.2 %copy-start.8 = (f32[512]{0:T(512)S(1)}, f32[512]{0:T(512)}, u32[]{:S(2)}) copy-start(f32[512]{0:T(512)} %param.23) | copy-start | bytes 6148
  49.5 31.9 %copy-start.7 = (f32[4,512]{1,0:T(4,128)S(1)}, f32[4,512]{1,0:T(4,128)}, u32[]{:S(2)}) copy-start(f32[4,512]{1,0:T(4,128)} %latent_ref.1) | copy-start | bytes 24580
  59.4 22.0 %all-to-all-start = ((bf16[32,48,256]{2,1,0:T(8,128)(2,1)}), bf16[32,48,256]{2,1,0:T(8,128)(2,1)S(1)}, u32[]{:S(2)}, u32[]{:S(2)}) async-start(bf16[32,48,256]{2,1,0:T(8,128)(2,1)} %bitcast.22), calls=%async_computation | async-start | bytes 1572864 | tf_op jit(solution)/shard_map/all_to_all | solution.py:417
